TPU v7x, 256 devices: a whole 4x4x8 slice. The times are simulated.
256 devices in a mesh: dp: 32 (over x, y, core), seq: 8 (over z).
Axes of the slice: x: 4, y: 4, z: 8, core: 2. Of those that a mesh axis runs over, the one named last changes fastest.
Arguments:
- hidden: bfloat16 [32, 8192, 4096], P('dp', 'seq')
- gain: float32 [4096], replicated, may hold values from 0.25 to 1.75
- seg_start: int32 [32, 256], P('dp'), may hold values from 0 to 8191, as said below
- owner: int32 [32, 256], P('dp'), may hold values from 0 to 7, as said below
- queries: bfloat16 [16384, 4096], P('seq', 'dp')
- positive: int32 [16384], P('seq'), may hold values from 0 to 8191
- logit_scale: float32 [1], replicated, may hold values from 200 to 300
Outputs:
- pooled: bfloat16 [8192, 4096], P(('dp', 'seq'))
- log_prob: float32 [16384], P('seq')
Inputs may be any that keep to these rules, and one draw needn't show every extreme that they name: `seg_start`: each row's starts rise strictly, the first is 0, and every passage covers at least 16 positions. `owner`: in every row each index of seq owns exactly 32 passages.
All inputs are finite; a program needn't handle non-finite values.
Results may differ from a plain program's by a relative error of at most 0.0049.
Values may be sent and summed in bfloat16 or wider, within the bound.
No kernel may reach another device: no remote copies, remote signals or barrier semaphores. Data moves between devices by JAX's collectives and lax.ppermute only.
A program may use at most 128 MiB of HBM per device.

v0:
```python
import jax
import jax.numpy as jnp
from jax import lax
from jax.sharding import PartitionSpec as P


def finish(sums, counts):
    mean = sums / counts[:, None]
    return (mean * lax.rsqrt(jnp.sum(mean * mean, axis=1, keepdims=True) + 1e-06)).astype(
        jnp.bfloat16
    )


def per_device(hidden, gain, seg_start, owner, queries, positive, logit_scale):
    seq_count = lax.axis_size("seq")
    tok_count = hidden.shape[1]
    seg_count = seg_start.shape[1]
    seg_owned = seg_count // seq_count
    row_length = tok_count * seq_count
    seq_place = lax.axis_index("seq")
    full_queries = lax.all_gather(queries, "dp", axis=1, tiled=True)
    states = hidden[0].astype(jnp.float32)
    meansq = jnp.mean(states * states, axis=-1, keepdims=True)
    normed = (states * lax.rsqrt(meansq + 1e-05) * gain).astype(jnp.bfloat16)
    starts = seg_start[0]
    ends = jnp.concatenate([starts[1:], jnp.full((1,), row_length, jnp.int32)])
    own = owner[0]
    table = (own[:, None] == jnp.arange(seq_count, dtype=jnp.int32)[None, :]).astype(jnp.int32)
    ranked = jnp.sum((jnp.cumsum(table, axis=0) - 1) * table, axis=1)
    slot = own * seg_owned + ranked
    match = (slot[None, :] == jnp.arange(seg_count, dtype=jnp.int32)[:, None]).astype(jnp.int32)
    seg_of_slot = jnp.sum(match * jnp.arange(seg_count, dtype=jnp.int32)[None, :], axis=1)
    slot_start = jnp.sum(match * starts[None, :], axis=1)
    slot_end = jnp.sum(match * ends[None, :], axis=1)
    places = seq_place * tok_count + jnp.arange(tok_count, dtype=jnp.int32)
    member = (
        (slot_start[:, None] <= places[None, :]) & (places[None, :] < slot_end[:, None])
    ).astype(jnp.bfloat16)
    partial_value = jnp.dot(member, normed, preferred_element_type=jnp.float32)
    counts = (slot_end - slot_start).astype(jnp.float32)
    own_sums = lax.psum_scatter(partial_value, "seq", scatter_dimension=0, tiled=True)
    own_counts = lax.dynamic_slice_in_dim(counts, seq_place * seg_owned, seg_owned)
    pooled = finish(own_sums, own_counts)
    passages = lax.all_gather(pooled, "seq", axis=0, tiled=True)
    squares = jnp.einsum("qd,qd->q", full_queries, full_queries, preferred_element_type=jnp.float32)
    factor = logit_scale[0] * lax.rsqrt(squares + 1e-06)
    scores = lax.dot_general(
        full_queries, passages, (((1,), (1,)), ((), ())), preferred_element_type=jnp.float32
    )
    scores = scores * factor[:, None]
    local_pick = positive % seg_count
    in_block = positive // seg_count == lax.axis_index("dp")
    hit = (seg_of_slot[None, :] == local_pick[:, None]) & in_block[:, None]
    pos_part = jnp.sum(jnp.where(hit, scores, 0.0), axis=1)
    local_top = jnp.max(scores, axis=1)
    top = lax.pmax(local_top, "dp")
    local_total = jnp.sum(jnp.exp(scores - top[:, None]), axis=1)
    total, chosen = lax.psum((local_total, pos_part), "dp")
    log_prob = chosen - top - jnp.log(total)
    return (pooled, log_prob)


def solution(mesh):
    in_specs = (
        P("dp", "seq", None),
        P(),
        P("dp", None),
        P("dp", None),
        P("seq", "dp"),
        P("seq"),
        P(),
    )
    out_specs = (P(("dp", "seq"), None), P("seq"))
    return jax.shard_map(
        per_device, mesh=mesh, in_specs=in_specs, out_specs=out_specs, check_vma=False
    )
```

profile of v0, /device:TPU:1, one launch (start us, length us, event | category | flops | bytes accessed | tf_op | source)
XLA Modules:
  0.0 358.2 jit_solution(15058082254090922367)
XLA Ops:
  8.0 0.0 copy-start.2
  8.0 0.0 copy-start.3
  8.0 0.0 reduce-scatter.2.cloned.1.call-start
  8.1 0.7 fusion.20
  8.8 0.6 reduce-window.6
  9.3 0.2 slice_reduce_fusion
  9.6 0.8 fusion.19
  10.4 0.7 multiply_add_fusion
  11.0 0.8 slice.14
  11.8 5.2 %fusion.1 = f32[1024]{0:T(1024)S(1)} fusion(bf16[1,1024,4096]{2,1,0:T(8,128)(2,1)} %param.7), kind=kLoop, calls=%fused_computation.4 | loop fusion | flops 12581888 | bytes 8392704 | tf_op jit(solution)/shard_map/reduce_sum | solution.py:23
  17.0 0.1 pad_add_fusion
  17.1 0.0 copy-done.2
  17.1 0.2 select_reduce_fusion
  17.3 0.2 copy-done
  17.6 4.7 %fusion.4 = f32[256,4096]{1,0:T(8,128)} fusion(bf16[1,1024,4096]{2,1,0:T(8,128)(2,1)S(1)} %copy-done, f32[4096]{0:T(1024)S(1)} %copy-done.3, f32[1024]{0:T(1024)S(1)} %add_rsqrt_fusion, s32[1024]{0:T(1024)S(1)} %iota_add_fusion, s32[256]{0:T(256)S(1)} %get-tuple-element.5, s32[256]{0:T(256)S(1)} %get-tuple-element.6), kind=kOutput, calls=%fused_computation.7 | convolution fusion | flops 2165047296 | bytes 12609536 | tf_op jit(solution)/shard_map/dot_general | solution.py:39
  22.2 0.0 reduce-scatter.2.cloned.1.call-update
  22.3 0.0 all-gather.5.cloned.1.call-start
  22.3 0.5 all-gather.5.cloned.1.call-update
  22.8 0.0 all-gather.3.cloned.1.call-start
  22.9 0.1 dynamic_slice.3
  23.0 58.6 %reduce-scatter.2.cloned.1.call-done = f32[32,4096]{1,0:T(8,128)} async-done(((f32[256,4096]{1,0:T(8,128)}), f32[32,4096]{1,0:T(8,128)}) %reduce-scatter.2.cloned.1.call-update) | async-done | bytes 524304 | tf_op jit(solution)/shard_map/reduce_scatter | solution.py:41
  81.6 1.3 multiply_reduce_fusion
  82.8 1.9 multiply_convert_fusion
  84.7 0.0 all-gather.3.cloned.1.call-update
  85.4 29.3 %all-gather.5.cloned.1.call-done = bf16[2048,4096]{1,0:T(8,128)(2,1)} async-done(((bf16[2048,128]{1,0:T(8,128)(2,1)}), bf16[2048,4096]{1,0:T(8,128)(2,1)}) %all-gather.5.cloned.1.call-update) | async-done | bytes 16777232 | tf_op jit(solution)/shard_map/all_gather | solution.py:21
  114.8 7.2 %fusion = f32[2048]{0:T(1024)S(1)} fusion(bf16[2048,4096]{1,0:T(8,128)(2,1)} %all-gather.5.cloned.1.call-done), kind=kLoop, calls=%fused_computation.1 | loop fusion | flops 25163776 | bytes 16785408 | tf_op jit(solution)/shard_map/qd,qd->q/dot_general | solution.py:45
  122.0 31.9 %all-gather.3.cloned.1.call-done = bf16[256,4096]{1,0:T(8,128)(2,1)} async-done(((bf16[32,4096]{1,0:T(8,128)(2,1)}), bf16[256,4096]{1,0:T(8,128)(2,1)}) %all-gather.3.cloned.1.call-update) | async-done | bytes 2097168 | tf_op jit(solution)/shard_map/all_gather | solution.py:44
  153.9 8.8 %fusion.23 = (f32[2048]{0:T(1024)S(1)}, f32[256,2048]{1,0:T(8,128)S(1)}) fusion(f32[2048]{0:T(1024)S(1)} %rsqrt_multiply_fusion, bf16[256,4096]{1,0:T(8,128)(2,1)} %all-gather.3.cloned.1.call-done, bf16[2048,4096]{1,0:T(8,128)(2,1)} %all-gather.5.cloned.1.call-done), kind=kOutput, calls=%fused_computation.53 | convolution fusion | flops 4296013824 | bytes 20987904 | tf_op jit(solution)/shard_map/dot_general | solution.py:47
  162.6 68.0 %pmax.7 = f32[2048]{0:T(1024)S(1)} all-reduce(f32[2048]{0:T(1024)S(1)} %get-tuple-element.9), channel_id=1, replica_groups=mesh['dp'=32,'seq'=8] {'dp'}, use_global_device_ids=true, to_apply=%region_12.13 | all-reduce | flops 2048 | bytes 16384 | tf_op jit(solution)/shard_map/pmax | solution.py:56
  230.6 0.7 fusion.9
  231.4 118.8 %all-reduce = (f32[2048]{0:T(1024)S(1)}, f32[2048]{0:T(1024)S(1)}) all-reduce(f32[2048]{0:T(1024)S(1)} %get-tuple-element.3, f32[2048]{0:T(1024)S(1)} %get-tuple-element.2), channel_id=1, replica_groups=mesh['dp'=32,'seq'=8] {'dp'}, use_global_device_ids=true, to_apply=%region_14.15 | all-reduce | flops 4096 | bytes 32768 | tf_op jit(solution)/shard_map/psum | solution.py:58
  350.2 0.6 log_subtract_fusion
  (13 shorter events, 0.1 us)
Async XLA Ops:
  8.0 9.1 %copy-start.2 = (s32[1,256]{1,0:T(1,128)S(1)}, s32[1,256]{1,0:T(1,128)}, u32[]{:S(2)}) copy-start(s32[1,256]{1,0:T(1,128)} %param.9) | copy-start | bytes 3076
  8.0 9.3 %copy-start.3 = (f32[4096]{0:T(1024)S(1)}, f32[4096]{0:T(1024)}, u32[]{:S(2)}) copy-start(f32[4096]{0:T(1024)} %param.8) | copy-start | bytes 49156
  8.0 73.5 %reduce-scatter.2.cloned.1.call-start = ((), (), s32[]{:S(2)}) async-start(), calls=%async_computation.1 | async-start | bytes 4718592 | tf_op jit(solution)/shard_map/reduce_scatter | solution.py:41
  11.8 5.8 %copy-start = (bf16[1,1024,4096]{2,1,0:T(8,128)(2,1)S(1)}, bf16[1,1024,4096]{2,1,0:T(8,128)(2,1)}, u32[]{:S(2)}) copy-start(bf16[1,1024,4096]{2,1,0:T(8,128)(2,1)} %param.7) | copy-start | bytes 25165828
  17.6 67.8 %copy-start.1 = (s32[2048]{0:T(1024)S(1)}, s32[2048]{0:T(1024)}, u32[]{:S(2)}) copy-start(s32[2048]{0:T(1024)} %param.12) | copy-start | bytes 24580
  22.3 92.5 %all-gather.5.cloned.1.call-start = ((), (), s32[]{:S(2)}) async-start(), calls=%async_computation.3 | async-start | bytes 17301504 | tf_op jit(solution)/shard_map/all_gather | solution.py:21
  22.8 131.0 %all-gather.3.cloned.1.call-start = ((), (), s32[]{:S(2)}) async-start(), calls=%async_computation.2 | async-start | bytes 2359296 | tf_op jit(solution)/shard_map/all_gather | solution.py:44
Sparse Core Ops, SparseCore 0:
  22.4 59.1 reduce-scatter.1
Sparse Core Ops, SparseCore 1:
  25.2 89.5 all-gather.4
  117.0 36.8 all-gather.2
where the time goes:
time: 362 us; the launch traced here: 358 us
  blocking collectives  187 us (52%)
  waiting for transfers between devices  120 us (33%)
  other arithmetic  20 us (6%)
  between operations  16.2 us (4%)
  matrix products  13.4 us (4%)
    psum x1, blocking collectives, per_device(): total, chosen = lax.psum((local_total, pos_part), 'dp')  119 us
    pmax x1, blocking collectives, per_device(): top = lax.pmax(local_top, 'dp')  68 us
    reduce_scatter x1, waiting for transfers between devices, per_device(): lax.psum_scatter(partial_value, 'seq', scatter_dimension=0, tiled=True)  58.6 us
    all_gather x1, waiting for transfers between devices, per_device(): passages = lax.all_gather(pooled, 'seq', axis=0, tiled=True)  31.9 us
    all_gather x1, waiting for transfers between devices, per_device(): full_queries = lax.all_gather(queries, 'dp', axis=1, tiled=True)  29.3 us
    dot_general x1, matrix products, per_device(): lax.dot_general(full_queries, passages, (((1,), (1,)), ((), ())), preferr...  8.76 us
  transfers between devices with their start and end apart: 3, of which 3 were waited for; matrix products, arithmetic and copies ran while one was open for 3% of the time, Pallas kernels for 0%

commit v1 on v0

v1 whole, which is shorter than its diff:
```python
import jax
import jax.numpy as jnp
from jax import lax
from jax.experimental import pallas as pl
from jax.experimental.pallas import tpu as pltpu
from jax.sharding import PartitionSpec as P

NX, NY, NC = 4, 4, 2
HALF_ROWS = 272
BF = jnp.bfloat16
F32 = jnp.float32
barrier = lax.optimization_barrier


def move(value, dx=0, dy=0, dc=0):
    pairs = []
    for x in range(NX):
        for y in range(NY):
            for c in range(NC):
                to = (((x + dx) % NX) * NY + (y + dy) % NY) * NC + (c + dc) % NC
                pairs.append(((x * NY + y) * NC + c, to))
    return lax.ppermute(value, "dp", pairs)


def turn(value, step):
    n = lax.axis_size("seq")
    return lax.ppermute(value, "seq", [(i, (i + step) % n) for i in range(n)])


def pool_kernel(place, starts, hidden, gain, out, acc):
    step = pl.program_id(0)
    rows = hidden.shape[0]

    @pl.when(step == 0)
    def _():
        acc[...] = jnp.zeros_like(acc)

    wide = hidden[...].astype(F32)
    meansq = jnp.mean(wide * wide, axis=1, keepdims=True)
    normed = (wide * lax.rsqrt(meansq + 1e-05) * gain[...]).astype(BF)
    first = place[0]
    pos = first + step * rows + lax.broadcasted_iota(jnp.int32, (rows, 1), 0)
    begun = (starts[...] <= pos).astype(jnp.int32)
    before = (starts[...] <= first).astype(jnp.int32)
    rel = jnp.sum(begun, axis=1, keepdims=True) - jnp.sum(before, axis=1, keepdims=True)
    lane = lax.broadcasted_iota(jnp.int32, (rows, 128), 1)
    member = (rel == lane).astype(F32).astype(BF)
    acc[...] += lax.dot_general(
        member, normed, (((0,), (0,)), ((), ())), preferred_element_type=F32
    )

    @pl.when(step == pl.num_programs(0) - 1)
    def _():
        for g in range(8):
            out[pl.ds(64 * g, 64), :] = acc[0:64, 512 * g : 512 * g + 512].astype(BF)
        tail = [acc[64:65, 512 * g : 512 * g + 512] for g in range(8)]
        tail.append(jnp.zeros((8, 512), F32))
        out[pl.ds(512, 16), :] = jnp.concatenate(tail, axis=0).astype(BF)


def pool(place, starts, hidden, gain):
    toks, d = hidden.shape
    blk = 256
    return pl.pallas_call(
        pool_kernel,
        out_shape=jax.ShapeDtypeStruct((528, 512), BF),
        grid_spec=pltpu.PrefetchScalarGridSpec(
            num_scalar_prefetch=1,
            grid=(toks // blk,),
            in_specs=[
                pl.BlockSpec((1, 256), lambda i, p: (0, 0)),
                pl.BlockSpec((blk, d), lambda i, p: (i, 0)),
                pl.BlockSpec((1, d), lambda i, p: (0, 0)),
            ],
            out_specs=pl.BlockSpec((528, 512), lambda i, p: (0, 0)),
            scratch_shapes=[pltpu.VMEM((128, d), F32)],
        ),
        compiler_params=pltpu.CompilerParams(vmem_limit_bytes=40 << 20),
        cost_estimate=pl.CostEstimate(
            flops=2 * 128 * toks * d, bytes_accessed=2 * toks * d, transcendentals=0
        ),
    )(place, starts, hidden, gain)


RING = (0, -1, 1, -2, 2, -3, 3, 4)


def embed_kernel(place, col_starts, counts, *refs):
    blocks, out, got, sums, sems = refs[:9], refs[9], refs[10], refs[11], refs[12]
    copies = []
    for k in range(7):
        copies.append(pltpu.make_async_copy(blocks[k], got.at[k], sems.at[k]))
    copies.append(pltpu.make_async_copy(blocks[7], got.at[7, pl.ds(0, HALF_ROWS)], sems.at[7]))
    copies.append(
        pltpu.make_async_copy(
            blocks[8], got.at[7, pl.ds(HALF_ROWS, 528 - HALF_ROWS)], sems.at[8]
        )
    )
    for copy in copies:
        copy.start()
    z = place[1]

    def first_of(k):
        far = jnp.zeros(k.shape, jnp.int32)
        for n, shift in enumerate(RING):
            far = jnp.where(k == n, shift, far)
        dev = lax.rem(z + far + 8, 8)
        begun = (col_starts[...] <= dev * 1024).astype(jnp.int32)
        return jnp.sum(begun, axis=0, keepdims=True) - 1

    seg = lax.broadcasted_iota(jnp.int32, (256, 512), 0)
    lane = lax.broadcasted_iota(jnp.int32, (1, 512), 1)
    pick = (seg == first_of(lane // 64) + lane % 64).astype(F32).astype(BF)
    tlane = lax.broadcasted_iota(jnp.int32, (1, 128), 1)
    tail_hit = lax.broadcasted_iota(jnp.int32, (256, 128), 0) == first_of(tlane // 16) + 64
    for copy in copies:
        copy.wait()
    tail = jnp.concatenate([got[k, 512:528, :] for k in range(8)], axis=0)
    square = jnp.zeros((256, 1), F32)
    for g in range(8):
        main = jnp.concatenate([got[k, 64 * g : 64 * g + 64, :] for k in range(8)], axis=0)
        tpick = (tail_hit & (tlane % 16 == g)).astype(F32).astype(BF)
        mean = (
            jnp.dot(pick, main, preferred_element_type=F32)
            + jnp.dot(tpick, tail, preferred_element_type=F32)
        ) / counts[...]
        sums[:, 512 * g : 512 * g + 512] = mean
        square += jnp.sum(mean * mean, axis=1, keepdims=True)
    scale = lax.rsqrt(square + 1e-06)
    for g in range(8):
        cols = slice(512 * g, 512 * g + 512)
        out[:, cols] = (sums[:, cols] * scale).astype(BF)


def embed(place, col_starts, counts, blocks):
    any_spec = pl.BlockSpec(memory_space=pl.ANY)
    vmem = pl.BlockSpec(memory_space=pltpu.VMEM)
    return pl.pallas_call(
        embed_kernel,
        out_shape=jax.ShapeDtypeStruct((256, 4096), BF),
        in_specs=[pl.BlockSpec(memory_space=pltpu.SMEM), vmem, vmem] + [any_spec] * 9,
        out_specs=vmem,
        scratch_shapes=[
            pltpu.VMEM((8, 528, 512), BF),
            pltpu.VMEM((256, 4096), F32),
            pltpu.SemaphoreType.DMA((9,)),
        ],
        compiler_params=pltpu.CompilerParams(vmem_limit_bytes=40 << 20),
        cost_estimate=pl.CostEstimate(
            flops=2 * 256 * 640 * 4096, bytes_accessed=7 << 20, transcendentals=0
        ),
    )(place, col_starts, counts, *blocks)


def score_kernel(place, scale, ids, positive, mine, other, *refs):
    q_refs, out, wide_q, stats, sems = refs[:10], refs[10], refs[11], refs[12], refs[13]
    x, y = place[2], place[3]

    def block_of(n):
        return (0, -1, 1, 2)[n]

    copies = []

    def add(src, row, rows, dx, dy):
        chip = lax.rem(x + dx + 4, 4) * 4 + lax.rem(y + dy + 4, 4)
        cols = pl.ds(pl.multiple_of(chip * 256, 256), 256)
        copies.append(
            pltpu.make_async_copy(src, wide_q.at[pl.ds(row, rows), cols], sems.at[len(copies)])
        )

    for half in range(2):
        own, plus, minus, far_lo, far_hi = q_refs[5 * half : 5 * half + 5]
        base = 512 * half
        for n in range(4):
            near = block_of(n)
            for ref, row, rows, along in (
                (own, 0, 512, 0),
                (plus, 0, 512, -1),
                (minus, 0, 512, 1),
                (far_lo, 0, 256, 2),
                (far_hi, 256, 256, 2),
            ):
                dx, dy = (near, along) if half == 0 else (along, near)
                add(ref.at[n], base + row, rows, dx, dy)
    for copy in copies:
        copy.start()
    for copy in copies:
        copy.wait()
    tile = 256

    def body(t, carry):
        rows = pl.ds(pl.multiple_of(t * tile, tile), tile)
        q = wide_q[rows, :]
        wq = q.astype(F32)
        factor = scale[0] * lax.rsqrt(jnp.sum(wq * wq, axis=1, keepdims=True) + 1e-06)
        nt = (((1,), (1,)), ((), ()))
        s0 = lax.dot_general(q, mine[...], nt, preferred_element_type=F32) * factor
        s1 = lax.dot_general(q, other[...], nt, preferred_element_type=F32) * factor
        pos = positive[rows, :]
        chosen = jnp.sum(
            jnp.where(ids[:, 0:256] == pos, s0, 0.0) + jnp.where(ids[:, 256:512] == pos, s1, 0.0),
            axis=1,
            keepdims=True,
        )
        top = jnp.max(jnp.maximum(s0, s1), axis=1, keepdims=True)
        total = jnp.sum(jnp.exp(s0 - top) + jnp.exp(s1 - top), axis=1, keepdims=True)
        lane = lax.broadcasted_iota(jnp.int32, (tile, 128), 1)
        stats[rows, :] = jnp.where(
            lane == 0, top, jnp.where(lane == 1, total, jnp.where(lane == 2, chosen, 0.0))
        )
        return carry

    lax.fori_loop(0, 1024 // tile, body, 0)
    out[...] = jnp.transpose(stats[...])[0:8, :]


def score(place, scale, ids, positive, mine, other, blocks):
    any_spec = pl.BlockSpec(memory_space=pl.ANY)
    vmem = pl.BlockSpec(memory_space=pltpu.VMEM)
    smem = pl.BlockSpec(memory_space=pltpu.SMEM)
    return pl.pallas_call(
        score_kernel,
        out_shape=jax.ShapeDtypeStruct((8, 1024), F32),
        in_specs=[smem, smem, vmem, vmem, vmem, vmem] + [any_spec] * 10,
        out_specs=vmem,
        scratch_shapes=[
            pltpu.VMEM((1024, 4096), BF),
            pltpu.VMEM((1024, 128), F32),
            pltpu.SemaphoreType.DMA((40,)),
        ],
        compiler_params=pltpu.CompilerParams(vmem_limit_bytes=48 << 20),
        cost_estimate=pl.CostEstimate(
            flops=2 * 1024 * 512 * 4096, bytes_accessed=12 << 20, transcendentals=1024 * 512
        ),
    )(place, scale, ids, positive, mine, other, *blocks)


def merge(parts):
    top = parts[0][0]
    for p in parts[1:]:
        top = jnp.maximum(top, p[0])
    total = sum(p[1] * jnp.exp(p[0] - top) for p in parts)
    chosen = sum(p[2] for p in parts)
    return jnp.stack([top, total, chosen])


def per_device(hidden, gain, seg_start, owner, queries, positive, logit_scale):
    seq_count = lax.axis_size("seq")
    tok_count = hidden.shape[1]
    seg_count = seg_start.shape[1]
    seg_owned = seg_count // seq_count
    dp, z = lax.axis_index("dp"), lax.axis_index("seq")
    core = dp % NC
    place = jnp.stack([z * tok_count, z, dp // (NY * NC), (dp // NC) % NY]).astype(jnp.int32)
    quarter = queries.shape[0] // 4
    half = queries.shape[0] // 2

    own = lax.dynamic_slice_in_dim(queries, core * half, half)
    away = lax.dynamic_slice_in_dim(queries, (1 - core) * half, half)
    back = move(away, dc=1)
    block = jnp.where(
        core == 0, jnp.concatenate([own, back], 1), jnp.concatenate([back, own], 1)
    )
    a, b = block[:quarter], block[quarter:]
    a, b, hidden = barrier((a, b, hidden))
    a_near = (a, move(a, dx=1), move(a, dx=-1), move(a, dx=2))
    b_near = (b, move(b, dy=1), move(b, dy=-1), move(b, dy=2))

    packed = pool(place, seg_start, hidden[0], gain[None, :])
    ring = [packed, turn(packed, 1), turn(packed, -1)]

    a_line, b_line = jnp.stack(a_near), jnp.stack(b_near)
    a_line, b_line = barrier((a_line, b_line))
    a_plus, a_minus = move(a_line, dy=1), move(a_line, dy=-1)
    b_plus, b_minus = move(b_line, dx=1), move(b_line, dx=-1)
    for _ in range(2):
        ring[-2:] = barrier(tuple(ring[-2:]))
        ring += [turn(ring[-2], 1), turn(ring[-1], -1)]
    ring[-2:] = barrier(tuple(ring[-2:]))
    ring += [turn(ring[-2][:HALF_ROWS], 1), turn(ring[-1][HALF_ROWS:], -1)]
    eighth = quarter // 2
    a_plus, a_minus, b_plus, b_minus = barrier((a_plus, a_minus, b_plus, b_minus))
    a_far = (move(a_plus[:, :eighth], dy=1), move(a_minus[:, eighth:], dy=-1))
    b_far = (move(b_plus[:, :eighth], dx=1), move(b_minus[:, eighth:], dx=-1))

    starts = seg_start[0]
    ends = jnp.concatenate([starts[1:], jnp.full((1,), tok_count * seq_count, jnp.int32)])
    counts = (ends - starts).astype(F32)
    mine = embed(place, starts[:, None], counts[:, None], ring)
    other = move(mine, dc=1)

    seg = jnp.arange(seg_count, dtype=jnp.int32)
    ids = jnp.concatenate([dp * seg_count + seg, (dp + 1 - 2 * core) * seg_count + seg])[None, :]
    picks = lax.dynamic_slice_in_dim(positive, core * half, half)[:, None]
    blocks = [a_line, a_plus, a_minus, *a_far, b_line, b_plus, b_minus, *b_far]
    stats = score(place, logit_scale, ids, picks, mine, other, blocks)

    hold = owner[0] == z
    rank = jnp.cumsum(hold.astype(jnp.int32)) - 1
    pick = (
        hold[None, :] & (rank[None, :] == jnp.arange(seg_owned, dtype=jnp.int32)[:, None])
    ).astype(BF)
    pooled = jnp.dot(pick, mine, preferred_element_type=F32).astype(BF)

    stats = stats[:3]
    stats = merge([stats, move(stats, dx=1), move(stats, dx=-1), move(stats, dx=2)])
    stats = merge([stats, move(stats, dy=1), move(stats, dy=-1), move(stats, dy=2)])
    part = stats[2] - stats[0] - jnp.log(stats[1])
    rest = move(part, dc=1)
    log_prob = jnp.where(core == 0, jnp.concatenate([part, rest]), jnp.concatenate([rest, part]))
    return pooled, log_prob


def solution(mesh):
    in_specs = (
        P("dp", "seq", None),
        P(),
        P("dp", None),
        P("dp", None),
        P("seq", "dp"),
        P("seq"),
        P(),
    )
    out_specs = (P(("dp", "seq"), None), P("seq"))
    return jax.shard_map(
        per_device, mesh=mesh, in_specs=in_specs, out_specs=out_specs, check_vma=False
    )
```

time: 362 us -> 193 us (0.53)
  blocking collectives: 187 us -> 0 us
  starting transfers between devices: 0.12 us -> 50.8 us
  waiting for transfers between devices: 120 us -> 85.8 us
  local copies, waits for them, and re-layouts: 1.28 us -> 28.1 us
  Pallas kernels: 0 us -> 21.1 us
  other arithmetic: 20 us -> 3.88 us
  between operations: 16.2 us -> 1.54 us
  matrix products: 13.4 us -> 1.15 us
    psum x1 -> x0, blocking collectives: 119 us -> none  [per_device(): total, chosen = lax.psum((local_total, pos_part), 'dp')]
    ppermute x0 -> x31, waiting for transfers between devices: none -> 85.8 us  [the longest x23 53 us: move(): return lax.ppermute(value, 'dp', pairs)]
    pmax x1 -> x0, blocking collectives: 68 us -> none  [per_device(): top = lax.pmax(local_top, 'dp')]
    all_gather x2 -> x0, waiting for transfers between devices: 61.2 us -> none  [the longest x1 31.9 us: per_device(): passages = lax.all_gather(pooled, 'seq', axis=0, tiled=True)]
    reduce_scatter x1 -> x0, waiting for transfers between devices: 58.6 us -> none  [per_device(): lax.psum_scatter(partial_value, 'seq', scatter_dimension=0, tiled=True)]
    ppermute x0 -> x31, starting transfers between devices: none -> 50.8 us  [the longest x23 37.7 us: move(): return lax.ppermute(value, 'dp', pairs)]
    pallas_call x0 -> x3, Pallas kernels: none -> 21.1 us  [the longest x1 12.1 us: score(): pl.pallas_call(score_kernel, out_shape=jax.ShapeDtypeStruct((8, 1024), F3...]
    unnamed x8 -> x44, local copies, waits for them, and re-layouts: 0.24 us -> 17 us
  transfers between devices with their start and end apart: 3 -> 31, of which waited for: 3 -> 18; matrix products, arithmetic and copies ran while one was open for 3% -> 7% of each run, Pallas kernels for 0% -> 2%
where the time goes in v1:
time: 193 us; the launch traced here: 192 us
  waiting for transfers between devices  85.8 us (44%)
  starting transfers between devices  50.8 us (26%)
  local copies, waits for them, and re-layouts  28.1 us (15%)
  Pallas kernels  21.1 us (11%)
  other arithmetic  3.88 us (2%)
    ppermute x23, waiting for transfers between devices, move(): return lax.ppermute(value, 'dp', pairs)  53 us
    ppermute x23, starting transfers between devices, move(): return lax.ppermute(value, 'dp', pairs)  37.7 us
    ppermute x8, waiting for transfers between devices, turn(): return lax.ppermute(value, 'seq', [(i, (i + step) % n) for i in range(n)])  32.8 us
    unnamed x44, local copies, waits for them, and re-layouts  17 us
    ppermute x8, starting transfers between devices, turn(): return lax.ppermute(value, 'seq', [(i, (i + step) % n) for i in range(n)])  13.1 us
    pallas_call x1, Pallas kernels, score(): pl.pallas_call(score_kernel, out_shape=jax.ShapeDtypeStruct((8, 1024), F3...  12.1 us
    pallas_call x1, Pallas kernels, pool(): pl.pallas_call(pool_kernel, out_shape=jax.ShapeDtypeStruct((528, 512), BF...  5.59 us
  transfers between devices with their start and end apart: 31, of which 18 were waited for; matrix products, arithmetic and copies ran while one was open for 7% of the time, Pallas kernels for 2%

profile of v1, /device:TPU:1, one launch (start us, length us, event | category | flops | bytes accessed | tf_op | source)
XLA Modules:
  0.0 192.4 jit_solution(17944023373242019235)
XLA Ops:
  1.7 3.3 %collective-permute-start = (bf16[1024,128]{1,0:T(8,128)(2,1)S(1)}, bf16[1024,128]{1,0:T(8,128)(2,1)S(1)}, u32[]{:S(2)}, u32[]{:S(2)}) collective-permute-start(bf16[1024,128]{1,0:T(8,128)(2,1)S(1)} %get-tuple-element.35), channel_id=1, source_target_pairs={{0,8},{8,0},{16,24},{24,16},{32,40},{40,32},{48,56},{56,48},{64,72... | collective-permute-start | bytes 786440 | tf_op jit(solution)/shard_map/ppermute | solution.py:22
  7.3 3.4 %copy-done = bf16[1,1024,4096]{2,1,0:T(8,128)(2,1)S(1)} copy-done((bf16[1,1024,4096]{2,1,0:T(8,128)(2,1)S(1)}, bf16[1,1024,4096]{2,1,0:T(8,128)(2,1)}, u32[]{:S(2)}) %copy-start) | copy-done | bytes 8388632
  10.7 5.6 %shard_map.86.refs_0_ = bf16[528,512]{1,0:T(8,128)(2,1)S(1)} custom-call(s32[4]{0:T(128)S(1)} %pad_add_fusion.1.place, s32[1,256]{1,0:T(1,128)S(1)} %copy-done.19, bf16[1024,4096]{1,0:T(8,128)(2,1)S(1)} %bitcast.39, f32[1,4096]{1,0:T(1,128)S(1)} %bitcast.40), custom_call_target="tpu_custom_call" | custom-call | flops 1073741824 | bytes 8388608 | tf_op jit(solution)/shard_map/pallas_call | solution.py:64
  16.2 3.9 %collective-permute-start.2 = (bf16[528,512]{1,0:T(8,128)(2,1)S(1)}, bf16[528,512]{1,0:T(8,128)(2,1)S(1)}, u32[]{:S(2)}, u32[]{:S(2)}) collective-permute-start(bf16[528,512]{1,0:T(8,128)(2,1)S(1)} %shard_map.86.refs_0_), channel_id=1, source_target_pairs={{0,7},{1,0},{2,1},{3,2},{4,3},{5,4},{6,5},{7,6},{8,15},{9,8},{10,9... | collective-permute-start | bytes 1622024 | tf_op jit(solution)/shard_map/ppermute | solution.py:27
  20.2 11.3 %collective-permute-done.2.refs_2_ = bf16[528,512]{1,0:T(8,128)(2,1)S(1)} collective-permute-done((bf16[528,512]{1,0:T(8,128)(2,1)S(1)}, bf16[528,512]{1,0:T(8,128)(2,1)S(1)}, u32[]{:S(2)}, u32[]{:S(2)}) %collective-permute-start.2) | collective-permute-done | bytes 540704 | tf_op jit(solution)/shard_map/ppermute | solution.py:27
  31.5 3.1 %collective-permute-done.1.refs_1_ = bf16[528,512]{1,0:T(8,128)(2,1)S(1)} collective-permute-done((bf16[528,512]{1,0:T(8,128)(2,1)S(1)}, bf16[528,512]{1,0:T(8,128)(2,1)S(1)}, u32[]{:S(2)}, u32[]{:S(2)}) %collective-permute-start.1) | collective-permute-done | bytes 540704 | tf_op jit(solution)/shard_map/ppermute | solution.py:27
  35.4 2.7 %collective-permute-start.4 = (bf16[528,512]{1,0:T(8,128)(2,1)S(1)}, bf16[528,512]{1,0:T(8,128)(2,1)S(1)}, u32[]{:S(2)}, u32[]{:S(2)}) collective-permute-start(bf16[528,512]{1,0:T(8,128)(2,1)S(1)} %collective-permute-done.2.refs_2_), channel_id=1, source_target_pairs={{0,7},{1,0},{2,1},{3,2},{4,3},{5,4},{6,5},{7,6},{8,15},{9,8},{10,9... | collective-permute-start | bytes 1622024 | tf_op jit(solution)/shard_map/ppermute | solution.py:27
  38.8 9.2 %collective-permute-done.3.refs_3_ = bf16[528,512]{1,0:T(8,128)(2,1)S(1)} collective-permute-done((bf16[528,512]{1,0:T(8,128)(2,1)S(1)}, bf16[528,512]{1,0:T(8,128)(2,1)S(1)}, u32[]{:S(2)}, u32[]{:S(2)}) %collective-permute-start.3) | collective-permute-done | bytes 540704 | tf_op jit(solution)/shard_map/ppermute | solution.py:27
  48.8 3.2 %collective-permute-start.6 = (bf16[528,512]{1,0:T(8,128)(2,1)S(1)}, bf16[528,512]{1,0:T(8,128)(2,1)S(1)}, u32[]{:S(2)}, u32[]{:S(2)}) collective-permute-start(bf16[528,512]{1,0:T(8,128)(2,1)S(1)} %collective-permute-done.4.refs_4_), channel_id=1, source_target_pairs={{0,7},{1,0},{2,1},{3,2},{4,3},{5,4},{6,5},{7,6},{8,15},{9,8},{10,9... | collective-permute-start | bytes 1622024 | tf_op jit(solution)/shard_map/ppermute | solution.py:27
  52.9 8.2 %collective-permute-done.5.refs_5_ = bf16[528,512]{1,0:T(8,128)(2,1)S(1)} collective-permute-done((bf16[528,512]{1,0:T(8,128)(2,1)S(1)}, bf16[528,512]{1,0:T(8,128)(2,1)S(1)}, u32[]{:S(2)}, u32[]{:S(2)}) %collective-permute-start.5) | collective-permute-done | bytes 540704 | tf_op jit(solution)/shard_map/ppermute | solution.py:27
  61.9 3.2 %collective-permute-start.8 = (bf16[256,512]{1,0:T(8,128)(2,1)S(1)}, bf16[256,512]{1,0:T(8,128)(2,1)S(1)}, u32[]{:S(2)}, u32[]{:S(2)}) collective-permute-start(bf16[256,512]{1,0:T(8,128)(2,1)S(1)} %slice.117), channel_id=1, source_target_pairs={{0,7},{1,0},{2,1},{3,2},{4,3},{5,4},{6,5},{7,6},{8,15},{9,8},{10,9... | collective-permute-start | bytes 786440 | tf_op jit(solution)/shard_map/ppermute | solution.py:27
  65.3 2.7 %collective-permute-start.12 = (bf16[512,256]{1,0:T(8,128)(2,1)}, bf16[512,256]{1,0:T(8,128)(2,1)}, u32[]{:S(2)}, u32[]{:S(2)}) collective-permute-start(bf16[512,256]{1,0:T(8,128)(2,1)} %get-tuple-element.24), channel_id=1, source_target_pairs={{0,128},{8,136},{16,144},{24,152},{32,160},{40,168},{48,176},{56,1... | collective-permute-start | bytes 786440 | tf_op jit(solution)/shard_map/ppermute | solution.py:22
  79.7 3.4 %shard_map.87.mine = bf16[256,4096]{1,0:T(8,128)(2,1)S(1)} custom-call(s32[4]{0:T(128)S(1)} %pad_add_fusion.1.place, s32[256,1]{1,0:T(8,128)S(1)} %copy.18.col_starts, f32[256,1]{1,0:T(8,128)S(1)} %convert_element_type.23.counts, bf16[528,512]{1,0:T(8,128)(2,1)S(1)} %shard_map.86.refs_0_, bf16[528,512]{1,0:T(8,128)(2,1)S(1)} %copy-done.8, ...), custom_call_target="tpu_custom_call" | custom-call | flops 1342177280 | bytes 7340032 | tf_op jit(solution)/shard_map/pallas_call | solution.py:138
  83.1 5.2 %collective-permute-start.9 = (bf16[256,4096]{1,0:T(8,128)(2,1)S(1)}, bf16[256,4096]{1,0:T(8,128)(2,1)}, u32[]{:S(2)}, u32[]{:S(2)}) collective-permute-start(bf16[256,4096]{1,0:T(8,128)(2,1)S(1)} %shard_map.87.mine), channel_id=1, source_target_pairs={{0,8},{8,0},{16,24},{24,16},{32,40},{40,32},{48,56},{56,48},{64,72... | collective-permute-start | bytes 6291464 | tf_op jit(solution)/shard_map/ppermute | solution.py:22
  88.3 2.9 %collective-permute-start.15 = (bf16[512,256]{1,0:T(8,128)(2,1)S(1)}, bf16[512,256]{1,0:T(8,128)(2,1)S(1)}, u32[]{:S(2)}, u32[]{:S(2)}) collective-permute-start(bf16[512,256]{1,0:T(8,128)(2,1)S(1)} %copy-done.20), channel_id=1, source_target_pairs={{0,32},{8,40},{16,48},{24,56},{32,0},{40,8},{48,16},{56,24},{64,96... | collective-permute-start | bytes 786440 | tf_op jit(solution)/shard_map/ppermute | solution.py:22
  93.9 3.8 %collective-permute-done.15 = bf16[512,256]{1,0:T(8,128)(2,1)S(1)} collective-permute-done((bf16[512,256]{1,0:T(8,128)(2,1)S(1)}, bf16[512,256]{1,0:T(8,128)(2,1)S(1)}, u32[]{:S(2)}, u32[]{:S(2)}) %collective-permute-start.15) | collective-permute-done | bytes 262176 | tf_op jit(solution)/shard_map/ppermute | solution.py:22
  97.7 5.9 %collective-permute-done.14 = bf16[512,256]{1,0:T(8,128)(2,1)S(1)} collective-permute-done((bf16[512,256]{1,0:T(8,128)(2,1)S(1)}, bf16[512,256]{1,0:T(8,128)(2,1)S(1)}, u32[]{:S(2)}, u32[]{:S(2)}) %collective-permute-start.14) | collective-permute-done | bytes 262176 | tf_op jit(solution)/shard_map/ppermute | solution.py:22
  104.7 2.7 %collective-permute-start.17 = (bf16[4,512,256]{2,1,0:T(8,128)(2,1)S(1)}, bf16[4,512,256]{2,1,0:T(8,128)(2,1)}, u32[]{:S(2)}, u32[]{:S(2)}) collective-permute-start(bf16[4,512,256]{2,1,0:T(8,128)(2,1)S(1)} %pad_maximum_fusion.refs_0_), channel_id=1, source_target_pairs={{0,48},{8,56},{16,0},{24,8},{32,16},{40,24},{48,32},{56,40},{64,11... | collective-permute-start | bytes 3145736 | tf_op jit(solution)/shard_map/ppermute | solution.py:22
  107.5 2.5 %collective-permute-start.19 = (bf16[4,512,256]{2,1,0:T(8,128)(2,1)}, bf16[4,512,256]{2,1,0:T(8,128)(2,1)}, u32[]{:S(2)}, u32[]{:S(2)}) collective-permute-start(bf16[4,512,256]{2,1,0:T(8,128)(2,1)} %pad_maximum_fusion.1.refs_5_), channel_id=1, source_target_pairs={{0,192},{8,200},{16,208},{24,216},{32,224},{40,232},{48,240},{56,2... | collective-permute-start | bytes 3145736 | tf_op jit(solution)/shard_map/ppermute | solution.py:22
  110.6 18.9 %collective-permute-done.17.refs_2_ = bf16[4,512,256]{2,1,0:T(8,128)(2,1)} collective-permute-done((bf16[4,512,256]{2,1,0:T(8,128)(2,1)S(1)}, bf16[4,512,256]{2,1,0:T(8,128)(2,1)}, u32[]{:S(2)}, u32[]{:S(2)}) %collective-permute-start.17) | collective-permute-done | bytes 1048608 | tf_op jit(solution)/shard_map/ppermute | solution.py:22
  129.5 3.2 %collective-permute-done.16.refs_1_ = bf16[4,512,256]{2,1,0:T(8,128)(2,1)} collective-permute-done((bf16[4,512,256]{2,1,0:T(8,128)(2,1)S(1)}, bf16[4,512,256]{2,1,0:T(8,128)(2,1)}, u32[]{:S(2)}, u32[]{:S(2)}) %collective-permute-start.16) | collective-permute-done | bytes 1048608 | tf_op jit(solution)/shard_map/ppermute | solution.py:22
  132.7 2.4 %collective-permute-done.18.refs_6_ = bf16[4,512,256]{2,1,0:T(8,128)(2,1)} collective-permute-done((bf16[4,512,256]{2,1,0:T(8,128)(2,1)}, bf16[4,512,256]{2,1,0:T(8,128)(2,1)}, u32[]{:S(2)}, u32[]{:S(2)}) %collective-permute-start.18) | collective-permute-done | bytes 1048608 | tf_op jit(solution)/shard_map/ppermute | solution.py:22
  137.0 1.9 slice.119
  140.8 1.9 slice.121
  144.1 2.4 %collective-permute-start.21 = (bf16[4,256,256]{2,1,0:T(8,128)(2,1)}, bf16[4,256,256]{2,1,0:T(8,128)(2,1)}, u32[]{:S(2)}, u32[]{:S(2)}) collective-permute-start(bf16[4,256,256]{2,1,0:T(8,128)(2,1)} %slice.119), channel_id=1, source_target_pairs={{0,48},{8,56},{16,0},{24,8},{32,16},{40,24},{48,32},{56,40},{64,11... | collective-permute-start | bytes 1572872 | tf_op jit(solution)/shard_map/ppermute | solution.py:22
  148.2 6.3 %collective-permute-done.23.refs_9_ = bf16[4,256,256]{2,1,0:T(8,128)(2,1)} collective-permute-done((bf16[4,256,256]{2,1,0:T(8,128)(2,1)}, bf16[4,256,256]{2,1,0:T(8,128)(2,1)}, u32[]{:S(2)}, u32[]{:S(2)}) %collective-permute-start.23) | collective-permute-done | bytes 524320 | tf_op jit(solution)/shard_map/ppermute | solution.py:22
  156.0 2.4 %collective-permute-done.20.refs_3_ = bf16[4,256,256]{2,1,0:T(8,128)(2,1)} collective-permute-done((bf16[4,256,256]{2,1,0:T(8,128)(2,1)}, bf16[4,256,256]{2,1,0:T(8,128)(2,1)}, u32[]{:S(2)}, u32[]{:S(2)}) %collective-permute-start.20) | collective-permute-done | bytes 524320 | tf_op jit(solution)/shard_map/ppermute | solution.py:22
  159.5 12.1 %shard_map.88 = f32[8,1024]{1,0:T(8,128)S(1)} custom-call(s32[4]{0:T(128)S(1)} %pad_add_fusion.1.place, f32[1]{0:T(128)S(6)} %copy.20.scale, s32[1,512]{1,0:T(1,128)S(1)} %bitcast.42, s32[1024,1]{1,0:T(8,128)S(1)} %copy-done.13, bf16[256,4096]{1,0:T(8,128)(2,1)} %copy-done.1, bf16[256,4096]{1,0:T(8,128)(2,1)} %collective-permute-done.9.other, ...), custom_call_target="tpu_custom_call" | custom-call | flops 4294967296 | bytes 12582912 | tf_op jit(solution)/shard_map/pallas_call | solution.py:221
  172.3 2.1 %collective-permute-start.25 = (f32[3,1024]{1,0:T(4,128)S(1)}, f32[3,1024]{1,0:T(4,128)S(1)}, u32[]{:S(2)}, u32[]{:S(2)}) collective-permute-start(f32[3,1024]{1,0:T(4,128)S(1)} %slice.147), channel_id=1, source_target_pairs={{0,192},{8,200},{16,208},{24,216},{32,224},{40,232},{48,240},{56,2... | collective-permute-start | bytes 36872 | tf_op jit(solution)/shard_map/ppermute | solution.py:22
  175.8 2.4 %collective-permute-done.24 = f32[3,1024]{1,0:T(4,128)S(1)} collective-permute-done((f32[3,1024]{1,0:T(4,128)S(1)}, f32[3,1024]{1,0:T(4,128)S(1)}, u32[]{:S(2)}, u32[]{:S(2)}) %collective-permute-start.24) | collective-permute-done | bytes 12320 | tf_op jit(solution)/shard_map/ppermute | solution.py:22
  179.9 2.5 %collective-permute-done.29 = f32[3,1024]{1,0:T(4,128)S(1)} collective-permute-done((f32[3,1024]{1,0:T(4,128)S(1)}, f32[3,1024]{1,0:T(4,128)S(1)}, u32[]{:S(2)}, u32[]{:S(2)}) %collective-permute-start.29) | collective-permute-done | bytes 12320 | tf_op jit(solution)/shard_map/ppermute | solution.py:22
  183.7 6.9 %collective-permute-start.30 = (f32[1024]{0:T(1024)S(1)}, f32[1024]{0:T(1024)S(1)}, u32[]{:S(2)}, u32[]{:S(2)}) collective-permute-start(f32[1024]{0:T(1024)S(1)} %log_subtract_fusion), channel_id=1, source_target_pairs={{0,8},{8,0},{16,24},{24,16},{32,40},{40,32},{48,56},{56,48},{64,72... | collective-permute-start | bytes 12296 | tf_op jit(solution)/shard_map/ppermute | solution.py:22
  (115 shorter events, 39.3 us)
Async XLA Ops:
  1.7 4.5 %collective-permute-start = (bf16[1024,128]{1,0:T(8,128)(2,1)S(1)}, bf16[1024,128]{1,0:T(8,128)(2,1)S(1)}, u32[]{:S(2)}, u32[]{:S(2)}) collective-permute-start(bf16[1024,128]{1,0:T(8,128)(2,1)S(1)} %get-tuple-element.35), channel_id=1, source_target_pairs={{0,8},{8,0},{16,24},{24,16},{32,40},{40,32},{48,56},{56,48},{64,72... | collective-permute-start | bytes 786440 | tf_op jit(solution)/shard_map/ppermute | solution.py:22
  16.2 15.2 %collective-permute-start.2 = (bf16[528,512]{1,0:T(8,128)(2,1)S(1)}, bf16[528,512]{1,0:T(8,128)(2,1)S(1)}, u32[]{:S(2)}, u32[]{:S(2)}) collective-permute-start(bf16[528,512]{1,0:T(8,128)(2,1)S(1)} %shard_map.86.refs_0_), channel_id=1, source_target_pairs={{0,7},{1,0},{2,1},{3,2},{4,3},{5,4},{6,5},{7,6},{8,15},{9,8},{10,9... | collective-permute-start | bytes 1622024 | tf_op jit(solution)/shard_map/ppermute | solution.py:27
  20.2 14.4 %collective-permute-start.1 = (bf16[528,512]{1,0:T(8,128)(2,1)S(1)}, bf16[528,512]{1,0:T(8,128)(2,1)S(1)}, u32[]{:S(2)}, u32[]{:S(2)}) collective-permute-start(bf16[528,512]{1,0:T(8,128)(2,1)S(1)} %shard_map.86.refs_0_), channel_id=1, source_target_pairs={{0,1},{1,2},{2,3},{3,4},{4,5},{5,6},{6,7},{7,0},{8,9},{9,10},{10,1... | collective-permute-start | bytes 1622024 | tf_op jit(solution)/shard_map/ppermute | solution.py:27
  34.6 13.5 %collective-permute-start.3 = (bf16[528,512]{1,0:T(8,128)(2,1)S(1)}, bf16[528,512]{1,0:T(8,128)(2,1)S(1)}, u32[]{:S(2)}, u32[]{:S(2)}) collective-permute-start(bf16[528,512]{1,0:T(8,128)(2,1)S(1)} %collective-permute-done.1.refs_1_), channel_id=1, source_target_pairs={{0,1},{1,2},{2,3},{3,4},{4,5},{5,6},{6,7},{7,0},{8,9},{9,10},{10,1... | collective-permute-start | bytes 1622024 | tf_op jit(solution)/shard_map/ppermute | solution.py:27
  35.4 12.7 %collective-permute-start.4 = (bf16[528,512]{1,0:T(8,128)(2,1)S(1)}, bf16[528,512]{1,0:T(8,128)(2,1)S(1)}, u32[]{:S(2)}, u32[]{:S(2)}) collective-permute-start(bf16[528,512]{1,0:T(8,128)(2,1)S(1)} %collective-permute-done.2.refs_2_), channel_id=1, source_target_pairs={{0,7},{1,0},{2,1},{3,2},{4,3},{5,4},{6,5},{7,6},{8,15},{9,8},{10,9... | collective-permute-start | bytes 1622024 | tf_op jit(solution)/shard_map/ppermute | solution.py:27
  48.0 13.1 %collective-permute-start.5 = (bf16[528,512]{1,0:T(8,128)(2,1)S(1)}, bf16[528,512]{1,0:T(8,128)(2,1)S(1)}, u32[]{:S(2)}, u32[]{:S(2)}) collective-permute-start(bf16[528,512]{1,0:T(8,128)(2,1)S(1)} %collective-permute-done.3.refs_3_), channel_id=1, source_target_pairs={{0,1},{1,2},{2,3},{3,4},{4,5},{5,6},{6,7},{7,0},{8,9},{9,10},{10,1... | collective-permute-start | bytes 1622024 | tf_op jit(solution)/shard_map/ppermute | solution.py:27
  48.8 12.2 %collective-permute-start.6 = (bf16[528,512]{1,0:T(8,128)(2,1)S(1)}, bf16[528,512]{1,0:T(8,128)(2,1)S(1)}, u32[]{:S(2)}, u32[]{:S(2)}) collective-permute-start(bf16[528,512]{1,0:T(8,128)(2,1)S(1)} %collective-permute-done.4.refs_4_), channel_id=1, source_target_pairs={{0,7},{1,0},{2,1},{3,2},{4,3},{5,4},{6,5},{7,6},{8,15},{9,8},{10,9... | collective-permute-start | bytes 1622024 | tf_op jit(solution)/shard_map/ppermute | solution.py:27
  61.9 8.2 %collective-permute-start.8 = (bf16[256,512]{1,0:T(8,128)(2,1)S(1)}, bf16[256,512]{1,0:T(8,128)(2,1)S(1)}, u32[]{:S(2)}, u32[]{:S(2)}) collective-permute-start(bf16[256,512]{1,0:T(8,128)(2,1)S(1)} %slice.117), channel_id=1, source_target_pairs={{0,7},{1,0},{2,1},{3,2},{4,3},{5,4},{6,5},{7,6},{8,15},{9,8},{10,9... | collective-permute-start | bytes 786440 | tf_op jit(solution)/shard_map/ppermute | solution.py:27
  65.2 6.7 %collective-permute-start.7 = (bf16[272,512]{1,0:T(8,128)(2,1)S(1)}, bf16[272,512]{1,0:T(8,128)(2,1)S(1)}, u32[]{:S(2)}, u32[]{:S(2)}) collective-permute-start(bf16[272,512]{1,0:T(8,128)(2,1)S(1)} %slice.116), channel_id=1, source_target_pairs={{0,1},{1,2},{2,3},{3,4},{4,5},{5,6},{6,7},{7,0},{8,9},{9,10},{10,1... | collective-permute-start | bytes 835592 | tf_op jit(solution)/shard_map/ppermute | solution.py:27
  65.3 25.8 %collective-permute-start.12 = (bf16[512,256]{1,0:T(8,128)(2,1)}, bf16[512,256]{1,0:T(8,128)(2,1)}, u32[]{:S(2)}, u32[]{:S(2)}) collective-permute-start(bf16[512,256]{1,0:T(8,128)(2,1)} %get-tuple-element.24), channel_id=1, source_target_pairs={{0,128},{8,136},{16,144},{24,152},{32,160},{40,168},{48,176},{56,1... | collective-permute-start | bytes 786440 | tf_op jit(solution)/shard_map/ppermute | solution.py:22
  68.0 23.9 %collective-permute-start.11 = (bf16[512,256]{1,0:T(8,128)(2,1)}, bf16[512,256]{1,0:T(8,128)(2,1)}, u32[]{:S(2)}, u32[]{:S(2)}) collective-permute-start(bf16[512,256]{1,0:T(8,128)(2,1)} %get-tuple-element.24), channel_id=1, source_target_pairs={{0,192},{8,200},{16,208},{24,216},{32,224},{40,232},{48,240},{56,2... | collective-permute-start | bytes 786440 | tf_op jit(solution)/shard_map/ppermute | solution.py:22
  69.3 23.3 %collective-permute-start.10 = (bf16[512,256]{1,0:T(8,128)(2,1)}, bf16[512,256]{1,0:T(8,128)(2,1)S(1)}, u32[]{:S(2)}, u32[]{:S(2)}) collective-permute-start(bf16[512,256]{1,0:T(8,128)(2,1)} %get-tuple-element.24), channel_id=1, source_target_pairs={{0,64},{8,72},{16,80},{24,88},{32,96},{40,104},{48,112},{56,120},{... | collective-permute-start | bytes 786440 | tf_op jit(solution)/shard_map/ppermute | solution.py:22
  83.1 75.3 %collective-permute-start.9 = (bf16[256,4096]{1,0:T(8,128)(2,1)S(1)}, bf16[256,4096]{1,0:T(8,128)(2,1)}, u32[]{:S(2)}, u32[]{:S(2)}) collective-permute-start(bf16[256,4096]{1,0:T(8,128)(2,1)S(1)} %shard_map.87.mine), channel_id=1, source_target_pairs={{0,8},{8,0},{16,24},{24,16},{32,40},{40,32},{48,56},{56,48},{64,72... | collective-permute-start | bytes 6291464 | tf_op jit(solution)/shard_map/ppermute | solution.py:22
  88.3 9.4 %collective-permute-start.15 = (bf16[512,256]{1,0:T(8,128)(2,1)S(1)}, bf16[512,256]{1,0:T(8,128)(2,1)S(1)}, u32[]{:S(2)}, u32[]{:S(2)}) collective-permute-start(bf16[512,256]{1,0:T(8,128)(2,1)S(1)} %copy-done.20), channel_id=1, source_target_pairs={{0,32},{8,40},{16,48},{24,56},{32,0},{40,8},{48,16},{56,24},{64,96... | collective-permute-start | bytes 786440 | tf_op jit(solution)/shard_map/ppermute | solution.py:22
  91.2 12.4 %collective-permute-start.14 = (bf16[512,256]{1,0:T(8,128)(2,1)S(1)}, bf16[512,256]{1,0:T(8,128)(2,1)S(1)}, u32[]{:S(2)}, u32[]{:S(2)}) collective-permute-start(bf16[512,256]{1,0:T(8,128)(2,1)S(1)} %copy-done.20), channel_id=1, source_target_pairs={{0,48},{8,56},{16,0},{24,8},{32,16},{40,24},{48,32},{56,40},{64,11... | collective-permute-start | bytes 786440 | tf_op jit(solution)/shard_map/ppermute | solution.py:22
  92.0 11.7 %collective-permute-start.13 = (bf16[512,256]{1,0:T(8,128)(2,1)S(1)}, bf16[512,256]{1,0:T(8,128)(2,1)S(1)}, u32[]{:S(2)}, u32[]{:S(2)}) collective-permute-start(bf16[512,256]{1,0:T(8,128)(2,1)S(1)} %copy-done.20), channel_id=1, source_target_pairs={{0,16},{8,24},{16,32},{24,40},{32,48},{40,56},{48,0},{56,8},{64,80... | collective-permute-start | bytes 786440 | tf_op jit(solution)/shard_map/ppermute | solution.py:22
  104.7 24.8 %collective-permute-start.17 = (bf16[4,512,256]{2,1,0:T(8,128)(2,1)S(1)}, bf16[4,512,256]{2,1,0:T(8,128)(2,1)}, u32[]{:S(2)}, u32[]{:S(2)}) collective-permute-start(bf16[4,512,256]{2,1,0:T(8,128)(2,1)S(1)} %pad_maximum_fusion.refs_0_), channel_id=1, source_target_pairs={{0,48},{8,56},{16,0},{24,8},{32,16},{40,24},{48,32},{56,40},{64,11... | collective-permute-start | bytes 3145736 | tf_op jit(solution)/shard_map/ppermute | solution.py:22
  107.5 25.3 %collective-permute-start.16 = (bf16[4,512,256]{2,1,0:T(8,128)(2,1)S(1)}, bf16[4,512,256]{2,1,0:T(8,128)(2,1)}, u32[]{:S(2)}, u32[]{:S(2)}) collective-permute-start(bf16[4,512,256]{2,1,0:T(8,128)(2,1)S(1)} %pad_maximum_fusion.refs_0_), channel_id=1, source_target_pairs={{0,16},{8,24},{16,32},{24,40},{32,48},{40,56},{48,0},{56,8},{64,80... | collective-permute-start | bytes 3145736 | tf_op jit(solution)/shard_map/ppermute | solution.py:22
  107.5 25.3 %collective-permute-start.19 = (bf16[4,512,256]{2,1,0:T(8,128)(2,1)}, bf16[4,512,256]{2,1,0:T(8,128)(2,1)}, u32[]{:S(2)}, u32[]{:S(2)}) collective-permute-start(bf16[4,512,256]{2,1,0:T(8,128)(2,1)} %pad_maximum_fusion.1.refs_5_), channel_id=1, source_target_pairs={{0,192},{8,200},{16,208},{24,216},{32,224},{40,232},{48,240},{56,2... | collective-permute-start | bytes 3145736 | tf_op jit(solution)/shard_map/ppermute | solution.py:22
  110.0 25.1 %collective-permute-start.18 = (bf16[4,512,256]{2,1,0:T(8,128)(2,1)}, bf16[4,512,256]{2,1,0:T(8,128)(2,1)}, u32[]{:S(2)}, u32[]{:S(2)}) collective-permute-start(bf16[4,512,256]{2,1,0:T(8,128)(2,1)} %pad_maximum_fusion.1.refs_5_), channel_id=1, source_target_pairs={{0,64},{8,72},{16,80},{24,88},{32,96},{40,104},{48,112},{56,120},{... | collective-permute-start | bytes 3145736 | tf_op jit(solution)/shard_map/ppermute | solution.py:22
  110.6 36.4 %dynamic-slice-start = ((s32[2048]{0:T(1024)}, s32[]{:T(128)}), s32[1024]{0:T(1024)S(1)}, s32[]{:S(2)}) async-start(s32[2048]{0:T(1024)} %param.12, s32[]{:T(128)} %select_n.46), calls=%async_computation | async-start | bytes 8704 | tf_op jit(solution)/shard_map/dynamic_slice | solution.py:294
  142.7 11.8 %collective-permute-start.23 = (bf16[4,256,256]{2,1,0:T(8,128)(2,1)}, bf16[4,256,256]{2,1,0:T(8,128)(2,1)}, u32[]{:S(2)}, u32[]{:S(2)}) collective-permute-start(bf16[4,256,256]{2,1,0:T(8,128)(2,1)} %slice.121), channel_id=1, source_target_pairs={{0,192},{8,200},{16,208},{24,216},{32,224},{40,232},{48,240},{56,2... | collective-permute-start | bytes 1572872 | tf_op jit(solution)/shard_map/ppermute | solution.py:22
  143.0 13.0 %collective-permute-start.22 = (bf16[4,256,256]{2,1,0:T(8,128)(2,1)}, bf16[4,256,256]{2,1,0:T(8,128)(2,1)}, u32[]{:S(2)}, u32[]{:S(2)}) collective-permute-start(bf16[4,256,256]{2,1,0:T(8,128)(2,1)} %slice.120), channel_id=1, source_target_pairs={{0,64},{8,72},{16,80},{24,88},{32,96},{40,104},{48,112},{56,120},{... | collective-permute-start | bytes 1572872 | tf_op jit(solution)/shard_map/ppermute | solution.py:22
  144.1 11.9 %collective-permute-start.21 = (bf16[4,256,256]{2,1,0:T(8,128)(2,1)}, bf16[4,256,256]{2,1,0:T(8,128)(2,1)}, u32[]{:S(2)}, u32[]{:S(2)}) collective-permute-start(bf16[4,256,256]{2,1,0:T(8,128)(2,1)} %slice.119), channel_id=1, source_target_pairs={{0,48},{8,56},{16,0},{24,8},{32,16},{40,24},{48,32},{56,40},{64,11... | collective-permute-start | bytes 1572872 | tf_op jit(solution)/shard_map/ppermute | solution.py:22
  146.5 11.9 %collective-permute-start.20 = (bf16[4,256,256]{2,1,0:T(8,128)(2,1)}, bf16[4,256,256]{2,1,0:T(8,128)(2,1)}, u32[]{:S(2)}, u32[]{:S(2)}) collective-permute-start(bf16[4,256,256]{2,1,0:T(8,128)(2,1)} %slice.118), channel_id=1, source_target_pairs={{0,16},{8,24},{16,32},{24,40},{32,48},{40,56},{48,0},{56,8},{64,80... | collective-permute-start | bytes 1572872 | tf_op jit(solution)/shard_map/ppermute | solution.py:22
  171.6 4.2 %collective-permute-start.26 = (f32[3,1024]{1,0:T(4,128)S(1)}, f32[3,1024]{1,0:T(4,128)S(1)}, u32[]{:S(2)}, u32[]{:S(2)}) collective-permute-start(f32[3,1024]{1,0:T(4,128)S(1)} %slice.147), channel_id=1, source_target_pairs={{0,128},{8,136},{16,144},{24,152},{32,160},{40,168},{48,176},{56,1... | collective-permute-start | bytes 36872 | tf_op jit(solution)/shard_map/ppermute | solution.py:22
  172.3 3.5 %collective-permute-start.25 = (f32[3,1024]{1,0:T(4,128)S(1)}, f32[3,1024]{1,0:T(4,128)S(1)}, u32[]{:S(2)}, u32[]{:S(2)}) collective-permute-start(f32[3,1024]{1,0:T(4,128)S(1)} %slice.147), channel_id=1, source_target_pairs={{0,192},{8,200},{16,208},{24,216},{32,224},{40,232},{48,240},{56,2... | collective-permute-start | bytes 36872 | tf_op jit(solution)/shard_map/ppermute | solution.py:22
  174.4 3.8 %collective-permute-start.24 = (f32[3,1024]{1,0:T(4,128)S(1)}, f32[3,1024]{1,0:T(4,128)S(1)}, u32[]{:S(2)}, u32[]{:S(2)}) collective-permute-start(f32[3,1024]{1,0:T(4,128)S(1)} %slice.147), channel_id=1, source_target_pairs={{0,64},{8,72},{16,80},{24,88},{32,96},{40,104},{48,112},{56,120},{... | collective-permute-start | bytes 36872 | tf_op jit(solution)/shard_map/ppermute | solution.py:22
  178.2 4.2 %collective-permute-start.29 = (f32[3,1024]{1,0:T(4,128)S(1)}, f32[3,1024]{1,0:T(4,128)S(1)}, u32[]{:S(2)}, u32[]{:S(2)}) collective-permute-start(f32[3,1024]{1,0:T(4,128)S(1)} %pad_maximum_fusion.2), channel_id=1, source_target_pairs={{0,32},{8,40},{16,48},{24,56},{32,0},{40,8},{48,16},{56,24},{64,96... | collective-permute-start | bytes 36872 | tf_op jit(solution)/shard_map/ppermute | solution.py:22
  178.3 4.1 %collective-permute-start.28 = (f32[3,1024]{1,0:T(4,128)S(1)}, f32[3,1024]{1,0:T(4,128)S(1)}, u32[]{:S(2)}, u32[]{:S(2)}) collective-permute-start(f32[3,1024]{1,0:T(4,128)S(1)} %pad_maximum_fusion.2), channel_id=1, source_target_pairs={{0,48},{8,56},{16,0},{24,8},{32,16},{40,24},{48,32},{56,40},{64,11... | collective-permute-start | bytes 36872 | tf_op jit(solution)/shard_map/ppermute | solution.py:22
  179.8 3.8 %collective-permute-start.27 = (f32[3,1024]{1,0:T(4,128)S(1)}, f32[3,1024]{1,0:T(4,128)S(1)}, u32[]{:S(2)}, u32[]{:S(2)}) collective-permute-start(f32[3,1024]{1,0:T(4,128)S(1)} %pad_maximum_fusion.2), channel_id=1, source_target_pairs={{0,16},{8,24},{16,32},{24,40},{32,48},{40,56},{48,0},{56,8},{64,80... | collective-permute-start | bytes 36872 | tf_op jit(solution)/shard_map/ppermute | solution.py:22
  183.7 8.1 %collective-permute-start.30 = (f32[1024]{0:T(1024)S(1)}, f32[1024]{0:T(1024)S(1)}, u32[]{:S(2)}, u32[]{:S(2)}) collective-permute-start(f32[1024]{0:T(1024)S(1)} %log_subtract_fusion), channel_id=1, source_target_pairs={{0,8},{8,0},{16,24},{24,16},{32,40},{40,32},{48,56},{56,48},{64,72... | collective-permute-start | bytes 12296 | tf_op jit(solution)/shard_map/ppermute | solution.py:22
  (22 other events, 127.6 us)

commit v2 on v0

v2 whole, which is shorter than its diff:
```python
import jax
import jax.numpy as jnp
from jax import lax
from jax.experimental import pallas as pl
from jax.experimental.pallas import tpu as pltpu
from jax.sharding import PartitionSpec as P

NX, NY, NC, NZ = 4, 4, 2, 8
PACKED = 528
CUT = 256
RING = (0, -1, 1, -2, 2, -3, 3, 4)
BF = jnp.bfloat16
F32 = jnp.float32
barrier = lax.optimization_barrier


def along(core):
    return 1 - 2 * core


def move(value, dx=0, dy=0, dc=0):
    pairs = []
    for x in range(NX):
        for y in range(NY):
            for c in range(NC):
                to = (((x + dx) % NX) * NY + (y + dy) % NY) * NC + (c + dc) % NC
                pairs.append(((x * NY + y) * NC + c, to))
    return lax.ppermute(value, "dp", pairs)


def _hop(axis_and_step):
    pairs = []
    for x in range(NX):
        for y in range(NY):
            for c in range(NC):
                for z in range(NZ):
                    axis, step = axis_and_step(c)
                    to = [x, y, z]
                    to[axis] = (to[axis] + step) % (NX, NY, NZ)[axis]
                    here = ((x * NY + y) * NC + c) * NZ + z
                    pairs.append((here, ((to[0] * NY + to[1]) * NC + c) * NZ + to[2]))
    return pairs


def turn(value, step):
    return lax.ppermute(value, "seq", [(i, (i + step) % NZ) for i in range(NZ)])


def pass_on(value, second, step):
    return lax.ppermute(value, ("dp", "seq"), _hop(lambda c: ((c + second) % 2, step)))


def place():
    dp, z = lax.axis_index("dp"), lax.axis_index("seq")
    return lax.div(dp, NY * NC), lax.rem(lax.div(dp, NC), NY), lax.rem(dp, NC), z


def column(row):
    n = row.shape[1]
    same = lax.broadcasted_iota(jnp.int32, (n, n), 0) == lax.broadcasted_iota(jnp.int32, (n, n), 1)
    return jnp.sum(jnp.where(same, row, 0), axis=1, keepdims=True)


POOL_ROWS = 256


def pool_kernel(starts, owner, gain, hidden, out, info, pick, token, buf, weights, sems):
    toks = hidden.shape[1]
    steps = toks // POOL_ROWS
    copies = [
        pltpu.make_async_copy(hidden.at[0, pl.ds(POOL_ROWS * n, POOL_ROWS)], buf.at[pl.ds(POOL_ROWS * n, POOL_ROWS)], sems.at[n])
        for n in range(steps)
    ]
    for copy in copies:
        copy.start()
    z = lax.axis_index("seq")
    first = z * hidden.shape[1]
    length = hidden.shape[1] * NZ
    segs = starts.shape[1]
    from_row = starts[...]
    lane = lax.broadcasted_iota(jnp.int32, (segs, segs), 1)
    line = lax.broadcasted_iota(jnp.int32, (segs, segs), 0)
    begin = jnp.sum(jnp.where(lane == line, from_row, 0), axis=1, keepdims=True)
    end = jnp.sum(jnp.where(lane == line + 1, from_row, 0), axis=1, keepdims=True)
    end = jnp.where(lax.broadcasted_iota(jnp.int32, (segs, 1), 0) == segs - 1, length, end)
    token[...] = jnp.zeros_like(token)
    info[:, 0:128] = jnp.broadcast_to(begin, (segs, 128)).astype(F32)
    info[:, 128:256] = jnp.broadcast_to(end - begin, (segs, 128)).astype(F32)
    hold = (owner[...] == z).astype(jnp.int32)
    hold_col = jnp.sum(jnp.where(lane == line, hold, 0), axis=1, keepdims=True)
    rank = jnp.sum(jnp.where(line < lane, hold_col, 0), axis=0, keepdims=True)
    slot = lax.broadcasted_iota(jnp.int32, (pick.shape[0], segs), 0)
    pick[...] = jnp.where((rank == slot) & (hold == 1), 1.0, 0.0).astype(BF)

    before = jnp.sum((from_row <= first).astype(jnp.int32), axis=1, keepdims=True)
    for n in range(steps):
        copies[n].wait()
        wide = buf[POOL_ROWS * n : POOL_ROWS * n + POOL_ROWS, :].astype(F32)
        rate = lax.rsqrt(jnp.mean(wide * wide, axis=1, keepdims=True) + 1e-05)
        high = rate.astype(BF).astype(F32)
        pos = first + n * POOL_ROWS + lax.broadcasted_iota(jnp.int32, (POOL_ROWS, 1), 0)
        rel = jnp.sum((from_row <= pos).astype(jnp.int32), axis=1, keepdims=True) - before
        at = lax.broadcasted_iota(jnp.int32, (POOL_ROWS, 128), 1)
        weight = jnp.where((rel == at) & (at < 64), high, 0.0)
        weight = jnp.where((rel + 64 == at), rate - high, weight)
        weights[:, POOL_ROWS * n : POOL_ROWS * n + POOL_ROWS] = jnp.transpose(weight).astype(BF)
    weight = weights[...]
    end_weight = jnp.where(rel[POOL_ROWS - 16 :] == 64, rate[POOL_ROWS - 16 :], 0.0)
    tail = []
    for g in range(8):
        cols = slice(512 * g, 512 * g + 512)
        part = jnp.dot(weight, buf[:, cols], preferred_element_type=F32)
        out[64 * g : 64 * g + 64, :] = ((part[0:64] + part[64:128]) * gain[:, cols]).astype(BF)
        end_rows = buf[toks - 16 : toks, cols].astype(F32)
        tail.append(jnp.sum(end_rows * end_weight, axis=0, keepdims=True) * gain[:, cols])
    tail.append(jnp.zeros((8, 512), F32))
    out[512:528, :] = jnp.concatenate(tail, axis=0).astype(BF)


def pool(starts, owner, gain, hidden):
    _, toks, d = hidden.shape
    segs = starts.shape[1]
    vmem = pl.BlockSpec(memory_space=pltpu.VMEM)
    return pl.pallas_call(
        pool_kernel,
        out_shape=(
            jax.ShapeDtypeStruct((PACKED, 512), BF),
            jax.ShapeDtypeStruct((segs, 256), F32),
            jax.ShapeDtypeStruct((segs // NZ, segs), BF),
            jax.ShapeDtypeStruct((8, 128), F32),
        ),
        in_specs=[vmem, vmem, vmem, pl.BlockSpec(memory_space=pltpu.HBM)],
        out_specs=(vmem,) * 4,
        scratch_shapes=[
            pltpu.VMEM((toks, d), BF),
            pltpu.VMEM((128, toks), BF),
            pltpu.SemaphoreType.DMA((toks // POOL_ROWS,)),
        ],
        compiler_params=pltpu.CompilerParams(vmem_limit_bytes=56 << 20),
        cost_estimate=pl.CostEstimate(
            flops=2 * 128 * toks * d, bytes_accessed=2 * toks * d, transcendentals=0
        ),
    )(starts, owner, gain, hidden)


def embed_kernel(info, _, *refs):
    blocks, out, sums = refs[:9], refs[9], refs[10]
    z = lax.axis_index("seq")
    starts = info[:, 0:1]
    counts = info[:, 128:129]

    def first_of(k):
        far = jnp.zeros(k.shape, jnp.int32)
        for n, shift in enumerate(RING):
            far = jnp.where(k == n, shift, far)
        dev = lax.rem(z + far + 8, 8) * 1024
        begun = (starts <= dev.astype(F32)).astype(F32)
        return (jnp.sum(begun, axis=0, keepdims=True) - 1.0).astype(jnp.int32)

    seg = lax.broadcasted_iota(jnp.int32, (256, 512), 0)
    lane = lax.broadcasted_iota(jnp.int32, (1, 512), 1)
    pick = jnp.where(seg == first_of(lane // 64) + lane % 64, 1.0, 0.0).astype(BF)
    tlane = lax.broadcasted_iota(jnp.int32, (1, 128), 1)
    tail_hit = lax.broadcasted_iota(jnp.int32, (256, 128), 0) == first_of(tlane // 16) + 64

    def rows_of(row, rows):
        parts = [block[row : row + rows, :] for block in blocks[:7]]
        if row < CUT:
            parts.append(blocks[7][row : row + rows, :])
        else:
            parts.append(blocks[8][row - CUT : row - CUT + rows, :])
        return jnp.concatenate(parts, axis=0)

    tail = rows_of(512, 16)
    square = jnp.zeros((256, 1), F32)
    for g in range(8):
        tpick = jnp.where(tail_hit & (tlane % 16 == g), 1.0, 0.0).astype(BF)
        mean = (
            jnp.dot(pick, rows_of(64 * g, 64), preferred_element_type=F32)
            + jnp.dot(tpick, tail, preferred_element_type=F32)
        ) / counts
        sums[g] = mean
        square += jnp.sum(mean * mean, axis=1, keepdims=True)
    scale = lax.rsqrt(square + 1e-06)
    for g in range(8):
        out[:, 512 * g : 512 * g + 512] = (sums[g] * scale).astype(BF)


def embed(info, token, blocks):
    vmem = pl.BlockSpec(memory_space=pltpu.VMEM)
    return pl.pallas_call(
        embed_kernel,
        out_shape=jax.ShapeDtypeStruct((256, 4096), BF),
        in_specs=[vmem] * 11,
        out_specs=vmem,
        scratch_shapes=[pltpu.VMEM((8, 256, 512), F32)],
        compiler_params=pltpu.CompilerParams(vmem_limit_bytes=24 << 20),
        cost_estimate=pl.CostEstimate(
            flops=2 * 256 * 640 * 4096, bytes_accessed=7 << 20, transcendentals=0
        ),
    )(info, token, *blocks)


NEAR = (0, -1, 1, 2)


def query_block(refs, row, n, m):
    if m < 3:
        return refs[m][1024 * n + row : 1024 * n + row + 256, :]
    at = 1024 * (n % 2) + row
    return refs[3 + n // 2][at : at + 256, :]


def order_features(passages, ordered):
    x, y, core, _ = place()
    for n, u in enumerate(NEAR):
        for m, v in enumerate(NEAR):
            dx, dy = u + core * (v - u), v + core * (u - v)
            chip = lax.rem(x + dx + 4, 4) * 4 + lax.rem(y + dy + 4, 4)
            cols = pl.ds(pl.multiple_of(chip * 256, 256), 256)
            to = 256 * (n * 4 + m)
            ordered[:, to : to + 256] = passages[:, cols]


def picks_of(positive, row):
    core = lax.rem(lax.axis_index("dp"), NC)
    at = core * 8 + row // 128
    return jnp.concatenate(
        [column(positive[pl.ds(at, 1), :]), column(positive[pl.ds(at + 1, 1), :])], axis=0
    )


def lanes(*values):
    lane = lax.broadcasted_iota(jnp.int32, (256, 128), 1)
    out = jnp.zeros((256, 128), F32)
    for n, value in enumerate(values):
        out = jnp.where(lane == n, value, out)
    return out


NT = (((1,), (1,)), ((), ()))


def own_kernel(scale, positive, passages, *refs):
    q_refs, all_q, stats, ordered = refs[:5], refs[5], refs[6], refs[7]
    order_features(passages, ordered)
    ids = lax.axis_index("dp") * 256 + lax.broadcasted_iota(jnp.int32, (1, 256), 1)
    for row in (0, 256, 512, 768):
        q = jnp.concatenate(
            [query_block(q_refs, row, n, m) for n in range(4) for m in range(4)], axis=1
        )
        rows = slice(row, row + 256)
        all_q[rows, :] = q
        wq = q.astype(F32)
        factor = scale[0] * lax.rsqrt(jnp.sum(wq * wq, axis=1, keepdims=True) + 1e-06)
        scores = lax.dot_general(q, ordered[...], NT, preferred_element_type=F32) * factor
        hit = ids == picks_of(positive, row)
        chosen = jnp.sum(jnp.where(hit, scores, 0.0), axis=1, keepdims=True)
        top = jnp.max(scores, axis=1, keepdims=True)
        total = jnp.sum(jnp.exp(scores - top), axis=1, keepdims=True)
        stats[rows, :] = lanes(top, total, chosen, factor)


def other_kernel(positive, passages, all_q, early, out, ordered, stats):
    order_features(passages, ordered)
    dp = lax.axis_index("dp")
    first = (dp + along(lax.rem(dp, NC))) * 256
    ids = first + lax.broadcasted_iota(jnp.int32, (1, 256), 1)

    for row in (0, 256, 512, 768):
        rows = pl.ds(row, 256)
        have = early[rows, :]
        factor = have[:, 3:4]
        scores = lax.dot_general(all_q[rows, :], ordered[...], NT, preferred_element_type=F32)
        scores = scores * factor
        hit = ids == picks_of(positive, row)
        chosen = jnp.sum(jnp.where(hit, scores, 0.0), axis=1, keepdims=True) + have[:, 2:3]
        top = jnp.maximum(jnp.max(scores, axis=1, keepdims=True), have[:, 0:1])
        total = jnp.sum(jnp.exp(scores - top), axis=1, keepdims=True)
        total = total + have[:, 1:2] * jnp.exp(have[:, 0:1] - top)
        stats[rows, :] = lanes(top, total, chosen)
    out[...] = jnp.transpose(stats[...])[0:8, :]


def score(scale, positive, mine, other, blocks):
    vmem = pl.BlockSpec(memory_space=pltpu.VMEM)
    smem = pl.BlockSpec(memory_space=pltpu.SMEM)
    params = pltpu.CompilerParams(vmem_limit_bytes=24 << 20)
    cost = pl.CostEstimate(
        flops=2 * 1024 * 256 * 4096, bytes_accessed=1 << 20, transcendentals=1024 * 256
    )
    all_q, early = pl.pallas_call(
        own_kernel,
        out_shape=(
            jax.ShapeDtypeStruct((1024, 4096), BF),
            jax.ShapeDtypeStruct((1024, 128), F32),
        ),
        in_specs=[smem] + [vmem] * 7,
        out_specs=(vmem, vmem),
        scratch_shapes=[pltpu.VMEM((256, 4096), BF)],
        compiler_params=params,
        cost_estimate=cost,
    )(scale, positive, mine, *blocks)
    return pl.pallas_call(
        other_kernel,
        out_shape=jax.ShapeDtypeStruct((8, 1024), F32),
        in_specs=[vmem] * 4,
        out_specs=vmem,
        scratch_shapes=[pltpu.VMEM((256, 4096), BF), pltpu.VMEM((1024, 128), F32)],
        compiler_params=params,
        cost_estimate=cost,
    )(positive, other, all_q, early)


ANY = pl.BlockSpec(memory_space=pl.ANY)


def fence(token):
    return pl.pallas_call(
        lambda token, out: None,
        out_shape=jax.ShapeDtypeStruct(token.shape, token.dtype),
        in_specs=[ANY],
        out_specs=ANY,
        input_output_aliases={0: 0},
        compiler_params=pltpu.CompilerParams(vmem_limit_bytes=1 << 20),
        cost_estimate=pl.CostEstimate(flops=20 * 10**9, bytes_accessed=8192, transcendentals=0),
    )(token)


def copied(rows_out, cuts, *arrays):
    def kernel(*refs):
        ins, outs, sems = refs[: len(arrays)], refs[len(arrays) : -1], refs[-1]
        copies = [
            pltpu.make_async_copy(
                ins[i].at[pl.ds(at, rows)], outs[o].at[pl.ds(to, rows)], sems.at[n]
            )
            for n, (i, at, rows, o, to) in enumerate(cuts)
        ]
        for copy in copies:
            copy.start()
        for copy in copies:
            copy.wait()

    return pl.pallas_call(
        kernel,
        out_shape=tuple(jax.ShapeDtypeStruct((rows, arrays[0].shape[1]), BF) for rows in rows_out),
        in_specs=[ANY] * len(arrays),
        out_specs=(ANY,) * len(rows_out),
        scratch_shapes=[pltpu.SemaphoreType.DMA((len(cuts),))],
        compiler_params=pltpu.CompilerParams(vmem_limit_bytes=1 << 20),
        cost_estimate=pl.CostEstimate(flops=10**6, bytes_accessed=1 << 20, transcendentals=0),
    )(*arrays)


def merge(parts):
    top = parts[0][0]
    for p in parts[1:]:
        top = jnp.maximum(top, p[0])
    total = sum(p[1] * jnp.exp(p[0] - top) for p in parts)
    chosen = sum(p[2] for p in parts)
    return jnp.stack([top, total, chosen])


def per_device(hidden, gain, seg_start, owner, queries, positive, logit_scale):
    core = lax.axis_index("dp") % NC
    half = queries.shape[0] // 2

    own = lax.dynamic_slice_in_dim(queries, core * half, half)
    away = lax.dynamic_slice_in_dim(queries, (1 - core) * half, half)
    back = move(away, dc=1)
    block = jnp.where(
        core == 0, jnp.concatenate([own, back], 1), jnp.concatenate([back, own], 1)
    )
    packed, info, pick, token = pool(seg_start, owner, gain[None, :], hidden)

    got = {("q", 0): block, ("f", 0): packed, ("b", 0): packed}
    last = []
    token = [token]

    def take(names):
        keys = [*names, *(k for k in last if k not in names)]
        *tied, mark = barrier((*(got[k] for k in keys), token[0]))
        got.update(zip(keys, tied))
        token[0] = fence(mark)
        last[:] = names

    def step(*names):
        take([(stream, n - 1) for stream, n in names])
        for stream, n in names:
            got[stream, n] = turn(got[stream, n - 1], 1 if stream == "f" else -1)

    got["f", 1], got["b", 1] = turn(packed, 1), turn(packed, -1)
    take([("q", 0)])
    got["+", 1], got["-", 1] = pass_on(got["q", 0], 0, 1), pass_on(got["q", 0], 0, -1)
    got["far", 1] = pass_on(got["q", 0], 0, 2)
    step(("f", 2), ("b", 2))
    take([("+", 1), ("-", 1), ("far", 1)])
    cuts = [(n, 0, half, 0, half * n) for n in range(4)]
    (line,) = copied((4 * half,), cuts, block, got["+", 1], got["-", 1], got["far", 1])
    got["+", 3], got["-", 3] = pass_on(line, 1, 1), pass_on(line, 1, -1)
    step(("f", 3), ("b", 3))
    take([("+", 3), ("-", 3)])
    cuts = [(0, 0, 2 * half, 0, 0), (1, 2 * half, 2 * half, 1, 0)]
    up, down = copied((2 * half, 2 * half), cuts, got["+", 3], got["-", 3])
    got["+", 4], got["-", 4] = pass_on(up, 1, 1), pass_on(down, 1, -1)
    take([("f", 3), ("b", 3)])
    cuts = [(0, 0, CUT, 0, 0), (1, CUT, PACKED - CUT, 1, 0)]
    up, down = copied((CUT, PACKED - CUT), cuts, got["f", 3], got["b", 3])
    got["f", 4], got["b", 4] = turn(up, 1), turn(down, -1)

    order = [packed, *(got[k, n] for n in (1, 2, 3, 4) for k in "fb")]
    mine = embed(info, token[0], order)
    late = [("+", 4), ("-", 4)]
    mine, *rest = barrier((mine, *(got[k] for k in late)))
    got.update(zip(late, rest))
    other = move(mine, dc=1)
    blocks = [line, *(got[k] for k in (("+", 3), ("-", 3), ("+", 4), ("-", 4)))]
    stats = score(logit_scale, positive.reshape(16, 128), mine, other, blocks)
    pooled = jnp.dot(pick, mine, preferred_element_type=F32).astype(BF)

    stats = stats[:3]
    stats = merge([stats, move(stats, dx=1), move(stats, dx=-1), move(stats, dx=2)])
    stats = merge([stats, move(stats, dy=1), move(stats, dy=-1), move(stats, dy=2)])
    part = stats[2] - stats[0] - jnp.log(stats[1])
    rest = move(part, dc=1)
    log_prob = jnp.where(core == 0, jnp.concatenate([part, rest]), jnp.concatenate([rest, part]))
    return pooled, log_prob


def solution(mesh):
    in_specs = (
        P("dp", "seq", None),
        P(),
        P("dp", None),
        P("dp", None),
        P("seq", "dp"),
        P("seq"),
        P(),
    )
    out_specs = (P(("dp", "seq"), None), P("seq"))
    return jax.shard_map(
        per_device, mesh=mesh, in_specs=in_specs, out_specs=out_specs, check_vma=False
    )
```

time: 362 us -> 105 us (0.29); the launches traced: 358 us -> 105 us
  blocking collectives: 187 us -> 0 us
  waiting for transfers between devices: 120 us -> 41.8 us
  starting transfers between devices: 0.12 us -> 39.8 us
  other arithmetic: 20 us -> 0.92 us
  Pallas kernels: 0 us -> 16.3 us
  between operations: 16.2 us -> 1.48 us
  matrix products: 13.4 us -> 1.17 us
    psum x1 -> x0, blocking collectives: 119 us -> none  [per_device(): total, chosen = lax.psum((local_total, pos_part), 'dp')]
    pmax x1 -> x0, blocking collectives: 68 us -> none  [per_device(): top = lax.pmax(local_top, 'dp')]
    all_gather x2 -> x0, waiting for transfers between devices: 61.2 us -> none  [the longest x1 31.9 us: per_device(): passages = lax.all_gather(pooled, 'seq', axis=0, tiled=True)]
    reduce_scatter x1 -> x0, waiting for transfers between devices: 58.6 us -> none  [per_device(): lax.psum_scatter(partial_value, 'seq', scatter_dimension=0, tiled=True)]
    ppermute x0 -> x24, waiting for transfers between devices: none -> 41.8 us  [the longest x8 22.2 us: turn(): return lax.ppermute(value, 'seq', [(i, (i + step) % NZ) for i in range(NZ)])]
    ppermute x0 -> x24, starting transfers between devices: none -> 39.8 us  [the longest x9 18.9 us: move(): return lax.ppermute(value, 'dp', pairs)]
    pallas_call x0 -> x13, Pallas kernels: none -> 16.3 us  [the longest x1 6.85 us: pool(): pl.pallas_call(pool_kernel, out_shape=(jax.ShapeDtypeStruct((PACKED, 512)...]
    dot_general x2 -> x1, matrix products: 13.4 us -> 1.17 us  [per_device(): pooled = jnp.dot(pick, mine, preferred_element_type=F32).astype(BF)]
  transfers between devices with their start and end apart: 3 -> 24, of which waited for: 3 -> 7; matrix products, arithmetic and copies ran while one was open for 3% -> 1% of each run, Pallas kernels for 0% -> 12%
where the time goes in v2:
time: 105 us
  waiting for transfers between devices  41.8 us (40%)
  starting transfers between devices  39.8 us (38%)
  Pallas kernels  16.3 us (16%)
  local copies, waits for them, and re-layouts  3.68 us (4%)
  between operations  1.48 us (1%)
  matrix products  1.17 us (1%)
    ppermute x8, waiting for transfers between devices, turn(): return lax.ppermute(value, 'seq', [(i, (i + step) % NZ) for i in range(NZ)])  22.2 us
    ppermute x9, starting transfers between devices, move(): return lax.ppermute(value, 'dp', pairs)  18.9 us
    ppermute x7, waiting for transfers between devices, pass_on(): lax.ppermute(value, ('dp', 'seq'), _hop(lambda c: ((c + second) % 2, step)))  14.1 us
    ppermute x8, starting transfers between devices, turn(): return lax.ppermute(value, 'seq', [(i, (i + step) % NZ) for i in range(NZ)])  10.9 us
    ppermute x7, starting transfers between devices, pass_on(): lax.ppermute(value, ('dp', 'seq'), _hop(lambda c: ((c + second) % 2, step)))  10.1 us
    pallas_call x1, Pallas kernels, pool(): pl.pallas_call(pool_kernel, out_shape=(jax.ShapeDtypeStruct((PACKED, 512)...  6.85 us
    ppermute x9, waiting for transfers between devices, move(): return lax.ppermute(value, 'dp', pairs)  5.41 us
    pallas_call x1, Pallas kernels, score(): pl.pallas_call(own_kernel, out_shape=(jax.ShapeDtypeStruct((1024, 4096),...  3.53 us
  transfers between devices with their start and end apart: 24, of which 7 were waited for; matrix products, arithmetic and copies ran while one was open for 1% of the time, Pallas kernels for 12%

profile of v2, /device:TPU:1, one launch (start us, length us, event | category | flops | bytes accessed | tf_op | source)
XLA Modules:
  0.0 105.2 jit_solution(13609051638030329823)
XLA Ops:
  1.7 3.3 %collective-permute-start.2 = (bf16[1024,128]{1,0:T(8,128)(2,1)S(1)}, bf16[1024,128]{1,0:T(8,128)(2,1)S(1)}, u32[]{:S(2)}, u32[]{:S(2)}) collective-permute-start(bf16[1024,128]{1,0:T(8,128)(2,1)S(1)} %get-tuple-element.77), channel_id=1, source_target_pairs={{0,8},{8,0},{16,24},{24,16},{32,40},{40,32},{48,56},{56,48},{64,72... | collective-permute-start | bytes 786440 | tf_op jit(solution)/shard_map/ppermute | solution.py:28
  5.1 6.9 %shard_map.86 = (bf16[528,512]{1,0:T(8,128)(2,1)}, f32[256,256]{1,0:T(8,128)}, bf16[32,256]{1,0:T(8,128)(2,1)}, f32[8,128]{1,0:T(8,128)}) custom-call(s32[1,256]{1,0:T(1,128)} %starts.1, s32[1,256]{1,0:T(1,128)} %owner.1, f32[1,4096]{1,0:T(1,128)} %bitcast.21, bf16[1,1024,4096]{2,1,0:T(8,128)(2,1)} %hidden.1), custom_call_target="tpu_custom_call" | custom-call | flops 1073741824 | bytes 8388608 | tf_op jit(solution)/shard_map/pallas_call | solution.py:124
  12.0 3.9 %collective-permute-start.1 = (bf16[528,512]{1,0:T(8,128)(2,1)}, bf16[528,512]{1,0:T(8,128)(2,1)S(1)}, u32[]{:S(2)}, u32[]{:S(2)}) collective-permute-start(bf16[528,512]{1,0:T(8,128)(2,1)} %get-tuple-element.41.refs_0_), channel_id=1, source_target_pairs={{0,7},{1,0},{2,1},{3,2},{4,3},{5,4},{6,5},{7,6},{8,15},{9,8},{10,9... | collective-permute-start | bytes 1622024 | tf_op jit(solution)/shard_map/ppermute | solution.py:46
  16.1 1.4 %collective-permute-start.5 = (bf16[1024,256]{1,0:T(8,128)(2,1)S(1)}, bf16[1024,256]{1,0:T(8,128)(2,1)S(1)}, u32[]{:S(2)}, u32[]{:S(2)}) collective-permute-start(bf16[1024,256]{1,0:T(8,128)(2,1)S(1)} %maximum_select_fusion.refs_0_), channel_id=1, source_target_pairs={{0,64},{1,65},{2,66},{3,67},{4,68},{5,69},{6,70},{7,71},{8,24},{9,... | collective-permute-start | bytes 1572872 | tf_op jit(solution)/shard_map/ppermute | solution.py:50
  17.5 1.5 %collective-permute-start.6 = (bf16[1024,256]{1,0:T(8,128)(2,1)S(1)}, bf16[1024,256]{1,0:T(8,128)(2,1)S(1)}, u32[]{:S(2)}, u32[]{:S(2)}) collective-permute-start(bf16[1024,256]{1,0:T(8,128)(2,1)S(1)} %maximum_select_fusion.refs_0_), channel_id=1, source_target_pairs={{0,192},{1,193},{2,194},{3,195},{4,196},{5,197},{6,198},{7,199},{8... | collective-permute-start | bytes 1572872 | tf_op jit(solution)/shard_map/ppermute | solution.py:50
  19.0 1.6 %collective-permute-start.7 = (bf16[1024,256]{1,0:T(8,128)(2,1)S(1)}, bf16[1024,256]{1,0:T(8,128)(2,1)S(1)}, u32[]{:S(2)}, u32[]{:S(2)}) collective-permute-start(bf16[1024,256]{1,0:T(8,128)(2,1)S(1)} %maximum_select_fusion.refs_0_), channel_id=1, source_target_pairs={{0,128},{1,129},{2,130},{3,131},{4,132},{5,133},{6,134},{7,135},{8... | collective-permute-start | bytes 1572872 | tf_op jit(solution)/shard_map/ppermute | solution.py:50
  21.9 6.8 %collective-permute-done.refs_1_ = bf16[528,512]{1,0:T(8,128)(2,1)S(1)} collective-permute-done((bf16[528,512]{1,0:T(8,128)(2,1)}, bf16[528,512]{1,0:T(8,128)(2,1)S(1)}, u32[]{:S(2)}, u32[]{:S(2)}) %collective-permute-start) | collective-permute-done | bytes 540704 | tf_op jit(solution)/shard_map/ppermute | solution.py:46
  30.0 2.7 %collective-permute-start.4 = (bf16[528,512]{1,0:T(8,128)(2,1)S(1)}, bf16[528,512]{1,0:T(8,128)(2,1)S(1)}, u32[]{:S(2)}, u32[]{:S(2)}) collective-permute-start(bf16[528,512]{1,0:T(8,128)(2,1)S(1)} %collective-permute-done.1.refs_2_), channel_id=1, source_target_pairs={{0,7},{1,0},{2,1},{3,2},{4,3},{5,4},{6,5},{7,6},{8,15},{9,8},{10,9... | collective-permute-start | bytes 1622024 | tf_op jit(solution)/shard_map/ppermute | solution.py:46
  32.8 1.3 %collective-permute-start.10 = (bf16[4096,256]{1,0:T(8,128)(2,1)S(1)}, bf16[4096,256]{1,0:T(8,128)(2,1)S(1)}, u32[]{:S(2)}, u32[]{:S(2)}) collective-permute-start(bf16[4096,256]{1,0:T(8,128)(2,1)S(1)} %shard_map.90.refs_0_), channel_id=1, source_target_pairs={{0,16},{1,17},{2,18},{3,19},{4,20},{5,21},{6,22},{7,23},{8,72},{9,... | collective-permute-start | bytes 6291464 | tf_op jit(solution)/shard_map/ppermute | solution.py:50
  34.1 1.5 %collective-permute-start.11 = (bf16[4096,256]{1,0:T(8,128)(2,1)S(1)}, bf16[4096,256]{1,0:T(8,128)(2,1)S(1)}, u32[]{:S(2)}, u32[]{:S(2)}) collective-permute-start(bf16[4096,256]{1,0:T(8,128)(2,1)S(1)} %shard_map.90.refs_0_), channel_id=1, source_target_pairs={{0,48},{1,49},{2,50},{3,51},{4,52},{5,53},{6,54},{7,55},{8,200},{9... | collective-permute-start | bytes 6291464 | tf_op jit(solution)/shard_map/ppermute | solution.py:50
  35.6 8.8 %collective-permute-done.3.refs_3_ = bf16[528,512]{1,0:T(8,128)(2,1)S(1)} collective-permute-done((bf16[528,512]{1,0:T(8,128)(2,1)S(1)}, bf16[528,512]{1,0:T(8,128)(2,1)S(1)}, u32[]{:S(2)}, u32[]{:S(2)}) %collective-permute-start.3) | collective-permute-done | bytes 540704 | tf_op jit(solution)/shard_map/ppermute | solution.py:46
  44.4 1.1 %collective-permute-start.8 = (bf16[528,512]{1,0:T(8,128)(2,1)S(1)}, bf16[528,512]{1,0:T(8,128)(2,1)S(1)}, u32[]{:S(2)}, u32[]{:S(2)}) collective-permute-start(bf16[528,512]{1,0:T(8,128)(2,1)S(1)} %collective-permute-done.3.refs_3_), channel_id=1, source_target_pairs={{0,1},{1,2},{2,3},{3,4},{4,5},{5,6},{6,7},{7,0},{8,9},{9,10},{10,1... | collective-permute-start | bytes 1622024 | tf_op jit(solution)/shard_map/ppermute | solution.py:46
  45.5 1.6 %collective-permute-start.9 = (bf16[528,512]{1,0:T(8,128)(2,1)S(1)}, bf16[528,512]{1,0:T(8,128)(2,1)S(1)}, u32[]{:S(2)}, u32[]{:S(2)}) collective-permute-start(bf16[528,512]{1,0:T(8,128)(2,1)S(1)} %collective-permute-done.4.refs_4_), channel_id=1, source_target_pairs={{0,7},{1,0},{2,1},{3,2},{4,3},{5,4},{6,5},{7,6},{8,15},{9,8},{10,9... | collective-permute-start | bytes 1622024 | tf_op jit(solution)/shard_map/ppermute | solution.py:46
  47.1 12.2 %collective-permute-done.10.refs_0_.refs_1_ = bf16[4096,256]{1,0:T(8,128)(2,1)S(1)} collective-permute-done((bf16[4096,256]{1,0:T(8,128)(2,1)S(1)}, bf16[4096,256]{1,0:T(8,128)(2,1)S(1)}, u32[]{:S(2)}, u32[]{:S(2)}) %collective-permute-start.10) | collective-permute-done | bytes 2097184 | tf_op jit(solution)/shard_map/ppermute | solution.py:50
  59.5 1.3 %collective-permute-start.14 = (bf16[2048,256]{1,0:T(8,128)(2,1)S(1)}, bf16[2048,256]{1,0:T(8,128)(2,1)S(1)}, u32[]{:S(2)}, u32[]{:S(2)}) collective-permute-start(bf16[2048,256]{1,0:T(8,128)(2,1)S(1)} %get-tuple-element.67), channel_id=1, source_target_pairs={{0,16},{1,17},{2,18},{3,19},{4,20},{5,21},{6,22},{7,23},{8,72},{9,... | collective-permute-start | bytes 3145736 | tf_op jit(solution)/shard_map/ppermute | solution.py:50
  60.8 1.5 %collective-permute-start.15 = (bf16[2048,256]{1,0:T(8,128)(2,1)S(1)}, bf16[2048,256]{1,0:T(8,128)(2,1)S(1)}, u32[]{:S(2)}, u32[]{:S(2)}) collective-permute-start(bf16[2048,256]{1,0:T(8,128)(2,1)S(1)} %get-tuple-element.68), channel_id=1, source_target_pairs={{0,48},{1,49},{2,50},{3,51},{4,52},{5,53},{6,54},{7,55},{8,200},{9... | collective-permute-start | bytes 3145736 | tf_op jit(solution)/shard_map/ppermute | solution.py:50
  62.4 1.4 %collective-permute-start.13 = (bf16[272,512]{1,0:T(8,128)(2,1)S(1)}, bf16[272,512]{1,0:T(8,128)(2,1)S(1)}, u32[]{:S(2)}, u32[]{:S(2)}) collective-permute-start(bf16[272,512]{1,0:T(8,128)(2,1)S(1)} %get-tuple-element.66), channel_id=1, source_target_pairs={{0,7},{1,0},{2,1},{3,2},{4,3},{5,4},{6,5},{7,6},{8,15},{9,8},{10,9... | collective-permute-start | bytes 835592 | tf_op jit(solution)/shard_map/ppermute | solution.py:46
  64.0 6.6 %collective-permute-done.12.refs_7_ = bf16[256,512]{1,0:T(8,128)(2,1)S(1)} collective-permute-done((bf16[256,512]{1,0:T(8,128)(2,1)S(1)}, bf16[256,512]{1,0:T(8,128)(2,1)S(1)}, u32[]{:S(2)}, u32[]{:S(2)}) %collective-permute-start.12) | collective-permute-done | bytes 262176 | tf_op jit(solution)/shard_map/ppermute | solution.py:46
  70.6 2.2 %shard_map.95.passages = bf16[256,4096]{1,0:T(8,128)(2,1)S(1)} custom-call(f32[256,256]{1,0:T(8,128)S(1)} %copy-done.1, f32[8,128]{1,0:T(8,128)S(1)} %shard_map.93._, bf16[528,512]{1,0:T(8,128)(2,1)S(1)} %copy-done, bf16[528,512]{1,0:T(8,128)(2,1)S(1)} %collective-permute-done.refs_1_, bf16[528,512]{1,0:T(8,128)(2,1)S(1)} %collective-permute-done.1.refs_2_, ...), custom_call_target="tpu_custom_call" | custom-call | flops 1342177280 | bytes 7340032 | tf_op jit(solution)/shard_map/pallas_call | solution.py:191
  72.8 1.9 %collective-permute-done.14.refs_3_ = bf16[2048,256]{1,0:T(8,128)(2,1)S(1)} collective-permute-done((bf16[2048,256]{1,0:T(8,128)(2,1)S(1)}, bf16[2048,256]{1,0:T(8,128)(2,1)S(1)}, u32[]{:S(2)}, u32[]{:S(2)}) %collective-permute-start.14) | collective-permute-done | bytes 1048608 | tf_op jit(solution)/shard_map/ppermute | solution.py:50
  74.7 3.6 %collective-permute-start.16 = (bf16[256,4096]{1,0:T(8,128)(2,1)S(1)}, bf16[256,4096]{1,0:T(8,128)(2,1)S(1)}, u32[]{:S(2)}, u32[]{:S(2)}) collective-permute-start(bf16[256,4096]{1,0:T(8,128)(2,1)S(1)} %shard_map.95.passages), channel_id=1, source_target_pairs={{0,8},{8,0},{16,24},{24,16},{32,40},{40,32},{48,56},{56,48},{64,72... | collective-permute-start | bytes 6291464 | tf_op jit(solution)/shard_map/ppermute | solution.py:28
  79.0 3.5 %shard_map.97 = (bf16[1024,4096]{1,0:T(8,128)(2,1)S(1)}, f32[1024,128]{1,0:T(8,128)S(1)}) custom-call(f32[1]{0:T(128)S(6)} %copy.21.scale, s32[16,128]{1,0:T(8,128)S(1)} %bitcast.19, bf16[256,4096]{1,0:T(8,128)(2,1)S(1)} %shard_map.95.passages, bf16[4096,256]{1,0:T(8,128)(2,1)S(1)} %shard_map.90.refs_0_, ...), custom_call_target="tpu_custom_call" | custom-call | flops 2147483648 | bytes 1048576 | tf_op jit(solution)/shard_map/pallas_call | solution.py:292
  82.6 3.3 %shard_map.98 = f32[8,1024]{1,0:T(8,128)S(1)} custom-call(s32[16,128]{1,0:T(8,128)S(1)} %bitcast.20, bf16[256,4096]{1,0:T(8,128)(2,1)S(1)} %collective-permute-done.16.passages, bf16[1024,4096]{1,0:T(8,128)(2,1)S(1)} %get-tuple-element.74.all_q, f32[1024,128]{1,0:T(8,128)S(1)} %get-tuple-element.75.early), custom_call_target="tpu_custom_call" | custom-call | flops 2147483648 | bytes 1048576 | tf_op jit(solution)/shard_map/pallas_call | solution.py:304
  85.9 1.5 %collective-permute-start.17 = (f32[3,1024]{1,0:T(4,128)S(1)}, f32[3,1024]{1,0:T(4,128)S(1)}, u32[]{:S(2)}, u32[]{:S(2)}) collective-permute-start(f32[3,1024]{1,0:T(4,128)S(1)} %slice.99), channel_id=1, source_target_pairs={{0,64},{8,72},{16,80},{24,88},{32,96},{40,104},{48,112},{56,120},{... | collective-permute-start | bytes 36872 | tf_op jit(solution)/shard_map/ppermute | solution.py:28
  87.3 1.5 %collective-permute-start.18 = (f32[3,1024]{1,0:T(4,128)S(1)}, f32[3,1024]{1,0:T(4,128)S(1)}, u32[]{:S(2)}, u32[]{:S(2)}) collective-permute-start(f32[3,1024]{1,0:T(4,128)S(1)} %slice.99), channel_id=1, source_target_pairs={{0,192},{8,200},{16,208},{24,216},{32,224},{40,232},{48,240},{56,2... | collective-permute-start | bytes 36872 | tf_op jit(solution)/shard_map/ppermute | solution.py:28
  88.8 1.5 %collective-permute-start.19 = (f32[3,1024]{1,0:T(4,128)S(1)}, f32[3,1024]{1,0:T(4,128)S(1)}, u32[]{:S(2)}, u32[]{:S(2)}) collective-permute-start(f32[3,1024]{1,0:T(4,128)S(1)} %slice.99), channel_id=1, source_target_pairs={{0,128},{8,136},{16,144},{24,152},{32,160},{40,168},{48,176},{56,1... | collective-permute-start | bytes 36872 | tf_op jit(solution)/shard_map/ppermute | solution.py:28
  90.3 2.6 %collective-permute-done.19 = f32[3,1024]{1,0:T(4,128)S(1)} collective-permute-done((f32[3,1024]{1,0:T(4,128)S(1)}, f32[3,1024]{1,0:T(4,128)S(1)}, u32[]{:S(2)}, u32[]{:S(2)}) %collective-permute-start.19) | collective-permute-done | bytes 12320 | tf_op jit(solution)/shard_map/ppermute | solution.py:28
  94.1 1.7 %collective-permute-start.21 = (f32[3,1024]{1,0:T(4,128)S(1)}, f32[3,1024]{1,0:T(4,128)S(1)}, u32[]{:S(2)}, u32[]{:S(2)}) collective-permute-start(f32[3,1024]{1,0:T(4,128)S(1)} %pad_maximum_fusion), channel_id=1, source_target_pairs={{0,48},{8,56},{16,0},{24,8},{32,16},{40,24},{48,32},{56,40},{64,11... | collective-permute-start | bytes 36872 | tf_op jit(solution)/shard_map/ppermute | solution.py:28
  95.7 1.2 %collective-permute-start.22 = (f32[3,1024]{1,0:T(4,128)S(1)}, f32[3,1024]{1,0:T(4,128)S(1)}, u32[]{:S(2)}, u32[]{:S(2)}) collective-permute-start(f32[3,1024]{1,0:T(4,128)S(1)} %pad_maximum_fusion), channel_id=1, source_target_pairs={{0,32},{8,40},{16,48},{24,56},{32,0},{40,8},{48,16},{56,24},{64,96... | collective-permute-start | bytes 36872 | tf_op jit(solution)/shard_map/ppermute | solution.py:28
  97.0 2.8 %collective-permute-done.22 = f32[3,1024]{1,0:T(4,128)S(1)} collective-permute-done((f32[3,1024]{1,0:T(4,128)S(1)}, f32[3,1024]{1,0:T(4,128)S(1)}, u32[]{:S(2)}, u32[]{:S(2)}) %collective-permute-start.22) | collective-permute-done | bytes 12320 | tf_op jit(solution)/shard_map/ppermute | solution.py:28
  99.9 3.5 %collective-permute-start.23 = (f32[1024]{0:T(1024)S(1)}, f32[1024]{0:T(1024)S(1)}, u32[]{:S(2)}, u32[]{:S(2)}) collective-permute-start(f32[1024]{0:T(1024)S(1)} %log_subtract_fusion), channel_id=1, source_target_pairs={{0,8},{8,0},{16,24},{24,16},{32,40},{40,32},{48,56},{56,48},{64,72... | collective-permute-start | bytes 12296 | tf_op jit(solution)/shard_map/ppermute | solution.py:28
  103.4 1.2 %convolution_convert_fusion = bf16[32,4096]{1,0:T(8,128)(2,1)} fusion(bf16[32,256]{1,0:T(8,128)(2,1)S(1)} %copy-done.8, bf16[256,4096]{1,0:T(8,128)(2,1)S(1)} %shard_map.95.passages), kind=kOutput, calls=%fused_computation | convolution fusion | flops 67239936 | bytes 2375680 | tf_op jit(solution)/shard_map/dot_general | solution.py:419
  (59 shorter events, 6.4 us)
Async XLA Ops:
  1.7 14.2 %collective-permute-start.2 = (bf16[1024,128]{1,0:T(8,128)(2,1)S(1)}, bf16[1024,128]{1,0:T(8,128)(2,1)S(1)}, u32[]{:S(2)}, u32[]{:S(2)}) collective-permute-start(bf16[1024,128]{1,0:T(8,128)(2,1)S(1)} %get-tuple-element.77), channel_id=1, source_target_pairs={{0,8},{8,0},{16,24},{24,16},{32,40},{40,32},{48,56},{56,48},{64,72... | collective-permute-start | bytes 786440 | tf_op jit(solution)/shard_map/ppermute | solution.py:28
  11.9 16.8 %collective-permute-start = (bf16[528,512]{1,0:T(8,128)(2,1)}, bf16[528,512]{1,0:T(8,128)(2,1)S(1)}, u32[]{:S(2)}, u32[]{:S(2)}) collective-permute-start(bf16[528,512]{1,0:T(8,128)(2,1)} %get-tuple-element.41.refs_0_), channel_id=1, source_target_pairs={{0,1},{1,2},{2,3},{3,4},{4,5},{5,6},{6,7},{7,0},{8,9},{9,10},{10,1... | collective-permute-start | bytes 1622024 | tf_op jit(solution)/shard_map/ppermute | solution.py:46
  12.0 16.7 %collective-permute-start.1 = (bf16[528,512]{1,0:T(8,128)(2,1)}, bf16[528,512]{1,0:T(8,128)(2,1)S(1)}, u32[]{:S(2)}, u32[]{:S(2)}) collective-permute-start(bf16[528,512]{1,0:T(8,128)(2,1)} %get-tuple-element.41.refs_0_), channel_id=1, source_target_pairs={{0,7},{1,0},{2,1},{3,2},{4,3},{5,4},{6,5},{7,6},{8,15},{9,8},{10,9... | collective-permute-start | bytes 1622024 | tf_op jit(solution)/shard_map/ppermute | solution.py:46
  16.1 16.5 %collective-permute-start.5 = (bf16[1024,256]{1,0:T(8,128)(2,1)S(1)}, bf16[1024,256]{1,0:T(8,128)(2,1)S(1)}, u32[]{:S(2)}, u32[]{:S(2)}) collective-permute-start(bf16[1024,256]{1,0:T(8,128)(2,1)S(1)} %maximum_select_fusion.refs_0_), channel_id=1, source_target_pairs={{0,64},{1,65},{2,66},{3,67},{4,68},{5,69},{6,70},{7,71},{8,24},{9,... | collective-permute-start | bytes 1572872 | tf_op jit(solution)/shard_map/ppermute | solution.py:50
  17.5 15.2 %collective-permute-start.6 = (bf16[1024,256]{1,0:T(8,128)(2,1)S(1)}, bf16[1024,256]{1,0:T(8,128)(2,1)S(1)}, u32[]{:S(2)}, u32[]{:S(2)}) collective-permute-start(bf16[1024,256]{1,0:T(8,128)(2,1)S(1)} %maximum_select_fusion.refs_0_), channel_id=1, source_target_pairs={{0,192},{1,193},{2,194},{3,195},{4,196},{5,197},{6,198},{7,199},{8... | collective-permute-start | bytes 1572872 | tf_op jit(solution)/shard_map/ppermute | solution.py:50
  19.0 13.6 %collective-permute-start.7 = (bf16[1024,256]{1,0:T(8,128)(2,1)S(1)}, bf16[1024,256]{1,0:T(8,128)(2,1)S(1)}, u32[]{:S(2)}, u32[]{:S(2)}) collective-permute-start(bf16[1024,256]{1,0:T(8,128)(2,1)S(1)} %maximum_select_fusion.refs_0_), channel_id=1, source_target_pairs={{0,128},{1,129},{2,130},{3,131},{4,132},{5,133},{6,134},{7,135},{8... | collective-permute-start | bytes 1572872 | tf_op jit(solution)/shard_map/ppermute | solution.py:50
  20.6 0.7 copy-start.3
  21.3 0.6 copy-start.4
  28.7 0.7 copy-start.5
  30.0 14.4 %collective-permute-start.3 = (bf16[528,512]{1,0:T(8,128)(2,1)S(1)}, bf16[528,512]{1,0:T(8,128)(2,1)S(1)}, u32[]{:S(2)}, u32[]{:S(2)}) collective-permute-start(bf16[528,512]{1,0:T(8,128)(2,1)S(1)} %collective-permute-done.refs_1_), channel_id=1, source_target_pairs={{0,1},{1,2},{2,3},{3,4},{4,5},{5,6},{6,7},{7,0},{8,9},{9,10},{10,1... | collective-permute-start | bytes 1622024 | tf_op jit(solution)/shard_map/ppermute | solution.py:46
  30.0 5.6 %copy-start.7 = (f32[8,128]{1,0:T(8,128)S(1)}, f32[8,128]{1,0:T(8,128)}, u32[]{:S(2)}) copy-start(f32[8,128]{1,0:T(8,128)} %copy-done.6) | copy-start | bytes 12292
  30.0 14.4 %collective-permute-start.4 = (bf16[528,512]{1,0:T(8,128)(2,1)S(1)}, bf16[528,512]{1,0:T(8,128)(2,1)S(1)}, u32[]{:S(2)}, u32[]{:S(2)}) collective-permute-start(bf16[528,512]{1,0:T(8,128)(2,1)S(1)} %collective-permute-done.1.refs_2_), channel_id=1, source_target_pairs={{0,7},{1,0},{2,1},{3,2},{4,3},{5,4},{6,5},{7,6},{8,15},{9,8},{10,9... | collective-permute-start | bytes 1622024 | tf_op jit(solution)/shard_map/ppermute | solution.py:46
  32.8 26.5 %collective-permute-start.10 = (bf16[4096,256]{1,0:T(8,128)(2,1)S(1)}, bf16[4096,256]{1,0:T(8,128)(2,1)S(1)}, u32[]{:S(2)}, u32[]{:S(2)}) collective-permute-start(bf16[4096,256]{1,0:T(8,128)(2,1)S(1)} %shard_map.90.refs_0_), channel_id=1, source_target_pairs={{0,16},{1,17},{2,18},{3,19},{4,20},{5,21},{6,22},{7,23},{8,72},{9,... | collective-permute-start | bytes 6291464 | tf_op jit(solution)/shard_map/ppermute | solution.py:50
  34.1 25.2 %collective-permute-start.11 = (bf16[4096,256]{1,0:T(8,128)(2,1)S(1)}, bf16[4096,256]{1,0:T(8,128)(2,1)S(1)}, u32[]{:S(2)}, u32[]{:S(2)}) collective-permute-start(bf16[4096,256]{1,0:T(8,128)(2,1)S(1)} %shard_map.90.refs_0_), channel_id=1, source_target_pairs={{0,48},{1,49},{2,50},{3,51},{4,52},{5,53},{6,54},{7,55},{8,200},{9... | collective-permute-start | bytes 6291464 | tf_op jit(solution)/shard_map/ppermute | solution.py:50
  44.4 17.9 %collective-permute-start.8 = (bf16[528,512]{1,0:T(8,128)(2,1)S(1)}, bf16[528,512]{1,0:T(8,128)(2,1)S(1)}, u32[]{:S(2)}, u32[]{:S(2)}) collective-permute-start(bf16[528,512]{1,0:T(8,128)(2,1)S(1)} %collective-permute-done.3.refs_3_), channel_id=1, source_target_pairs={{0,1},{1,2},{2,3},{3,4},{4,5},{5,6},{6,7},{7,0},{8,9},{9,10},{10,1... | collective-permute-start | bytes 1622024 | tf_op jit(solution)/shard_map/ppermute | solution.py:46
  45.5 16.8 %collective-permute-start.9 = (bf16[528,512]{1,0:T(8,128)(2,1)S(1)}, bf16[528,512]{1,0:T(8,128)(2,1)S(1)}, u32[]{:S(2)}, u32[]{:S(2)}) collective-permute-start(bf16[528,512]{1,0:T(8,128)(2,1)S(1)} %collective-permute-done.4.refs_4_), channel_id=1, source_target_pairs={{0,7},{1,0},{2,1},{3,2},{4,3},{5,4},{6,5},{7,6},{8,15},{9,8},{10,9... | collective-permute-start | bytes 1622024 | tf_op jit(solution)/shard_map/ppermute | solution.py:46
  59.5 15.2 %collective-permute-start.14 = (bf16[2048,256]{1,0:T(8,128)(2,1)S(1)}, bf16[2048,256]{1,0:T(8,128)(2,1)S(1)}, u32[]{:S(2)}, u32[]{:S(2)}) collective-permute-start(bf16[2048,256]{1,0:T(8,128)(2,1)S(1)} %get-tuple-element.67), channel_id=1, source_target_pairs={{0,16},{1,17},{2,18},{3,19},{4,20},{5,21},{6,22},{7,23},{8,72},{9,... | collective-permute-start | bytes 3145736 | tf_op jit(solution)/shard_map/ppermute | solution.py:50
  60.8 13.9 %collective-permute-start.15 = (bf16[2048,256]{1,0:T(8,128)(2,1)S(1)}, bf16[2048,256]{1,0:T(8,128)(2,1)S(1)}, u32[]{:S(2)}, u32[]{:S(2)}) collective-permute-start(bf16[2048,256]{1,0:T(8,128)(2,1)S(1)} %get-tuple-element.68), channel_id=1, source_target_pairs={{0,48},{1,49},{2,50},{3,51},{4,52},{5,53},{6,54},{7,55},{8,200},{9... | collective-permute-start | bytes 3145736 | tf_op jit(solution)/shard_map/ppermute | solution.py:50
  62.4 8.2 %collective-permute-start.13 = (bf16[272,512]{1,0:T(8,128)(2,1)S(1)}, bf16[272,512]{1,0:T(8,128)(2,1)S(1)}, u32[]{:S(2)}, u32[]{:S(2)}) collective-permute-start(bf16[272,512]{1,0:T(8,128)(2,1)S(1)} %get-tuple-element.66), channel_id=1, source_target_pairs={{0,7},{1,0},{2,1},{3,2},{4,3},{5,4},{6,5},{7,6},{8,15},{9,8},{10,9... | collective-permute-start | bytes 835592 | tf_op jit(solution)/shard_map/ppermute | solution.py:46
  63.8 6.7 %copy-start = (bf16[528,512]{1,0:T(8,128)(2,1)S(1)}, bf16[528,512]{1,0:T(8,128)(2,1)}, u32[]{:S(2)}) copy-start(bf16[528,512]{1,0:T(8,128)(2,1)} %get-tuple-element.41.refs_0_) | copy-start | bytes 1622020
  63.8 6.7 %copy-start.1 = (f32[256,256]{1,0:T(8,128)S(1)}, f32[256,256]{1,0:T(8,128)}, u32[]{:S(2)}) copy-start(f32[256,256]{1,0:T(8,128)} %get-tuple-element.40.info) | copy-start | bytes 786436
  63.8 6.7 %collective-permute-start.12 = (bf16[256,512]{1,0:T(8,128)(2,1)S(1)}, bf16[256,512]{1,0:T(8,128)(2,1)S(1)}, u32[]{:S(2)}, u32[]{:S(2)}) collective-permute-start(bf16[256,512]{1,0:T(8,128)(2,1)S(1)} %get-tuple-element.65), channel_id=1, source_target_pairs={{0,1},{1,2},{2,3},{3,4},{4,5},{5,6},{6,7},{7,0},{8,9},{9,10},{10,1... | collective-permute-start | bytes 786440 | tf_op jit(solution)/shard_map/ppermute | solution.py:46
  70.6 8.4 %copy-start.2 = (s32[2048]{0:T(1024)S(1)}, s32[2048]{0:T(1024)}, u32[]{:S(2)}) copy-start(s32[2048]{0:T(1024)} %param.12) | copy-start | bytes 24580
  74.7 7.8 %collective-permute-start.16 = (bf16[256,4096]{1,0:T(8,128)(2,1)S(1)}, bf16[256,4096]{1,0:T(8,128)(2,1)S(1)}, u32[]{:S(2)}, u32[]{:S(2)}) collective-permute-start(bf16[256,4096]{1,0:T(8,128)(2,1)S(1)} %shard_map.95.passages), channel_id=1, source_target_pairs={{0,8},{8,0},{16,24},{24,16},{32,40},{40,32},{48,56},{56,48},{64,72... | collective-permute-start | bytes 6291464 | tf_op jit(solution)/shard_map/ppermute | solution.py:28
  82.5 20.9 %copy-start.8 = (bf16[32,256]{1,0:T(8,128)(2,1)S(1)}, bf16[32,256]{1,0:T(8,128)(2,1)}, u32[]{:S(2)}) copy-start(bf16[32,256]{1,0:T(8,128)(2,1)} %get-tuple-element.39) | copy-start | bytes 49156
  85.9 4.5 %collective-permute-start.17 = (f32[3,1024]{1,0:T(4,128)S(1)}, f32[3,1024]{1,0:T(4,128)S(1)}, u32[]{:S(2)}, u32[]{:S(2)}) collective-permute-start(f32[3,1024]{1,0:T(4,128)S(1)} %slice.99), channel_id=1, source_target_pairs={{0,64},{8,72},{16,80},{24,88},{32,96},{40,104},{48,112},{56,120},{... | collective-permute-start | bytes 36872 | tf_op jit(solution)/shard_map/ppermute | solution.py:28
  87.3 3.0 %collective-permute-start.18 = (f32[3,1024]{1,0:T(4,128)S(1)}, f32[3,1024]{1,0:T(4,128)S(1)}, u32[]{:S(2)}, u32[]{:S(2)}) collective-permute-start(f32[3,1024]{1,0:T(4,128)S(1)} %slice.99), channel_id=1, source_target_pairs={{0,192},{8,200},{16,208},{24,216},{32,224},{40,232},{48,240},{56,2... | collective-permute-start | bytes 36872 | tf_op jit(solution)/shard_map/ppermute | solution.py:28
  88.8 4.1 %collective-permute-start.19 = (f32[3,1024]{1,0:T(4,128)S(1)}, f32[3,1024]{1,0:T(4,128)S(1)}, u32[]{:S(2)}, u32[]{:S(2)}) collective-permute-start(f32[3,1024]{1,0:T(4,128)S(1)} %slice.99), channel_id=1, source_target_pairs={{0,128},{8,136},{16,144},{24,152},{32,160},{40,168},{48,176},{56,1... | collective-permute-start | bytes 36872 | tf_op jit(solution)/shard_map/ppermute | solution.py:28
  93.0 4.0 %collective-permute-start.20 = (f32[3,1024]{1,0:T(4,128)S(1)}, f32[3,1024]{1,0:T(4,128)S(1)}, u32[]{:S(2)}, u32[]{:S(2)}) collective-permute-start(f32[3,1024]{1,0:T(4,128)S(1)} %pad_maximum_fusion), channel_id=1, source_target_pairs={{0,16},{8,24},{16,32},{24,40},{32,48},{40,56},{48,0},{56,8},{64,80... | collective-permute-start | bytes 36872 | tf_op jit(solution)/shard_map/ppermute | solution.py:28
  94.1 2.9 %collective-permute-start.21 = (f32[3,1024]{1,0:T(4,128)S(1)}, f32[3,1024]{1,0:T(4,128)S(1)}, u32[]{:S(2)}, u32[]{:S(2)}) collective-permute-start(f32[3,1024]{1,0:T(4,128)S(1)} %pad_maximum_fusion), channel_id=1, source_target_pairs={{0,48},{8,56},{16,0},{24,8},{32,16},{40,24},{48,32},{56,40},{64,11... | collective-permute-start | bytes 36872 | tf_op jit(solution)/shard_map/ppermute | solution.py:28
  95.7 4.1 %collective-permute-start.22 = (f32[3,1024]{1,0:T(4,128)S(1)}, f32[3,1024]{1,0:T(4,128)S(1)}, u32[]{:S(2)}, u32[]{:S(2)}) collective-permute-start(f32[3,1024]{1,0:T(4,128)S(1)} %pad_maximum_fusion), channel_id=1, source_target_pairs={{0,32},{8,40},{16,48},{24,56},{32,0},{40,8},{48,16},{56,24},{64,96... | collective-permute-start | bytes 36872 | tf_op jit(solution)/shard_map/ppermute | solution.py:28
  99.9 4.7 %collective-permute-start.23 = (f32[1024]{0:T(1024)S(1)}, f32[1024]{0:T(1024)S(1)}, u32[]{:S(2)}, u32[]{:S(2)}) collective-permute-start(f32[1024]{0:T(1024)S(1)} %log_subtract_fusion), channel_id=1, source_target_pairs={{0,8},{8,0},{16,24},{24,16},{32,40},{40,32},{48,56},{56,48},{64,72... | collective-permute-start | bytes 12296 | tf_op jit(solution)/shard_map/ppermute | solution.py:28
  (1 other events, 0.6 us)

commit v3 on v2

--- a/solution.py
+++ b/solution.py
@@ -43,7 +43,7 @@
 
 
 def turn(value, step):
-    return lax.ppermute(value, "seq", [(i, (i + step) % NZ) for i in range(NZ)])
+    return lax.ppermute(value, ("dp", "seq"), _hop(lambda c: (2, step * along(c))))
 
 
 def pass_on(value, second, step):
@@ -64,7 +64,7 @@
 POOL_ROWS = 256
 
 
-def pool_kernel(starts, owner, gain, hidden, out, info, pick, token, buf, weights, sems):
+def pool_kernel(starts, hidden, out, info, token, buf, weights, sems):
     toks = hidden.shape[1]
     steps = toks // POOL_ROWS
     copies = [
@@ -86,11 +86,6 @@
     token[...] = jnp.zeros_like(token)
     info[:, 0:128] = jnp.broadcast_to(begin, (segs, 128)).astype(F32)
     info[:, 128:256] = jnp.broadcast_to(end - begin, (segs, 128)).astype(F32)
-    hold = (owner[...] == z).astype(jnp.int32)
-    hold_col = jnp.sum(jnp.where(lane == line, hold, 0), axis=1, keepdims=True)
-    rank = jnp.sum(jnp.where(line < lane, hold_col, 0), axis=0, keepdims=True)
-    slot = lax.broadcasted_iota(jnp.int32, (pick.shape[0], segs), 0)
-    pick[...] = jnp.where((rank == slot) & (hold == 1), 1.0, 0.0).astype(BF)
 
     before = jnp.sum((from_row <= first).astype(jnp.int32), axis=1, keepdims=True)
     for n in range(steps):
@@ -110,14 +105,14 @@
     for g in range(8):
         cols = slice(512 * g, 512 * g + 512)
         part = jnp.dot(weight, buf[:, cols], preferred_element_type=F32)
-        out[64 * g : 64 * g + 64, :] = ((part[0:64] + part[64:128]) * gain[:, cols]).astype(BF)
+        out[64 * g : 64 * g + 64, :] = (part[0:64] + part[64:128]).astype(BF)
         end_rows = buf[toks - 16 : toks, cols].astype(F32)
-        tail.append(jnp.sum(end_rows * end_weight, axis=0, keepdims=True) * gain[:, cols])
+        tail.append(jnp.sum(end_rows * end_weight, axis=0, keepdims=True))
     tail.append(jnp.zeros((8, 512), F32))
     out[512:528, :] = jnp.concatenate(tail, axis=0).astype(BF)
 
 
-def pool(starts, owner, gain, hidden):
+def pool(starts, hidden):
     _, toks, d = hidden.shape
     segs = starts.shape[1]
     vmem = pl.BlockSpec(memory_space=pltpu.VMEM)
@@ -126,26 +121,26 @@
         out_shape=(
             jax.ShapeDtypeStruct((PACKED, 512), BF),
             jax.ShapeDtypeStruct((segs, 256), F32),
-            jax.ShapeDtypeStruct((segs // NZ, segs), BF),
             jax.ShapeDtypeStruct((8, 128), F32),
         ),
-        in_specs=[vmem, vmem, vmem, pl.BlockSpec(memory_space=pltpu.HBM)],
-        out_specs=(vmem,) * 4,
+        in_specs=[vmem, pl.BlockSpec(memory_space=pltpu.HBM)],
+        out_specs=(vmem,) * 3,
         scratch_shapes=[
             pltpu.VMEM((toks, d), BF),
             pltpu.VMEM((128, toks), BF),
             pltpu.SemaphoreType.DMA((toks // POOL_ROWS,)),
         ],
-        compiler_params=pltpu.CompilerParams(vmem_limit_bytes=56 << 20),
+        compiler_params=pltpu.CompilerParams(vmem_limit_bytes=50 << 20),
         cost_estimate=pl.CostEstimate(
             flops=2 * 128 * toks * d, bytes_accessed=2 * toks * d, transcendentals=0
         ),
-    )(starts, owner, gain, hidden)
-
-
-def embed_kernel(info, _, *refs):
+    )(starts, hidden)
+
+
+def embed_kernel(info, _, gain, *refs):
     blocks, out, sums = refs[:9], refs[9], refs[10]
-    z = lax.axis_index("seq")
+    _, _, core, z = place()
+    way = along(core)
     starts = info[:, 0:1]
     counts = info[:, 128:129]
 
@@ -153,7 +148,7 @@
         far = jnp.zeros(k.shape, jnp.int32)
         for n, shift in enumerate(RING):
             far = jnp.where(k == n, shift, far)
-        dev = lax.rem(z + far + 8, 8) * 1024
+        dev = lax.rem(z + way * far + 8, 8) * 1024
         begun = (starts <= dev.astype(F32)).astype(F32)
         return (jnp.sum(begun, axis=0, keepdims=True) - 1.0).astype(jnp.int32)
 
@@ -178,7 +173,7 @@
         mean = (
             jnp.dot(pick, rows_of(64 * g, 64), preferred_element_type=F32)
             + jnp.dot(tpick, tail, preferred_element_type=F32)
-        ) / counts
+        ) * gain[:, 512 * g : 512 * g + 512] / counts
         sums[g] = mean
         square += jnp.sum(mean * mean, axis=1, keepdims=True)
     scale = lax.rsqrt(square + 1e-06)
@@ -186,19 +181,44 @@
         out[:, 512 * g : 512 * g + 512] = (sums[g] * scale).astype(BF)
 
 
-def embed(info, token, blocks):
+def embed(info, token, gain, blocks):
     vmem = pl.BlockSpec(memory_space=pltpu.VMEM)
     return pl.pallas_call(
         embed_kernel,
         out_shape=jax.ShapeDtypeStruct((256, 4096), BF),
-        in_specs=[vmem] * 11,
+        in_specs=[vmem] * 12,
         out_specs=vmem,
         scratch_shapes=[pltpu.VMEM((8, 256, 512), F32)],
         compiler_params=pltpu.CompilerParams(vmem_limit_bytes=24 << 20),
         cost_estimate=pl.CostEstimate(
             flops=2 * 256 * 640 * 4096, bytes_accessed=7 << 20, transcendentals=0
         ),
-    )(info, token, *blocks)
+    )(info, token, gain, *blocks)
+
+
+def owned_kernel(owner, passages, out):
+    hold = (owner[...] == lax.axis_index("seq")).astype(jnp.int32)
+    segs = owner.shape[1]
+    line = lax.broadcasted_iota(jnp.int32, (segs, segs), 0)
+    lane = lax.broadcasted_iota(jnp.int32, (segs, segs), 1)
+    rank = jnp.sum(jnp.where(line < lane, column(hold), 0), axis=0, keepdims=True)
+    slot = lax.broadcasted_iota(jnp.int32, (out.shape[0], segs), 0)
+    pick = jnp.where((rank == slot) & (hold == 1), 1.0, 0.0).astype(BF)
+    out[...] = jnp.dot(pick, passages[...], preferred_element_type=F32).astype(BF)
+
+
+def owned(owner, passages):
+    vmem = pl.BlockSpec(memory_space=pltpu.VMEM)
+    return pl.pallas_call(
+        owned_kernel,
+        out_shape=jax.ShapeDtypeStruct((passages.shape[0] // NZ, passages.shape[1]), BF),
+        in_specs=[vmem] * 2,
+        out_specs=vmem,
+        compiler_params=pltpu.CompilerParams(vmem_limit_bytes=16 << 20),
+        cost_estimate=pl.CostEstimate(
+            flops=2 * 32 * 256 * 4096, bytes_accessed=3 << 20, transcendentals=0
+        ),
+    )(owner, passages)
 
 
 NEAR = (0, -1, 1, 2)
@@ -252,7 +272,7 @@
         rows = slice(row, row + 256)
         all_q[rows, :] = q
         wq = q.astype(F32)
-        factor = scale[0] * lax.rsqrt(jnp.sum(wq * wq, axis=1, keepdims=True) + 1e-06)
+        factor = scale[...] * lax.rsqrt(jnp.sum(wq * wq, axis=1, keepdims=True) + 1e-06)
         scores = lax.dot_general(q, ordered[...], NT, preferred_element_type=F32) * factor
         hit = ids == picks_of(positive, row)
         chosen = jnp.sum(jnp.where(hit, scores, 0.0), axis=1, keepdims=True)
@@ -284,7 +304,6 @@
 
 def score(scale, positive, mine, other, blocks):
     vmem = pl.BlockSpec(memory_space=pltpu.VMEM)
-    smem = pl.BlockSpec(memory_space=pltpu.SMEM)
     params = pltpu.CompilerParams(vmem_limit_bytes=24 << 20)
     cost = pl.CostEstimate(
         flops=2 * 1024 * 256 * 4096, bytes_accessed=1 << 20, transcendentals=1024 * 256
@@ -295,12 +314,12 @@
             jax.ShapeDtypeStruct((1024, 4096), BF),
             jax.ShapeDtypeStruct((1024, 128), F32),
         ),
-        in_specs=[smem] + [vmem] * 7,
+        in_specs=[vmem] * 8,
         out_specs=(vmem, vmem),
         scratch_shapes=[pltpu.VMEM((256, 4096), BF)],
         compiler_params=params,
         cost_estimate=cost,
-    )(scale, positive, mine, *blocks)
+    )(scale.reshape(1, 1), positive, mine, *blocks)
     return pl.pallas_call(
         other_kernel,
         out_shape=jax.ShapeDtypeStruct((8, 1024), F32),
@@ -371,35 +390,35 @@
     block = jnp.where(
         core == 0, jnp.concatenate([own, back], 1), jnp.concatenate([back, own], 1)
     )
-    packed, info, pick, token = pool(seg_start, owner, gain[None, :], hidden)
+    packed, info, token = pool(seg_start, hidden)
 
     got = {("q", 0): block, ("f", 0): packed, ("b", 0): packed}
     last = []
     token = [token]
 
-    def take(names):
+    def take(names, hold=False):
         keys = [*names, *(k for k in last if k not in names)]
         *tied, mark = barrier((*(got[k] for k in keys), token[0]))
         got.update(zip(keys, tied))
-        token[0] = fence(mark)
+        token[0] = fence(mark) if hold else mark
         last[:] = names
 
     def step(*names):
-        take([(stream, n - 1) for stream, n in names])
+        take([(stream, n - 1) for stream, n in names], hold=True)
         for stream, n in names:
             got[stream, n] = turn(got[stream, n - 1], 1 if stream == "f" else -1)
 
-    got["f", 1], got["b", 1] = turn(packed, 1), turn(packed, -1)
-    take([("q", 0)])
+    take([("q", 0)], hold=True)
     got["+", 1], got["-", 1] = pass_on(got["q", 0], 0, 1), pass_on(got["q", 0], 0, -1)
     got["far", 1] = pass_on(got["q", 0], 0, 2)
-    step(("f", 2), ("b", 2))
-    take([("+", 1), ("-", 1), ("far", 1)])
+    step(("f", 1), ("b", 1))
+    take([("+", 1), ("-", 1), ("far", 1)], hold=True)
     cuts = [(n, 0, half, 0, half * n) for n in range(4)]
     (line,) = copied((4 * half,), cuts, block, got["+", 1], got["-", 1], got["far", 1])
     got["+", 3], got["-", 3] = pass_on(line, 1, 1), pass_on(line, 1, -1)
+    step(("f", 2), ("b", 2))
     step(("f", 3), ("b", 3))
-    take([("+", 3), ("-", 3)])
+    take([("+", 3), ("-", 3)], hold=True)
     cuts = [(0, 0, 2 * half, 0, 0), (1, 2 * half, 2 * half, 1, 0)]
     up, down = copied((2 * half, 2 * half), cuts, got["+", 3], got["-", 3])
     got["+", 4], got["-", 4] = pass_on(up, 1, 1), pass_on(down, 1, -1)
@@ -409,17 +428,18 @@
     got["f", 4], got["b", 4] = turn(up, 1), turn(down, -1)
 
     order = [packed, *(got[k, n] for n in (1, 2, 3, 4) for k in "fb")]
-    mine = embed(info, token[0], order)
+    mine = embed(info, token[0], gain[None, :], order)
     late = [("+", 4), ("-", 4)]
     mine, *rest = barrier((mine, *(got[k] for k in late)))
     got.update(zip(late, rest))
     other = move(mine, dc=1)
     blocks = [line, *(got[k] for k in (("+", 3), ("-", 3), ("+", 4), ("-", 4)))]
     stats = score(logit_scale, positive.reshape(16, 128), mine, other, blocks)
-    pooled = jnp.dot(pick, mine, preferred_element_type=F32).astype(BF)
+    pooled = owned(owner, mine)
 
     stats = stats[:3]
     stats = merge([stats, move(stats, dx=1), move(stats, dx=-1), move(stats, dx=2)])
+    stats, pooled = barrier((stats, pooled))
     stats = merge([stats, move(stats, dy=1), move(stats, dy=-1), move(stats, dy=2)])
     part = stats[2] - stats[0] - jnp.log(stats[1])
     rest = move(part, dc=1)

time: 105 us -> 103 us (0.981)
  waiting for transfers between devices: 41.8 us -> 46 us
  starting transfers between devices: 39.8 us -> 36.7 us
  local copies, waits for them, and re-layouts: 3.68 us -> 1.77 us
  matrix products: 1.17 us -> 0 us
    ppermute x8, waiting for transfers between devices: 22.2 us -> 30.9 us  [turn(): lax.ppermute(value, ('dp', 'seq'), _hop(lambda c: (2, step * along(c))))]
    ppermute x7, waiting for transfers between devices: 14.1 us -> 9.9 us  [pass_on(): lax.ppermute(value, ('dp', 'seq'), _hop(lambda c: ((c + second) % 2, step)))]
    unnamed x18 -> x8, local copies, waits for them, and re-layouts: 2.58 us -> 0.69 us
    ppermute x9, starting transfers between devices: 18.9 us -> 17.1 us  [move(): return lax.ppermute(value, 'dp', pairs)]
    ppermute x7, starting transfers between devices: 10.1 us -> 8.35 us  [pass_on(): lax.ppermute(value, ('dp', 'seq'), _hop(lambda c: ((c + second) % 2, step)))]
    pallas_call x1, Pallas kernels: 6.85 us -> 5.35 us  [pool(): pl.pallas_call(pool_kernel, out_shape=(jax.ShapeDtypeStruct((PACKED, 512)...]
    pallas_call x0 -> x1, Pallas kernels: none -> 1.31 us  [owned(): pl.pallas_call(owned_kernel, out_shape=jax.ShapeDtypeStruct((passages.sha...]
    dot_general x1 -> x0, matrix products: 1.17 us -> none  [per_device(): pooled = jnp.dot(pick, mine, preferred_element_type=F32).astype(BF)]
  transfers between devices with their start and end apart: 24 -> 24, of which waited for: 7 -> 15; matrix products, arithmetic and copies ran while one was open for 1% -> 0% of each run, Pallas kernels for 12% -> 13%
where the time goes in v3:
time: 103 us
  waiting for transfers between devices  46 us (45%)
  starting transfers between devices  36.7 us (36%)
  Pallas kernels  16.4 us (16%)
  local copies, waits for them, and re-layouts  1.77 us (2%)
  between operations  1.47 us (1%)
    ppermute x8, waiting for transfers between devices, turn(): lax.ppermute(value, ('dp', 'seq'), _hop(lambda c: (2, step * along(c))))  30.9 us
    ppermute x9, starting transfers between devices, move(): return lax.ppermute(value, 'dp', pairs)  17.1 us
    ppermute x8, starting transfers between devices, turn(): lax.ppermute(value, ('dp', 'seq'), _hop(lambda c: (2, step * along(c))))  11.2 us
    ppermute x7, waiting for transfers between devices, pass_on(): lax.ppermute(value, ('dp', 'seq'), _hop(lambda c: ((c + second) % 2, step)))  9.9 us
    ppermute x7, starting transfers between devices, pass_on(): lax.ppermute(value, ('dp', 'seq'), _hop(lambda c: ((c + second) % 2, step)))  8.35 us
    pallas_call x1, Pallas kernels, pool(): pl.pallas_call(pool_kernel, out_shape=(jax.ShapeDtypeStruct((PACKED, 512)...  5.35 us
    ppermute x9, waiting for transfers between devices, move(): return lax.ppermute(value, 'dp', pairs)  5.21 us
    pallas_call x1, Pallas kernels, score(): pl.pallas_call(own_kernel, out_shape=(jax.ShapeDtypeStruct((1024, 4096),...  3.68 us
  transfers between devices with their start and end apart: 24, of which 15 were waited for; matrix products, arithmetic and copies ran while one was open for 0% of the time, Pallas kernels for 13%

profile of v3, /device:TPU:1, one launch (start us, length us, event | category | flops | bytes accessed | tf_op | source)
XLA Modules:
  0.0 103.1 jit_solution(15836849236515304992)
XLA Ops:
  0.7 1.1 %constant_dynamic-slice_fusion.1 = (bf16[1024,128]{1,0:T(8,128)(2,1)S(1)}, bf16[1024,128]{1,0:T(8,128)(2,1)S(1)}) fusion(bf16[2048,128]{1,0:T(8,128)(2,1)} %param.11, s32[]{:T(128)S(6)} %select_n.31, s32[]{:T(128)S(6)} %select_n.32), kind=kLoop, calls=%fused_computation.19 | loop fusion | bytes 1048584 | tf_op jit(solution)/shard_map/dynamic_slice | solution.py:387
  1.7 3.3 %collective-permute-start = (bf16[1024,128]{1,0:T(8,128)(2,1)S(1)}, bf16[1024,128]{1,0:T(8,128)(2,1)S(1)}, u32[]{:S(2)}, u32[]{:S(2)}) collective-permute-start(bf16[1024,128]{1,0:T(8,128)(2,1)S(1)} %get-tuple-element.87), channel_id=1, source_target_pairs={{0,8},{8,0},{16,24},{24,16},{32,40},{40,32},{48,56},{56,48},{64,72... | collective-permute-start | bytes 786440 | tf_op jit(solution)/shard_map/ppermute | solution.py:28
  5.7 5.3 %shard_map.86 = (bf16[528,512]{1,0:T(8,128)(2,1)S(1)}, f32[256,256]{1,0:T(8,128)S(1)}, f32[8,128]{1,0:T(8,128)S(1)}) custom-call(s32[1,256]{1,0:T(1,128)S(1)} %copy-done.2, bf16[1,1024,4096]{2,1,0:T(8,128)(2,1)} %hidden.1), custom_call_target="tpu_custom_call" | custom-call | flops 1073741824 | bytes 8388608 | tf_op jit(solution)/shard_map/pallas_call | solution.py:119
  11.4 2.7 %collective-permute-start.4 = (bf16[1024,256]{1,0:T(8,128)(2,1)S(1)}, bf16[1024,256]{1,0:T(8,128)(2,1)S(1)}, u32[]{:S(2)}, u32[]{:S(2)}) collective-permute-start(bf16[1024,256]{1,0:T(8,128)(2,1)S(1)} %maximum_select_fusion.refs_0_), channel_id=1, source_target_pairs={{0,192},{1,193},{2,194},{3,195},{4,196},{5,197},{6,198},{7,199},{8... | collective-permute-start | bytes 1572872 | tf_op jit(solution)/shard_map/ppermute | solution.py:50
  14.1 5.5 %collective-permute-start.1 = (bf16[528,512]{1,0:T(8,128)(2,1)S(1)}, bf16[528,512]{1,0:T(8,128)(2,1)S(1)}, u32[]{:S(2)}, u32[]{:S(2)}) collective-permute-start(bf16[528,512]{1,0:T(8,128)(2,1)S(1)} %get-tuple-element.49.refs_0_), channel_id=1, source_target_pairs={{0,1},{1,2},{2,3},{3,4},{4,5},{5,6},{6,7},{7,0},{8,15},{9,8},{10,9... | collective-permute-start | bytes 1622024 | tf_op jit(solution)/shard_map/ppermute | solution.py:46
  19.6 6.9 %collective-permute-done.3.refs_1_ = bf16[1024,256]{1,0:T(8,128)(2,1)S(1)} collective-permute-done((bf16[1024,256]{1,0:T(8,128)(2,1)S(1)}, bf16[1024,256]{1,0:T(8,128)(2,1)S(1)}, u32[]{:S(2)}, u32[]{:S(2)}) %collective-permute-start.3) | collective-permute-done | bytes 524320 | tf_op jit(solution)/shard_map/ppermute | solution.py:50
  27.2 2.3 %collective-permute-start.11 = (bf16[4096,256]{1,0:T(8,128)(2,1)S(1)}, bf16[4096,256]{1,0:T(8,128)(2,1)S(1)}, u32[]{:S(2)}, u32[]{:S(2)}) collective-permute-start(bf16[4096,256]{1,0:T(8,128)(2,1)S(1)} %shard_map.91.refs_0_), channel_id=1, source_target_pairs={{0,48},{1,49},{2,50},{3,51},{4,52},{5,53},{6,54},{7,55},{8,200},{9... | collective-permute-start | bytes 6291464 | tf_op jit(solution)/shard_map/ppermute | solution.py:50
  29.5 1.0 %collective-permute-done.1.refs_1_ = bf16[528,512]{1,0:T(8,128)(2,1)S(1)} collective-permute-done((bf16[528,512]{1,0:T(8,128)(2,1)S(1)}, bf16[528,512]{1,0:T(8,128)(2,1)S(1)}, u32[]{:S(2)}, u32[]{:S(2)}) %collective-permute-start.1) | collective-permute-done | bytes 540704 | tf_op jit(solution)/shard_map/ppermute | solution.py:46
  30.5 2.8 %collective-permute-done.2.refs_2_ = bf16[528,512]{1,0:T(8,128)(2,1)S(1)} collective-permute-done((bf16[528,512]{1,0:T(8,128)(2,1)S(1)}, bf16[528,512]{1,0:T(8,128)(2,1)S(1)}, u32[]{:S(2)}, u32[]{:S(2)}) %collective-permute-start.2) | collective-permute-done | bytes 540704 | tf_op jit(solution)/shard_map/ppermute | solution.py:46
  33.3 1.3 %collective-permute-start.6 = (bf16[528,512]{1,0:T(8,128)(2,1)S(1)}, bf16[528,512]{1,0:T(8,128)(2,1)S(1)}, u32[]{:S(2)}, u32[]{:S(2)}) collective-permute-start(bf16[528,512]{1,0:T(8,128)(2,1)S(1)} %collective-permute-done.1.refs_1_), channel_id=1, source_target_pairs={{0,1},{1,2},{2,3},{3,4},{4,5},{5,6},{6,7},{7,0},{8,15},{9,8},{10,9... | collective-permute-start | bytes 1622024 | tf_op jit(solution)/shard_map/ppermute | solution.py:46
  34.8 12.1 %collective-permute-done.6.refs_3_ = bf16[528,512]{1,0:T(8,128)(2,1)S(1)} collective-permute-done((bf16[528,512]{1,0:T(8,128)(2,1)S(1)}, bf16[528,512]{1,0:T(8,128)(2,1)S(1)}, u32[]{:S(2)}, u32[]{:S(2)}) %collective-permute-start.6) | collective-permute-done | bytes 540704 | tf_op jit(solution)/shard_map/ppermute | solution.py:46
  46.8 1.9 %collective-permute-done.7.refs_4_ = bf16[528,512]{1,0:T(8,128)(2,1)S(1)} collective-permute-done((bf16[528,512]{1,0:T(8,128)(2,1)S(1)}, bf16[528,512]{1,0:T(8,128)(2,1)S(1)}, u32[]{:S(2)}, u32[]{:S(2)}) %collective-permute-start.7) | collective-permute-done | bytes 540704 | tf_op jit(solution)/shard_map/ppermute | solution.py:46
  48.8 1.5 %collective-permute-start.9 = (bf16[528,512]{1,0:T(8,128)(2,1)S(1)}, bf16[528,512]{1,0:T(8,128)(2,1)S(1)}, u32[]{:S(2)}, u32[]{:S(2)}) collective-permute-start(bf16[528,512]{1,0:T(8,128)(2,1)S(1)} %collective-permute-done.7.refs_4_), channel_id=1, source_target_pairs={{0,7},{1,0},{2,1},{3,2},{4,3},{5,4},{6,5},{7,6},{8,9},{9,10},{10,1... | collective-permute-start | bytes 1622024 | tf_op jit(solution)/shard_map/ppermute | solution.py:46
  50.2 3.0 %collective-permute-done.10.refs_0_.refs_1_ = bf16[4096,256]{1,0:T(8,128)(2,1)S(1)} collective-permute-done((bf16[4096,256]{1,0:T(8,128)(2,1)S(1)}, bf16[4096,256]{1,0:T(8,128)(2,1)S(1)}, u32[]{:S(2)}, u32[]{:S(2)}) %collective-permute-start.10) | collective-permute-done | bytes 2097184 | tf_op jit(solution)/shard_map/ppermute | solution.py:50
  53.9 2.4 %collective-permute-start.15 = (bf16[2048,256]{1,0:T(8,128)(2,1)S(1)}, bf16[2048,256]{1,0:T(8,128)(2,1)S(1)}, u32[]{:S(2)}, u32[]{:S(2)}) collective-permute-start(bf16[2048,256]{1,0:T(8,128)(2,1)S(1)} %get-tuple-element.74), channel_id=1, source_target_pairs={{0,48},{1,49},{2,50},{3,51},{4,52},{5,53},{6,54},{7,55},{8,200},{9... | collective-permute-start | bytes 3145736 | tf_op jit(solution)/shard_map/ppermute | solution.py:50
  56.2 6.3 %collective-permute-done.8.refs_0_.refs_5_ = bf16[528,512]{1,0:T(8,128)(2,1)S(1)} collective-permute-done((bf16[528,512]{1,0:T(8,128)(2,1)S(1)}, bf16[528,512]{1,0:T(8,128)(2,1)S(1)}, u32[]{:S(2)}, u32[]{:S(2)}) %collective-permute-start.8) | collective-permute-done | bytes 540704 | tf_op jit(solution)/shard_map/ppermute | solution.py:46
  62.6 1.2 %collective-permute-done.9.refs_1_.refs_6_ = bf16[528,512]{1,0:T(8,128)(2,1)S(1)} collective-permute-done((bf16[528,512]{1,0:T(8,128)(2,1)S(1)}, bf16[528,512]{1,0:T(8,128)(2,1)S(1)}, u32[]{:S(2)}, u32[]{:S(2)}) %collective-permute-start.9) | collective-permute-done | bytes 540704 | tf_op jit(solution)/shard_map/ppermute | solution.py:46
  63.9 2.7 %collective-permute-start.12 = (bf16[256,512]{1,0:T(8,128)(2,1)S(1)}, bf16[256,512]{1,0:T(8,128)(2,1)S(1)}, u32[]{:S(2)}, u32[]{:S(2)}) collective-permute-start(bf16[256,512]{1,0:T(8,128)(2,1)S(1)} %get-tuple-element.71), channel_id=1, source_target_pairs={{0,1},{1,2},{2,3},{3,4},{4,5},{5,6},{6,7},{7,0},{8,15},{9,8},{10,9... | collective-permute-start | bytes 786440 | tf_op jit(solution)/shard_map/ppermute | solution.py:46
  66.6 5.4 %collective-permute-done.12.refs_7_ = bf16[256,512]{1,0:T(8,128)(2,1)S(1)} collective-permute-done((bf16[256,512]{1,0:T(8,128)(2,1)S(1)}, bf16[256,512]{1,0:T(8,128)(2,1)S(1)}, u32[]{:S(2)}, u32[]{:S(2)}) %collective-permute-start.12) | collective-permute-done | bytes 262176 | tf_op jit(solution)/shard_map/ppermute | solution.py:46
  72.1 2.3 %shard_map.95.passages = bf16[256,4096]{1,0:T(8,128)(2,1)S(1)} custom-call(f32[256,256]{1,0:T(8,128)S(1)} %get-tuple-element.43.info, f32[8,128]{1,0:T(8,128)S(1)} %shard_map.93._, f32[1,4096]{1,0:T(1,128)S(1)} %bitcast.15, bf16[528,512]{1,0:T(8,128)(2,1)S(1)} %get-tuple-element.49.refs_0_, bf16[528,512]{1,0:T(8,128)(2,1)S(1)} %collective-permute-done.1.refs_1_, ...), custom_call_target="tpu_custom_call" | custom-call | flops 1342177280 | bytes 7340032 | tf_op jit(solution)/shard_map/pallas_call | solution.py:186
  74.5 2.0 %collective-permute-start.16 = (bf16[256,4096]{1,0:T(8,128)(2,1)S(1)}, bf16[256,4096]{1,0:T(8,128)(2,1)S(1)}, u32[]{:S(2)}, u32[]{:S(2)}) collective-permute-start(bf16[256,4096]{1,0:T(8,128)(2,1)S(1)} %shard_map.95.passages), channel_id=1, source_target_pairs={{0,8},{8,0},{16,24},{24,16},{32,40},{40,32},{48,56},{56,48},{64,72... | collective-permute-start | bytes 6291464 | tf_op jit(solution)/shard_map/ppermute | solution.py:28
  77.1 3.7 %shard_map.97 = (bf16[1024,4096]{1,0:T(8,128)(2,1)S(1)}, f32[1024,128]{1,0:T(8,128)S(1)}) custom-call(f32[1,1]{1,0:T(1,128)} %bitcast.12.scale, s32[16,128]{1,0:T(8,128)S(1)} %bitcast.13, bf16[256,4096]{1,0:T(8,128)(2,1)S(1)} %shard_map.95.passages, bf16[4096,256]{1,0:T(8,128)(2,1)S(1)} %shard_map.91.refs_0_, ...), custom_call_target="tpu_custom_call" | custom-call | flops 2147483648 | bytes 1048576 | tf_op jit(solution)/shard_map/pallas_call | solution.py:311
  80.8 3.3 %shard_map.98 = f32[8,1024]{1,0:T(8,128)S(1)} custom-call(s32[16,128]{1,0:T(8,128)S(1)} %bitcast.14, bf16[256,4096]{1,0:T(8,128)(2,1)S(1)} %collective-permute-done.16.passages, bf16[1024,4096]{1,0:T(8,128)(2,1)S(1)} %get-tuple-element.80.all_q, f32[1024,128]{1,0:T(8,128)S(1)} %get-tuple-element.81.early), custom_call_target="tpu_custom_call" | custom-call | flops 2147483648 | bytes 1048576 | tf_op jit(solution)/shard_map/pallas_call | solution.py:323
  84.1 1.5 %collective-permute-start.17 = (f32[3,1024]{1,0:T(4,128)S(1)}, f32[3,1024]{1,0:T(4,128)S(1)}, u32[]{:S(2)}, u32[]{:S(2)}) collective-permute-start(f32[3,1024]{1,0:T(4,128)S(1)} %slice.112), channel_id=1, source_target_pairs={{0,64},{8,72},{16,80},{24,88},{32,96},{40,104},{48,112},{56,120},{... | collective-permute-start | bytes 36872 | tf_op jit(solution)/shard_map/ppermute | solution.py:28
  85.7 1.4 %collective-permute-start.18 = (f32[3,1024]{1,0:T(4,128)S(1)}, f32[3,1024]{1,0:T(4,128)S(1)}, u32[]{:S(2)}, u32[]{:S(2)}) collective-permute-start(f32[3,1024]{1,0:T(4,128)S(1)} %slice.112), channel_id=1, source_target_pairs={{0,192},{8,200},{16,208},{24,216},{32,224},{40,232},{48,240},{56,2... | collective-permute-start | bytes 36872 | tf_op jit(solution)/shard_map/ppermute | solution.py:28
  87.1 1.6 %collective-permute-start.19 = (f32[3,1024]{1,0:T(4,128)S(1)}, f32[3,1024]{1,0:T(4,128)S(1)}, u32[]{:S(2)}, u32[]{:S(2)}) collective-permute-start(f32[3,1024]{1,0:T(4,128)S(1)} %slice.112), channel_id=1, source_target_pairs={{0,128},{8,136},{16,144},{24,152},{32,160},{40,168},{48,176},{56,1... | collective-permute-start | bytes 36872 | tf_op jit(solution)/shard_map/ppermute | solution.py:28
  88.7 1.3 %shard_map.99 = bf16[32,4096]{1,0:T(8,128)(2,1)} custom-call(s32[1,256]{1,0:T(1,128)S(1)} %copy-done.3, bf16[256,4096]{1,0:T(8,128)(2,1)S(1)} %shard_map.95.passages), custom_call_target="tpu_custom_call" | custom-call | flops 67108864 | bytes 3145728 | tf_op jit(solution)/shard_map/pallas_call | solution.py:212
  90.1 1.1 %collective-permute-done.19 = f32[3,1024]{1,0:T(4,128)S(1)} collective-permute-done((f32[3,1024]{1,0:T(4,128)S(1)}, f32[3,1024]{1,0:T(4,128)S(1)}, u32[]{:S(2)}, u32[]{:S(2)}) %collective-permute-start.19) | collective-permute-done | bytes 12320 | tf_op jit(solution)/shard_map/ppermute | solution.py:28
  91.3 1.7 %collective-permute-start.20 = (f32[3,1024]{1,0:T(4,128)S(1)}, f32[3,1024]{1,0:T(4,128)S(1)}, u32[]{:S(2)}, u32[]{:S(2)}) collective-permute-start(f32[3,1024]{1,0:T(4,128)S(1)} %pad_maximum_fusion), channel_id=1, source_target_pairs={{0,16},{8,24},{16,32},{24,40},{32,48},{40,56},{48,0},{56,8},{64,80... | collective-permute-start | bytes 36872 | tf_op jit(solution)/shard_map/ppermute | solution.py:28
  93.0 1.0 collective-permute-start.21
  95.6 2.5 %collective-permute-done.22 = f32[3,1024]{1,0:T(4,128)S(1)} collective-permute-done((f32[3,1024]{1,0:T(4,128)S(1)}, f32[3,1024]{1,0:T(4,128)S(1)}, u32[]{:S(2)}, u32[]{:S(2)}) %collective-permute-start.22) | collective-permute-done | bytes 12320 | tf_op jit(solution)/shard_map/ppermute | solution.py:28
  98.2 3.5 %collective-permute-start.23 = (f32[1024]{0:T(1024)S(1)}, f32[1024]{0:T(1024)S(1)}, u32[]{:S(2)}, u32[]{:S(2)}) collective-permute-start(f32[1024]{0:T(1024)S(1)} %log_subtract_fusion), channel_id=1, source_target_pairs={{0,8},{8,0},{16,24},{24,16},{32,40},{40,32},{48,56},{56,48},{64,72... | collective-permute-start | bytes 12296 | tf_op jit(solution)/shard_map/ppermute | solution.py:28
  (46 shorter events, 5.9 us)
Async XLA Ops:
  1.7 9.4 %collective-permute-start = (bf16[1024,128]{1,0:T(8,128)(2,1)S(1)}, bf16[1024,128]{1,0:T(8,128)(2,1)S(1)}, u32[]{:S(2)}, u32[]{:S(2)}) collective-permute-start(bf16[1024,128]{1,0:T(8,128)(2,1)S(1)} %get-tuple-element.87), channel_id=1, source_target_pairs={{0,8},{8,0},{16,24},{24,16},{32,40},{40,32},{48,56},{56,48},{64,72... | collective-permute-start | bytes 786440 | tf_op jit(solution)/shard_map/ppermute | solution.py:28
  5.1 0.7 copy-start.2
  11.3 15.2 %collective-permute-start.3 = (bf16[1024,256]{1,0:T(8,128)(2,1)S(1)}, bf16[1024,256]{1,0:T(8,128)(2,1)S(1)}, u32[]{:S(2)}, u32[]{:S(2)}) collective-permute-start(bf16[1024,256]{1,0:T(8,128)(2,1)S(1)} %maximum_select_fusion.refs_0_), channel_id=1, source_target_pairs={{0,64},{1,65},{2,66},{3,67},{4,68},{5,69},{6,70},{7,71},{8,24},{9,... | collective-permute-start | bytes 1572872 | tf_op jit(solution)/shard_map/ppermute | solution.py:50
  11.4 15.1 %collective-permute-start.4 = (bf16[1024,256]{1,0:T(8,128)(2,1)S(1)}, bf16[1024,256]{1,0:T(8,128)(2,1)S(1)}, u32[]{:S(2)}, u32[]{:S(2)}) collective-permute-start(bf16[1024,256]{1,0:T(8,128)(2,1)S(1)} %maximum_select_fusion.refs_0_), channel_id=1, source_target_pairs={{0,192},{1,193},{2,194},{3,195},{4,196},{5,197},{6,198},{7,199},{8... | collective-permute-start | bytes 1572872 | tf_op jit(solution)/shard_map/ppermute | solution.py:50
  14.0 12.5 %collective-permute-start.5 = (bf16[1024,256]{1,0:T(8,128)(2,1)S(1)}, bf16[1024,256]{1,0:T(8,128)(2,1)S(1)}, u32[]{:S(2)}, u32[]{:S(2)}) collective-permute-start(bf16[1024,256]{1,0:T(8,128)(2,1)S(1)} %maximum_select_fusion.refs_0_), channel_id=1, source_target_pairs={{0,128},{1,129},{2,130},{3,131},{4,132},{5,133},{6,134},{7,135},{8... | collective-permute-start | bytes 1572872 | tf_op jit(solution)/shard_map/ppermute | solution.py:50
  14.1 16.5 %collective-permute-start.1 = (bf16[528,512]{1,0:T(8,128)(2,1)S(1)}, bf16[528,512]{1,0:T(8,128)(2,1)S(1)}, u32[]{:S(2)}, u32[]{:S(2)}) collective-permute-start(bf16[528,512]{1,0:T(8,128)(2,1)S(1)} %get-tuple-element.49.refs_0_), channel_id=1, source_target_pairs={{0,1},{1,2},{2,3},{3,4},{4,5},{5,6},{6,7},{7,0},{8,15},{9,8},{10,9... | collective-permute-start | bytes 1622024 | tf_op jit(solution)/shard_map/ppermute | solution.py:46
  19.6 13.7 %collective-permute-start.2 = (bf16[528,512]{1,0:T(8,128)(2,1)S(1)}, bf16[528,512]{1,0:T(8,128)(2,1)S(1)}, u32[]{:S(2)}, u32[]{:S(2)}) collective-permute-start(bf16[528,512]{1,0:T(8,128)(2,1)S(1)} %get-tuple-element.49.refs_0_), channel_id=1, source_target_pairs={{0,7},{1,0},{2,1},{3,2},{4,3},{5,4},{6,5},{7,6},{8,9},{9,10},{10,1... | collective-permute-start | bytes 1622024 | tf_op jit(solution)/shard_map/ppermute | solution.py:46
  26.7 26.5 %collective-permute-start.10 = (bf16[4096,256]{1,0:T(8,128)(2,1)S(1)}, bf16[4096,256]{1,0:T(8,128)(2,1)S(1)}, u32[]{:S(2)}, u32[]{:S(2)}) collective-permute-start(bf16[4096,256]{1,0:T(8,128)(2,1)S(1)} %shard_map.91.refs_0_), channel_id=1, source_target_pairs={{0,16},{1,17},{2,18},{3,19},{4,20},{5,21},{6,22},{7,23},{8,72},{9,... | collective-permute-start | bytes 6291464 | tf_op jit(solution)/shard_map/ppermute | solution.py:50
  27.2 26.0 %collective-permute-start.11 = (bf16[4096,256]{1,0:T(8,128)(2,1)S(1)}, bf16[4096,256]{1,0:T(8,128)(2,1)S(1)}, u32[]{:S(2)}, u32[]{:S(2)}) collective-permute-start(bf16[4096,256]{1,0:T(8,128)(2,1)S(1)} %shard_map.91.refs_0_), channel_id=1, source_target_pairs={{0,48},{1,49},{2,50},{3,51},{4,52},{5,53},{6,54},{7,55},{8,200},{9... | collective-permute-start | bytes 6291464 | tf_op jit(solution)/shard_map/ppermute | solution.py:50
  33.3 13.5 %collective-permute-start.6 = (bf16[528,512]{1,0:T(8,128)(2,1)S(1)}, bf16[528,512]{1,0:T(8,128)(2,1)S(1)}, u32[]{:S(2)}, u32[]{:S(2)}) collective-permute-start(bf16[528,512]{1,0:T(8,128)(2,1)S(1)} %collective-permute-done.1.refs_1_), channel_id=1, source_target_pairs={{0,1},{1,2},{2,3},{3,4},{4,5},{5,6},{6,7},{7,0},{8,15},{9,8},{10,9... | collective-permute-start | bytes 1622024 | tf_op jit(solution)/shard_map/ppermute | solution.py:46
  34.6 14.2 %collective-permute-start.7 = (bf16[528,512]{1,0:T(8,128)(2,1)S(1)}, bf16[528,512]{1,0:T(8,128)(2,1)S(1)}, u32[]{:S(2)}, u32[]{:S(2)}) collective-permute-start(bf16[528,512]{1,0:T(8,128)(2,1)S(1)} %collective-permute-done.2.refs_2_), channel_id=1, source_target_pairs={{0,7},{1,0},{2,1},{3,2},{4,3},{5,4},{6,5},{7,6},{8,9},{9,10},{10,1... | collective-permute-start | bytes 1622024 | tf_op jit(solution)/shard_map/ppermute | solution.py:46
  48.8 13.8 %collective-permute-start.8 = (bf16[528,512]{1,0:T(8,128)(2,1)S(1)}, bf16[528,512]{1,0:T(8,128)(2,1)S(1)}, u32[]{:S(2)}, u32[]{:S(2)}) collective-permute-start(bf16[528,512]{1,0:T(8,128)(2,1)S(1)} %collective-permute-done.6.refs_3_), channel_id=1, source_target_pairs={{0,1},{1,2},{2,3},{3,4},{4,5},{5,6},{6,7},{7,0},{8,15},{9,8},{10,9... | collective-permute-start | bytes 1622024 | tf_op jit(solution)/shard_map/ppermute | solution.py:46
  48.8 15.0 %collective-permute-start.9 = (bf16[528,512]{1,0:T(8,128)(2,1)S(1)}, bf16[528,512]{1,0:T(8,128)(2,1)S(1)}, u32[]{:S(2)}, u32[]{:S(2)}) collective-permute-start(bf16[528,512]{1,0:T(8,128)(2,1)S(1)} %collective-permute-done.7.refs_4_), channel_id=1, source_target_pairs={{0,7},{1,0},{2,1},{3,2},{4,3},{5,4},{6,5},{7,6},{8,9},{9,10},{10,1... | collective-permute-start | bytes 1622024 | tf_op jit(solution)/shard_map/ppermute | solution.py:46
  53.4 21.1 %collective-permute-start.14 = (bf16[2048,256]{1,0:T(8,128)(2,1)S(1)}, bf16[2048,256]{1,0:T(8,128)(2,1)S(1)}, u32[]{:S(2)}, u32[]{:S(2)}) collective-permute-start(bf16[2048,256]{1,0:T(8,128)(2,1)S(1)} %get-tuple-element.73), channel_id=1, source_target_pairs={{0,16},{1,17},{2,18},{3,19},{4,20},{5,21},{6,22},{7,23},{8,72},{9,... | collective-permute-start | bytes 3145736 | tf_op jit(solution)/shard_map/ppermute | solution.py:50
  53.9 18.2 %copy-start.1 = (f32[4096]{0:T(1024)S(1)}, f32[4096]{0:T(1024)}, u32[]{:S(2)}) copy-start(f32[4096]{0:T(1024)} %param.8) | copy-start | bytes 49156
  53.9 20.6 %collective-permute-start.15 = (bf16[2048,256]{1,0:T(8,128)(2,1)S(1)}, bf16[2048,256]{1,0:T(8,128)(2,1)S(1)}, u32[]{:S(2)}, u32[]{:S(2)}) collective-permute-start(bf16[2048,256]{1,0:T(8,128)(2,1)S(1)} %get-tuple-element.74), channel_id=1, source_target_pairs={{0,48},{1,49},{2,50},{3,51},{4,52},{5,53},{6,54},{7,55},{8,200},{9... | collective-permute-start | bytes 3145736 | tf_op jit(solution)/shard_map/ppermute | solution.py:50
  63.8 8.3 %collective-permute-start.13 = (bf16[272,512]{1,0:T(8,128)(2,1)S(1)}, bf16[272,512]{1,0:T(8,128)(2,1)S(1)}, u32[]{:S(2)}, u32[]{:S(2)}) collective-permute-start(bf16[272,512]{1,0:T(8,128)(2,1)S(1)} %get-tuple-element.72), channel_id=1, source_target_pairs={{0,7},{1,0},{2,1},{3,2},{4,3},{5,4},{6,5},{7,6},{8,9},{9,10},{10,1... | collective-permute-start | bytes 835592 | tf_op jit(solution)/shard_map/ppermute | solution.py:46
  63.9 8.1 %collective-permute-start.12 = (bf16[256,512]{1,0:T(8,128)(2,1)S(1)}, bf16[256,512]{1,0:T(8,128)(2,1)S(1)}, u32[]{:S(2)}, u32[]{:S(2)}) collective-permute-start(bf16[256,512]{1,0:T(8,128)(2,1)S(1)} %get-tuple-element.71), channel_id=1, source_target_pairs={{0,1},{1,2},{2,3},{3,4},{4,5},{5,6},{6,7},{7,0},{8,15},{9,8},{10,9... | collective-permute-start | bytes 786440 | tf_op jit(solution)/shard_map/ppermute | solution.py:46
  72.1 5.0 %copy-start = (s32[2048]{0:T(1024)S(1)}, s32[2048]{0:T(1024)}, u32[]{:S(2)}) copy-start(s32[2048]{0:T(1024)} %param.12) | copy-start | bytes 24580
  74.5 6.4 %collective-permute-start.16 = (bf16[256,4096]{1,0:T(8,128)(2,1)S(1)}, bf16[256,4096]{1,0:T(8,128)(2,1)S(1)}, u32[]{:S(2)}, u32[]{:S(2)}) collective-permute-start(bf16[256,4096]{1,0:T(8,128)(2,1)S(1)} %shard_map.95.passages), channel_id=1, source_target_pairs={{0,8},{8,0},{16,24},{24,16},{32,40},{40,32},{48,56},{56,48},{64,72... | collective-permute-start | bytes 6291464 | tf_op jit(solution)/shard_map/ppermute | solution.py:28
  80.8 7.9 %copy-start.3 = (s32[1,256]{1,0:T(1,128)S(1)}, s32[1,256]{1,0:T(1,128)}, u32[]{:S(2)}) copy-start(s32[1,256]{1,0:T(1,128)} %owner.1) | copy-start | bytes 3076
  84.1 5.9 %collective-permute-start.17 = (f32[3,1024]{1,0:T(4,128)S(1)}, f32[3,1024]{1,0:T(4,128)S(1)}, u32[]{:S(2)}, u32[]{:S(2)}) collective-permute-start(f32[3,1024]{1,0:T(4,128)S(1)} %slice.112), channel_id=1, source_target_pairs={{0,64},{8,72},{16,80},{24,88},{32,96},{40,104},{48,112},{56,120},{... | collective-permute-start | bytes 36872 | tf_op jit(solution)/shard_map/ppermute | solution.py:28
  85.7 4.4 %collective-permute-start.18 = (f32[3,1024]{1,0:T(4,128)S(1)}, f32[3,1024]{1,0:T(4,128)S(1)}, u32[]{:S(2)}, u32[]{:S(2)}) collective-permute-start(f32[3,1024]{1,0:T(4,128)S(1)} %slice.112), channel_id=1, source_target_pairs={{0,192},{8,200},{16,208},{24,216},{32,224},{40,232},{48,240},{56,2... | collective-permute-start | bytes 36872 | tf_op jit(solution)/shard_map/ppermute | solution.py:28
  87.1 4.1 %collective-permute-start.19 = (f32[3,1024]{1,0:T(4,128)S(1)}, f32[3,1024]{1,0:T(4,128)S(1)}, u32[]{:S(2)}, u32[]{:S(2)}) collective-permute-start(f32[3,1024]{1,0:T(4,128)S(1)} %slice.112), channel_id=1, source_target_pairs={{0,128},{8,136},{16,144},{24,152},{32,160},{40,168},{48,176},{56,1... | collective-permute-start | bytes 36872 | tf_op jit(solution)/shard_map/ppermute | solution.py:28
  91.3 3.9 %collective-permute-start.20 = (f32[3,1024]{1,0:T(4,128)S(1)}, f32[3,1024]{1,0:T(4,128)S(1)}, u32[]{:S(2)}, u32[]{:S(2)}) collective-permute-start(f32[3,1024]{1,0:T(4,128)S(1)} %pad_maximum_fusion), channel_id=1, source_target_pairs={{0,16},{8,24},{16,32},{24,40},{32,48},{40,56},{48,0},{56,8},{64,80... | collective-permute-start | bytes 36872 | tf_op jit(solution)/shard_map/ppermute | solution.py:28
  93.0 2.6 %collective-permute-start.21 = (f32[3,1024]{1,0:T(4,128)S(1)}, f32[3,1024]{1,0:T(4,128)S(1)}, u32[]{:S(2)}, u32[]{:S(2)}) collective-permute-start(f32[3,1024]{1,0:T(4,128)S(1)} %pad_maximum_fusion), channel_id=1, source_target_pairs={{0,48},{8,56},{16,0},{24,8},{32,16},{40,24},{48,32},{56,40},{64,11... | collective-permute-start | bytes 36872 | tf_op jit(solution)/shard_map/ppermute | solution.py:28
  94.0 4.1 %collective-permute-start.22 = (f32[3,1024]{1,0:T(4,128)S(1)}, f32[3,1024]{1,0:T(4,128)S(1)}, u32[]{:S(2)}, u32[]{:S(2)}) collective-permute-start(f32[3,1024]{1,0:T(4,128)S(1)} %pad_maximum_fusion), channel_id=1, source_target_pairs={{0,32},{8,40},{16,48},{24,56},{32,0},{40,8},{48,16},{56,24},{64,96... | collective-permute-start | bytes 36872 | tf_op jit(solution)/shard_map/ppermute | solution.py:28
  98.2 4.4 %collective-permute-start.23 = (f32[1024]{0:T(1024)S(1)}, f32[1024]{0:T(1024)S(1)}, u32[]{:S(2)}, u32[]{:S(2)}) collective-permute-start(f32[1024]{0:T(1024)S(1)} %log_subtract_fusion), channel_id=1, source_target_pairs={{0,8},{8,0},{16,24},{24,16},{32,40},{40,32},{48,56},{56,48},{64,72... | collective-permute-start | bytes 12296 | tf_op jit(solution)/shard_map/ppermute | solution.py:28

commit v4 on v3

--- a/solution.py
+++ b/solution.py
@@ -137,43 +137,52 @@
     )(starts, hidden)
 
 
-def embed_kernel(info, _, gain, *refs):
-    blocks, out, sums = refs[:9], refs[9], refs[10]
+def picks_for(info, ring):
     _, _, core, z = place()
-    way = along(core)
     starts = info[:, 0:1]
-    counts = info[:, 128:129]
+    count = len(ring)
 
     def first_of(k):
         far = jnp.zeros(k.shape, jnp.int32)
-        for n, shift in enumerate(RING):
+        for n, shift in enumerate(ring):
             far = jnp.where(k == n, shift, far)
-        dev = lax.rem(z + way * far + 8, 8) * 1024
+        dev = lax.rem(z + along(core) * far + 8, 8) * 1024
         begun = (starts <= dev.astype(F32)).astype(F32)
         return (jnp.sum(begun, axis=0, keepdims=True) - 1.0).astype(jnp.int32)
 
-    seg = lax.broadcasted_iota(jnp.int32, (256, 512), 0)
-    lane = lax.broadcasted_iota(jnp.int32, (1, 512), 1)
+    seg = lax.broadcasted_iota(jnp.int32, (256, 64 * count), 0)
+    lane = lax.broadcasted_iota(jnp.int32, (1, 64 * count), 1)
     pick = jnp.where(seg == first_of(lane // 64) + lane % 64, 1.0, 0.0).astype(BF)
-    tlane = lax.broadcasted_iota(jnp.int32, (1, 128), 1)
-    tail_hit = lax.broadcasted_iota(jnp.int32, (256, 128), 0) == first_of(tlane // 16) + 64
-
-    def rows_of(row, rows):
-        parts = [block[row : row + rows, :] for block in blocks[:7]]
-        if row < CUT:
-            parts.append(blocks[7][row : row + rows, :])
-        else:
-            parts.append(blocks[8][row - CUT : row - CUT + rows, :])
-        return jnp.concatenate(parts, axis=0)
-
-    tail = rows_of(512, 16)
+    tlane = lax.broadcasted_iota(jnp.int32, (1, 16 * count), 1)
+    tseg = lax.broadcasted_iota(jnp.int32, (256, 16 * count), 0)
+    tail_hit = tseg == first_of(tlane // 16) + 64
+    return pick, lambda g: jnp.where(tail_hit & (tlane % 16 == g), 1.0, 0.0).astype(BF)
+
+
+def gather_kernel(info, *refs):
+    blocks, sums = refs[:7], refs[7]
+    pick, tail_pick = picks_for(info, RING[:7])
+    tail = jnp.concatenate([block[512:528, :] for block in blocks], axis=0)
+    for g in range(8):
+        main = jnp.concatenate([block[64 * g : 64 * g + 64, :] for block in blocks], axis=0)
+        sums[g] = jnp.dot(pick, main, preferred_element_type=F32) + jnp.dot(
+            tail_pick(g), tail, preferred_element_type=F32
+        )
+
+
+def embed_kernel(info, _, gain, early, low, high, out, sums):
+    pick, tail_pick = picks_for(info, RING[7:])
+    tail = high[512 - CUT : 528 - CUT, :]
+    counts = info[:, 128:129]
     square = jnp.zeros((256, 1), F32)
     for g in range(8):
-        tpick = jnp.where(tail_hit & (tlane % 16 == g), 1.0, 0.0).astype(BF)
-        mean = (
-            jnp.dot(pick, rows_of(64 * g, 64), preferred_element_type=F32)
-            + jnp.dot(tpick, tail, preferred_element_type=F32)
-        ) * gain[:, 512 * g : 512 * g + 512] / counts
+        main = low[64 * g : 64 * g + 64, :] if 64 * g < CUT else high[64 * g - CUT : 64 * g - CUT + 64, :]
+        total = (
+            early[g]
+            + jnp.dot(pick, main, preferred_element_type=F32)
+            + jnp.dot(tail_pick(g), tail, preferred_element_type=F32)
+        )
+        mean = total * gain[:, 512 * g : 512 * g + 512] / counts
         sums[g] = mean
         square += jnp.sum(mean * mean, axis=1, keepdims=True)
     scale = lax.rsqrt(square + 1e-06)
@@ -181,19 +190,33 @@
         out[:, 512 * g : 512 * g + 512] = (sums[g] * scale).astype(BF)
 
 
-def embed(info, token, gain, blocks):
+def gather(info, blocks):
+    vmem = pl.BlockSpec(memory_space=pltpu.VMEM)
+    return pl.pallas_call(
+        gather_kernel,
+        out_shape=jax.ShapeDtypeStruct((8, 256, 512), F32),
+        in_specs=[vmem] * 8,
+        out_specs=vmem,
+        compiler_params=pltpu.CompilerParams(vmem_limit_bytes=16 << 20),
+        cost_estimate=pl.CostEstimate(
+            flops=2 * 256 * 560 * 4096, bytes_accessed=6 << 20, transcendentals=0
+        ),
+    )(info, *blocks)
+
+
+def embed(info, token, gain, early, low, high):
     vmem = pl.BlockSpec(memory_space=pltpu.VMEM)
     return pl.pallas_call(
         embed_kernel,
         out_shape=jax.ShapeDtypeStruct((256, 4096), BF),
-        in_specs=[vmem] * 12,
+        in_specs=[vmem] * 6,
         out_specs=vmem,
         scratch_shapes=[pltpu.VMEM((8, 256, 512), F32)],
-        compiler_params=pltpu.CompilerParams(vmem_limit_bytes=24 << 20),
+        compiler_params=pltpu.CompilerParams(vmem_limit_bytes=16 << 20),
         cost_estimate=pl.CostEstimate(
-            flops=2 * 256 * 640 * 4096, bytes_accessed=7 << 20, transcendentals=0
-        ),
-    )(info, token, gain, *blocks)
+            flops=2 * 256 * 80 * 4096, bytes_accessed=6 << 20, transcendentals=0
+        ),
+    )(info, token, gain, early, low, high)
 
 
 def owned_kernel(owner, passages, out):
@@ -427,8 +450,8 @@
     up, down = copied((CUT, PACKED - CUT), cuts, got["f", 3], got["b", 3])
     got["f", 4], got["b", 4] = turn(up, 1), turn(down, -1)
 
-    order = [packed, *(got[k, n] for n in (1, 2, 3, 4) for k in "fb")]
-    mine = embed(info, token[0], gain[None, :], order)
+    early = gather(info, [packed, *(got[k, n] for n in (1, 2, 3) for k in "fb")])
+    mine = embed(info, token[0], gain[None, :], early, got["f", 4], got["b", 4])
     late = [("+", 4), ("-", 4)]
     mine, *rest = barrier((mine, *(got[k] for k in late)))
     got.update(zip(late, rest))

time: 103 us -> 103 us (level)
  waiting for transfers between devices: 46 us -> 44 us
  Pallas kernels: 16.4 us -> 17.7 us
    pallas_call x0 -> x1, Pallas kernels: none -> 1.94 us  [gather(): pl.pallas_call(gather_kernel, out_shape=jax.ShapeDtypeStruct((8, 256, 512...]
    ppermute x8, waiting for transfers between devices: 30.9 us -> 28.9 us  [turn(): lax.ppermute(value, ('dp', 'seq'), _hop(lambda c: (2, step * along(c))))]
  transfers between devices with their start and end apart: 24 -> 24, of which waited for: 15 -> 15; matrix products, arithmetic and copies ran while one was open for 0% -> 0% of each run, Pallas kernels for 13% -> 14%
where the time goes in v4:
time: 103 us
  waiting for transfers between devices  44 us (43%)
  starting transfers between devices  36.6 us (36%)
  Pallas kernels  17.7 us (17%)
  local copies, waits for them, and re-layouts  1.77 us (2%)
  between operations  1.47 us (1%)
    ppermute x8, waiting for transfers between devices, turn(): lax.ppermute(value, ('dp', 'seq'), _hop(lambda c: (2, step * along(c))))  28.9 us
    ppermute x9, starting transfers between devices, move(): return lax.ppermute(value, 'dp', pairs)  17.1 us
    ppermute x8, starting transfers between devices, turn(): lax.ppermute(value, ('dp', 'seq'), _hop(lambda c: (2, step * along(c))))  11.2 us
    ppermute x7, waiting for transfers between devices, pass_on(): lax.ppermute(value, ('dp', 'seq'), _hop(lambda c: ((c + second) % 2, step)))  9.9 us
    ppermute x7, starting transfers between devices, pass_on(): lax.ppermute(value, ('dp', 'seq'), _hop(lambda c: ((c + second) % 2, step)))  8.34 us
    pallas_call x1, Pallas kernels, pool(): pl.pallas_call(pool_kernel, out_shape=(jax.ShapeDtypeStruct((PACKED, 512)...  5.35 us
    ppermute x9, waiting for transfers between devices, move(): return lax.ppermute(value, 'dp', pairs)  5.22 us
    pallas_call x1, Pallas kernels, score(): pl.pallas_call(own_kernel, out_shape=(jax.ShapeDtypeStruct((1024, 4096),...  3.72 us
  transfers between devices with their start and end apart: 24, of which 15 were waited for; matrix products, arithmetic and copies ran while one was open for 0% of the time, Pallas kernels for 14%

profile of v4, /device:TPU:1, one launch (start us, length us, event | category | flops | bytes accessed | tf_op | source)
XLA Modules:
  0.0 102.5 jit_solution(3881098819951292099)
XLA Ops:
  0.7 1.1 %constant_dynamic-slice_fusion.1 = (bf16[1024,128]{1,0:T(8,128)(2,1)S(1)}, bf16[1024,128]{1,0:T(8,128)(2,1)S(1)}) fusion(bf16[2048,128]{1,0:T(8,128)(2,1)} %param.11, s32[]{:T(128)S(6)} %select_n.31, s32[]{:T(128)S(6)} %select_n.32), kind=kLoop, calls=%fused_computation.19 | loop fusion | bytes 1048584 | tf_op jit(solution)/shard_map/dynamic_slice | solution.py:410
  1.7 3.3 %collective-permute-start = (bf16[1024,128]{1,0:T(8,128)(2,1)S(1)}, bf16[1024,128]{1,0:T(8,128)(2,1)S(1)}, u32[]{:S(2)}, u32[]{:S(2)}) collective-permute-start(bf16[1024,128]{1,0:T(8,128)(2,1)S(1)} %get-tuple-element.87), channel_id=1, source_target_pairs={{0,8},{8,0},{16,24},{24,16},{32,40},{40,32},{48,56},{56,48},{64,72... | collective-permute-start | bytes 786440 | tf_op jit(solution)/shard_map/ppermute | solution.py:28
  5.7 5.3 %shard_map.86 = (bf16[528,512]{1,0:T(8,128)(2,1)S(1)}, f32[256,256]{1,0:T(8,128)S(1)}, f32[8,128]{1,0:T(8,128)S(1)}) custom-call(s32[1,256]{1,0:T(1,128)S(1)} %copy-done.2, bf16[1,1024,4096]{2,1,0:T(8,128)(2,1)} %hidden.1), custom_call_target="tpu_custom_call" | custom-call | flops 1073741824 | bytes 8388608 | tf_op jit(solution)/shard_map/pallas_call | solution.py:119
  11.4 2.7 %collective-permute-start.4 = (bf16[1024,256]{1,0:T(8,128)(2,1)S(1)}, bf16[1024,256]{1,0:T(8,128)(2,1)S(1)}, u32[]{:S(2)}, u32[]{:S(2)}) collective-permute-start(bf16[1024,256]{1,0:T(8,128)(2,1)S(1)} %maximum_select_fusion.refs_0_), channel_id=1, source_target_pairs={{0,192},{1,193},{2,194},{3,195},{4,196},{5,197},{6,198},{7,199},{8... | collective-permute-start | bytes 1572872 | tf_op jit(solution)/shard_map/ppermute | solution.py:50
  14.1 5.5 %collective-permute-start.1 = (bf16[528,512]{1,0:T(8,128)(2,1)S(1)}, bf16[528,512]{1,0:T(8,128)(2,1)S(1)}, u32[]{:S(2)}, u32[]{:S(2)}) collective-permute-start(bf16[528,512]{1,0:T(8,128)(2,1)S(1)} %get-tuple-element.49.refs_0_), channel_id=1, source_target_pairs={{0,1},{1,2},{2,3},{3,4},{4,5},{5,6},{6,7},{7,0},{8,15},{9,8},{10,9... | collective-permute-start | bytes 1622024 | tf_op jit(solution)/shard_map/ppermute | solution.py:46
  19.6 6.9 %collective-permute-done.3.refs_1_ = bf16[1024,256]{1,0:T(8,128)(2,1)S(1)} collective-permute-done((bf16[1024,256]{1,0:T(8,128)(2,1)S(1)}, bf16[1024,256]{1,0:T(8,128)(2,1)S(1)}, u32[]{:S(2)}, u32[]{:S(2)}) %collective-permute-start.3) | collective-permute-done | bytes 524320 | tf_op jit(solution)/shard_map/ppermute | solution.py:50
  27.2 2.3 %collective-permute-start.11 = (bf16[4096,256]{1,0:T(8,128)(2,1)S(1)}, bf16[4096,256]{1,0:T(8,128)(2,1)S(1)}, u32[]{:S(2)}, u32[]{:S(2)}) collective-permute-start(bf16[4096,256]{1,0:T(8,128)(2,1)S(1)} %shard_map.91.refs_0_), channel_id=1, source_target_pairs={{0,48},{1,49},{2,50},{3,51},{4,52},{5,53},{6,54},{7,55},{8,200},{9... | collective-permute-start | bytes 6291464 | tf_op jit(solution)/shard_map/ppermute | solution.py:50
  30.5 2.8 %collective-permute-done.2.refs_2_ = bf16[528,512]{1,0:T(8,128)(2,1)S(1)} collective-permute-done((bf16[528,512]{1,0:T(8,128)(2,1)S(1)}, bf16[528,512]{1,0:T(8,128)(2,1)S(1)}, u32[]{:S(2)}, u32[]{:S(2)}) %collective-permute-start.2) | collective-permute-done | bytes 540704 | tf_op jit(solution)/shard_map/ppermute | solution.py:46
  33.3 1.3 %collective-permute-start.6 = (bf16[528,512]{1,0:T(8,128)(2,1)S(1)}, bf16[528,512]{1,0:T(8,128)(2,1)S(1)}, u32[]{:S(2)}, u32[]{:S(2)}) collective-permute-start(bf16[528,512]{1,0:T(8,128)(2,1)S(1)} %collective-permute-done.1.refs_1_), channel_id=1, source_target_pairs={{0,1},{1,2},{2,3},{3,4},{4,5},{5,6},{6,7},{7,0},{8,15},{9,8},{10,9... | collective-permute-start | bytes 1622024 | tf_op jit(solution)/shard_map/ppermute | solution.py:46
  34.8 12.1 %collective-permute-done.6.refs_3_ = bf16[528,512]{1,0:T(8,128)(2,1)S(1)} collective-permute-done((bf16[528,512]{1,0:T(8,128)(2,1)S(1)}, bf16[528,512]{1,0:T(8,128)(2,1)S(1)}, u32[]{:S(2)}, u32[]{:S(2)}) %collective-permute-start.6) | collective-permute-done | bytes 540704 | tf_op jit(solution)/shard_map/ppermute | solution.py:46
  46.8 1.9 %collective-permute-done.7.refs_4_ = bf16[528,512]{1,0:T(8,128)(2,1)S(1)} collective-permute-done((bf16[528,512]{1,0:T(8,128)(2,1)S(1)}, bf16[528,512]{1,0:T(8,128)(2,1)S(1)}, u32[]{:S(2)}, u32[]{:S(2)}) %collective-permute-start.7) | collective-permute-done | bytes 540704 | tf_op jit(solution)/shard_map/ppermute | solution.py:46
  48.8 1.5 %collective-permute-start.9 = (bf16[528,512]{1,0:T(8,128)(2,1)S(1)}, bf16[528,512]{1,0:T(8,128)(2,1)S(1)}, u32[]{:S(2)}, u32[]{:S(2)}) collective-permute-start(bf16[528,512]{1,0:T(8,128)(2,1)S(1)} %collective-permute-done.7.refs_4_), channel_id=1, source_target_pairs={{0,7},{1,0},{2,1},{3,2},{4,3},{5,4},{6,5},{7,6},{8,9},{9,10},{10,1... | collective-permute-start | bytes 1622024 | tf_op jit(solution)/shard_map/ppermute | solution.py:46
  50.2 3.0 %collective-permute-done.10.refs_0_.refs_1_ = bf16[4096,256]{1,0:T(8,128)(2,1)S(1)} collective-permute-done((bf16[4096,256]{1,0:T(8,128)(2,1)S(1)}, bf16[4096,256]{1,0:T(8,128)(2,1)S(1)}, u32[]{:S(2)}, u32[]{:S(2)}) %collective-permute-start.10) | collective-permute-done | bytes 2097184 | tf_op jit(solution)/shard_map/ppermute | solution.py:50
  53.9 2.3 %collective-permute-start.15 = (bf16[2048,256]{1,0:T(8,128)(2,1)S(1)}, bf16[2048,256]{1,0:T(8,128)(2,1)S(1)}, u32[]{:S(2)}, u32[]{:S(2)}) collective-permute-start(bf16[2048,256]{1,0:T(8,128)(2,1)S(1)} %get-tuple-element.74), channel_id=1, source_target_pairs={{0,48},{1,49},{2,50},{3,51},{4,52},{5,53},{6,54},{7,55},{8,200},{9... | collective-permute-start | bytes 3145736 | tf_op jit(solution)/shard_map/ppermute | solution.py:50
  56.2 6.3 %collective-permute-done.8.refs_5_.refs_0_ = bf16[528,512]{1,0:T(8,128)(2,1)S(1)} collective-permute-done((bf16[528,512]{1,0:T(8,128)(2,1)S(1)}, bf16[528,512]{1,0:T(8,128)(2,1)S(1)}, u32[]{:S(2)}, u32[]{:S(2)}) %collective-permute-start.8) | collective-permute-done | bytes 540704 | tf_op jit(solution)/shard_map/ppermute | solution.py:46
  62.6 1.2 %collective-permute-done.9.refs_6_.refs_1_ = bf16[528,512]{1,0:T(8,128)(2,1)S(1)} collective-permute-done((bf16[528,512]{1,0:T(8,128)(2,1)S(1)}, bf16[528,512]{1,0:T(8,128)(2,1)S(1)}, u32[]{:S(2)}, u32[]{:S(2)}) %collective-permute-start.9) | collective-permute-done | bytes 540704 | tf_op jit(solution)/shard_map/ppermute | solution.py:46
  63.9 2.7 %collective-permute-start.12 = (bf16[256,512]{1,0:T(8,128)(2,1)S(1)}, bf16[256,512]{1,0:T(8,128)(2,1)S(1)}, u32[]{:S(2)}, u32[]{:S(2)}) collective-permute-start(bf16[256,512]{1,0:T(8,128)(2,1)S(1)} %get-tuple-element.71), channel_id=1, source_target_pairs={{0,1},{1,2},{2,3},{3,4},{4,5},{5,6},{6,7},{7,0},{8,15},{9,8},{10,9... | collective-permute-start | bytes 786440 | tf_op jit(solution)/shard_map/ppermute | solution.py:46
  66.6 1.9 %shard_map.94.early = f32[8,256,512]{2,1,0:T(8,128)S(1)} custom-call(f32[256,256]{1,0:T(8,128)S(1)} %get-tuple-element.43.info, bf16[528,512]{1,0:T(8,128)(2,1)S(1)} %get-tuple-element.49.refs_0_, bf16[528,512]{1,0:T(8,128)(2,1)S(1)} %collective-permute-done.1.refs_1_, bf16[528,512]{1,0:T(8,128)(2,1)S(1)} %collective-permute-done.2.refs_2_, ...), custom_call_target="tpu_custom_call" | custom-call | flops 1174405120 | bytes 6291456 | tf_op jit(solution)/shard_map/pallas_call | solution.py:195
  68.6 3.5 %collective-permute-done.12.low = bf16[256,512]{1,0:T(8,128)(2,1)S(1)} collective-permute-done((bf16[256,512]{1,0:T(8,128)(2,1)S(1)}, bf16[256,512]{1,0:T(8,128)(2,1)S(1)}, u32[]{:S(2)}, u32[]{:S(2)}) %collective-permute-start.12) | collective-permute-done | bytes 262176 | tf_op jit(solution)/shard_map/ppermute | solution.py:46
  72.1 1.7 %shard_map.96.passages = bf16[256,4096]{1,0:T(8,128)(2,1)S(1)} custom-call(f32[256,256]{1,0:T(8,128)S(1)} %get-tuple-element.43.info, f32[8,128]{1,0:T(8,128)S(1)} %shard_map.93._, f32[1,4096]{1,0:T(1,128)S(1)} %bitcast.15, f32[8,256,512]{2,1,0:T(8,128)S(1)} %shard_map.94.early, bf16[256,512]{1,0:T(8,128)(2,1)S(1)} %collective-permute-done.12.low, ...), custom_call_target="tpu_custom_call" | custom-call | flops 167772160 | bytes 6291456 | tf_op jit(solution)/shard_map/pallas_call | solution.py:209
  73.8 2.2 %collective-permute-start.16 = (bf16[256,4096]{1,0:T(8,128)(2,1)S(1)}, bf16[256,4096]{1,0:T(8,128)(2,1)S(1)}, u32[]{:S(2)}, u32[]{:S(2)}) collective-permute-start(bf16[256,4096]{1,0:T(8,128)(2,1)S(1)} %shard_map.96.passages), channel_id=1, source_target_pairs={{0,8},{8,0},{16,24},{24,16},{32,40},{40,32},{48,56},{56,48},{64,72... | collective-permute-start | bytes 6291464 | tf_op jit(solution)/shard_map/ppermute | solution.py:28
  76.7 3.7 %shard_map.98 = (bf16[1024,4096]{1,0:T(8,128)(2,1)S(1)}, f32[1024,128]{1,0:T(8,128)S(1)}) custom-call(f32[1,1]{1,0:T(1,128)} %bitcast.12.scale, s32[16,128]{1,0:T(8,128)S(1)} %bitcast.13, bf16[256,4096]{1,0:T(8,128)(2,1)S(1)} %shard_map.96.passages, bf16[4096,256]{1,0:T(8,128)(2,1)S(1)} %shard_map.91.refs_0_, ...), custom_call_target="tpu_custom_call" | custom-call | flops 2147483648 | bytes 1048576 | tf_op jit(solution)/shard_map/pallas_call | solution.py:334
  80.5 3.3 %shard_map.99 = f32[8,1024]{1,0:T(8,128)S(1)} custom-call(s32[16,128]{1,0:T(8,128)S(1)} %bitcast.14, bf16[256,4096]{1,0:T(8,128)(2,1)S(1)} %collective-permute-done.16.passages, bf16[1024,4096]{1,0:T(8,128)(2,1)S(1)} %get-tuple-element.80.all_q, f32[1024,128]{1,0:T(8,128)S(1)} %get-tuple-element.81.early), custom_call_target="tpu_custom_call" | custom-call | flops 2147483648 | bytes 1048576 | tf_op jit(solution)/shard_map/pallas_call | solution.py:346
  83.8 1.3 %collective-permute-start.17 = (f32[3,1024]{1,0:T(4,128)S(1)}, f32[3,1024]{1,0:T(4,128)S(1)}, u32[]{:S(2)}, u32[]{:S(2)}) collective-permute-start(f32[3,1024]{1,0:T(4,128)S(1)} %slice.112), channel_id=1, source_target_pairs={{0,64},{8,72},{16,80},{24,88},{32,96},{40,104},{48,112},{56,120},{... | collective-permute-start | bytes 36872 | tf_op jit(solution)/shard_map/ppermute | solution.py:28
  85.1 1.5 %collective-permute-start.18 = (f32[3,1024]{1,0:T(4,128)S(1)}, f32[3,1024]{1,0:T(4,128)S(1)}, u32[]{:S(2)}, u32[]{:S(2)}) collective-permute-start(f32[3,1024]{1,0:T(4,128)S(1)} %slice.112), channel_id=1, source_target_pairs={{0,192},{8,200},{16,208},{24,216},{32,224},{40,232},{48,240},{56,2... | collective-permute-start | bytes 36872 | tf_op jit(solution)/shard_map/ppermute | solution.py:28
  86.5 1.6 %collective-permute-start.19 = (f32[3,1024]{1,0:T(4,128)S(1)}, f32[3,1024]{1,0:T(4,128)S(1)}, u32[]{:S(2)}, u32[]{:S(2)}) collective-permute-start(f32[3,1024]{1,0:T(4,128)S(1)} %slice.112), channel_id=1, source_target_pairs={{0,128},{8,136},{16,144},{24,152},{32,160},{40,168},{48,176},{56,1... | collective-permute-start | bytes 36872 | tf_op jit(solution)/shard_map/ppermute | solution.py:28
  88.2 1.3 %shard_map.100 = bf16[32,4096]{1,0:T(8,128)(2,1)} custom-call(s32[1,256]{1,0:T(1,128)S(1)} %copy-done.3, bf16[256,4096]{1,0:T(8,128)(2,1)S(1)} %shard_map.96.passages), custom_call_target="tpu_custom_call" | custom-call | flops 67108864 | bytes 3145728 | tf_op jit(solution)/shard_map/pallas_call | solution.py:235
  89.5 1.1 %collective-permute-done.19 = f32[3,1024]{1,0:T(4,128)S(1)} collective-permute-done((f32[3,1024]{1,0:T(4,128)S(1)}, f32[3,1024]{1,0:T(4,128)S(1)}, u32[]{:S(2)}, u32[]{:S(2)}) %collective-permute-start.19) | collective-permute-done | bytes 12320 | tf_op jit(solution)/shard_map/ppermute | solution.py:28
  90.7 1.7 %collective-permute-start.20 = (f32[3,1024]{1,0:T(4,128)S(1)}, f32[3,1024]{1,0:T(4,128)S(1)}, u32[]{:S(2)}, u32[]{:S(2)}) collective-permute-start(f32[3,1024]{1,0:T(4,128)S(1)} %pad_maximum_fusion), channel_id=1, source_target_pairs={{0,16},{8,24},{16,32},{24,40},{32,48},{40,56},{48,0},{56,8},{64,80... | collective-permute-start | bytes 36872 | tf_op jit(solution)/shard_map/ppermute | solution.py:28
  92.4 1.0 %collective-permute-start.21 = (f32[3,1024]{1,0:T(4,128)S(1)}, f32[3,1024]{1,0:T(4,128)S(1)}, u32[]{:S(2)}, u32[]{:S(2)}) collective-permute-start(f32[3,1024]{1,0:T(4,128)S(1)} %pad_maximum_fusion), channel_id=1, source_target_pairs={{0,48},{8,56},{16,0},{24,8},{32,16},{40,24},{48,32},{56,40},{64,11... | collective-permute-start | bytes 36872 | tf_op jit(solution)/shard_map/ppermute | solution.py:28
  95.0 2.5 %collective-permute-done.22 = f32[3,1024]{1,0:T(4,128)S(1)} collective-permute-done((f32[3,1024]{1,0:T(4,128)S(1)}, f32[3,1024]{1,0:T(4,128)S(1)}, u32[]{:S(2)}, u32[]{:S(2)}) %collective-permute-start.22) | collective-permute-done | bytes 12320 | tf_op jit(solution)/shard_map/ppermute | solution.py:28
  97.6 3.5 %collective-permute-start.23 = (f32[1024]{0:T(1024)S(1)}, f32[1024]{0:T(1024)S(1)}, u32[]{:S(2)}, u32[]{:S(2)}) collective-permute-start(f32[1024]{0:T(1024)S(1)} %log_subtract_fusion), channel_id=1, source_target_pairs={{0,8},{8,0},{16,24},{24,16},{32,40},{40,32},{48,56},{56,48},{64,72... | collective-permute-start | bytes 12296 | tf_op jit(solution)/shard_map/ppermute | solution.py:28
  (47 shorter events, 6.9 us)
Async XLA Ops:
  1.7 9.4 %collective-permute-start = (bf16[1024,128]{1,0:T(8,128)(2,1)S(1)}, bf16[1024,128]{1,0:T(8,128)(2,1)S(1)}, u32[]{:S(2)}, u32[]{:S(2)}) collective-permute-start(bf16[1024,128]{1,0:T(8,128)(2,1)S(1)} %get-tuple-element.87), channel_id=1, source_target_pairs={{0,8},{8,0},{16,24},{24,16},{32,40},{40,32},{48,56},{56,48},{64,72... | collective-permute-start | bytes 786440 | tf_op jit(solution)/shard_map/ppermute | solution.py:28
  5.1 0.7 copy-start.2
  11.3 15.2 %collective-permute-start.3 = (bf16[1024,256]{1,0:T(8,128)(2,1)S(1)}, bf16[1024,256]{1,0:T(8,128)(2,1)S(1)}, u32[]{:S(2)}, u32[]{:S(2)}) collective-permute-start(bf16[1024,256]{1,0:T(8,128)(2,1)S(1)} %maximum_select_fusion.refs_0_), channel_id=1, source_target_pairs={{0,64},{1,65},{2,66},{3,67},{4,68},{5,69},{6,70},{7,71},{8,24},{9,... | collective-permute-start | bytes 1572872 | tf_op jit(solution)/shard_map/ppermute | solution.py:50
  11.4 15.1 %collective-permute-start.4 = (bf16[1024,256]{1,0:T(8,128)(2,1)S(1)}, bf16[1024,256]{1,0:T(8,128)(2,1)S(1)}, u32[]{:S(2)}, u32[]{:S(2)}) collective-permute-start(bf16[1024,256]{1,0:T(8,128)(2,1)S(1)} %maximum_select_fusion.refs_0_), channel_id=1, source_target_pairs={{0,192},{1,193},{2,194},{3,195},{4,196},{5,197},{6,198},{7,199},{8... | collective-permute-start | bytes 1572872 | tf_op jit(solution)/shard_map/ppermute | solution.py:50
  14.0 12.5 %collective-permute-start.5 = (bf16[1024,256]{1,0:T(8,128)(2,1)S(1)}, bf16[1024,256]{1,0:T(8,128)(2,1)S(1)}, u32[]{:S(2)}, u32[]{:S(2)}) collective-permute-start(bf16[1024,256]{1,0:T(8,128)(2,1)S(1)} %maximum_select_fusion.refs_0_), channel_id=1, source_target_pairs={{0,128},{1,129},{2,130},{3,131},{4,132},{5,133},{6,134},{7,135},{8... | collective-permute-start | bytes 1572872 | tf_op jit(solution)/shard_map/ppermute | solution.py:50
  14.1 16.5 %collective-permute-start.1 = (bf16[528,512]{1,0:T(8,128)(2,1)S(1)}, bf16[528,512]{1,0:T(8,128)(2,1)S(1)}, u32[]{:S(2)}, u32[]{:S(2)}) collective-permute-start(bf16[528,512]{1,0:T(8,128)(2,1)S(1)} %get-tuple-element.49.refs_0_), channel_id=1, source_target_pairs={{0,1},{1,2},{2,3},{3,4},{4,5},{5,6},{6,7},{7,0},{8,15},{9,8},{10,9... | collective-permute-start | bytes 1622024 | tf_op jit(solution)/shard_map/ppermute | solution.py:46
  19.6 13.7 %collective-permute-start.2 = (bf16[528,512]{1,0:T(8,128)(2,1)S(1)}, bf16[528,512]{1,0:T(8,128)(2,1)S(1)}, u32[]{:S(2)}, u32[]{:S(2)}) collective-permute-start(bf16[528,512]{1,0:T(8,128)(2,1)S(1)} %get-tuple-element.49.refs_0_), channel_id=1, source_target_pairs={{0,7},{1,0},{2,1},{3,2},{4,3},{5,4},{6,5},{7,6},{8,9},{9,10},{10,1... | collective-permute-start | bytes 1622024 | tf_op jit(solution)/shard_map/ppermute | solution.py:46
  26.7 26.5 %collective-permute-start.10 = (bf16[4096,256]{1,0:T(8,128)(2,1)S(1)}, bf16[4096,256]{1,0:T(8,128)(2,1)S(1)}, u32[]{:S(2)}, u32[]{:S(2)}) collective-permute-start(bf16[4096,256]{1,0:T(8,128)(2,1)S(1)} %shard_map.91.refs_0_), channel_id=1, source_target_pairs={{0,16},{1,17},{2,18},{3,19},{4,20},{5,21},{6,22},{7,23},{8,72},{9,... | collective-permute-start | bytes 6291464 | tf_op jit(solution)/shard_map/ppermute | solution.py:50
  27.2 26.0 %collective-permute-start.11 = (bf16[4096,256]{1,0:T(8,128)(2,1)S(1)}, bf16[4096,256]{1,0:T(8,128)(2,1)S(1)}, u32[]{:S(2)}, u32[]{:S(2)}) collective-permute-start(bf16[4096,256]{1,0:T(8,128)(2,1)S(1)} %shard_map.91.refs_0_), channel_id=1, source_target_pairs={{0,48},{1,49},{2,50},{3,51},{4,52},{5,53},{6,54},{7,55},{8,200},{9... | collective-permute-start | bytes 6291464 | tf_op jit(solution)/shard_map/ppermute | solution.py:50
  33.3 13.5 %collective-permute-start.6 = (bf16[528,512]{1,0:T(8,128)(2,1)S(1)}, bf16[528,512]{1,0:T(8,128)(2,1)S(1)}, u32[]{:S(2)}, u32[]{:S(2)}) collective-permute-start(bf16[528,512]{1,0:T(8,128)(2,1)S(1)} %collective-permute-done.1.refs_1_), channel_id=1, source_target_pairs={{0,1},{1,2},{2,3},{3,4},{4,5},{5,6},{6,7},{7,0},{8,15},{9,8},{10,9... | collective-permute-start | bytes 1622024 | tf_op jit(solution)/shard_map/ppermute | solution.py:46
  34.6 14.2 %collective-permute-start.7 = (bf16[528,512]{1,0:T(8,128)(2,1)S(1)}, bf16[528,512]{1,0:T(8,128)(2,1)S(1)}, u32[]{:S(2)}, u32[]{:S(2)}) collective-permute-start(bf16[528,512]{1,0:T(8,128)(2,1)S(1)} %collective-permute-done.2.refs_2_), channel_id=1, source_target_pairs={{0,7},{1,0},{2,1},{3,2},{4,3},{5,4},{6,5},{7,6},{8,9},{9,10},{10,1... | collective-permute-start | bytes 1622024 | tf_op jit(solution)/shard_map/ppermute | solution.py:46
  48.8 13.8 %collective-permute-start.8 = (bf16[528,512]{1,0:T(8,128)(2,1)S(1)}, bf16[528,512]{1,0:T(8,128)(2,1)S(1)}, u32[]{:S(2)}, u32[]{:S(2)}) collective-permute-start(bf16[528,512]{1,0:T(8,128)(2,1)S(1)} %collective-permute-done.6.refs_3_), channel_id=1, source_target_pairs={{0,1},{1,2},{2,3},{3,4},{4,5},{5,6},{6,7},{7,0},{8,15},{9,8},{10,9... | collective-permute-start | bytes 1622024 | tf_op jit(solution)/shard_map/ppermute | solution.py:46
  48.8 15.0 %collective-permute-start.9 = (bf16[528,512]{1,0:T(8,128)(2,1)S(1)}, bf16[528,512]{1,0:T(8,128)(2,1)S(1)}, u32[]{:S(2)}, u32[]{:S(2)}) collective-permute-start(bf16[528,512]{1,0:T(8,128)(2,1)S(1)} %collective-permute-done.7.refs_4_), channel_id=1, source_target_pairs={{0,7},{1,0},{2,1},{3,2},{4,3},{5,4},{6,5},{7,6},{8,9},{9,10},{10,1... | collective-permute-start | bytes 1622024 | tf_op jit(solution)/shard_map/ppermute | solution.py:46
  53.4 20.5 %collective-permute-start.14 = (bf16[2048,256]{1,0:T(8,128)(2,1)S(1)}, bf16[2048,256]{1,0:T(8,128)(2,1)S(1)}, u32[]{:S(2)}, u32[]{:S(2)}) collective-permute-start(bf16[2048,256]{1,0:T(8,128)(2,1)S(1)} %get-tuple-element.73), channel_id=1, source_target_pairs={{0,16},{1,17},{2,18},{3,19},{4,20},{5,21},{6,22},{7,23},{8,72},{9,... | collective-permute-start | bytes 3145736 | tf_op jit(solution)/shard_map/ppermute | solution.py:50
  53.9 20.0 %collective-permute-start.15 = (bf16[2048,256]{1,0:T(8,128)(2,1)S(1)}, bf16[2048,256]{1,0:T(8,128)(2,1)S(1)}, u32[]{:S(2)}, u32[]{:S(2)}) collective-permute-start(bf16[2048,256]{1,0:T(8,128)(2,1)S(1)} %get-tuple-element.74), channel_id=1, source_target_pairs={{0,48},{1,49},{2,50},{3,51},{4,52},{5,53},{6,54},{7,55},{8,200},{9... | collective-permute-start | bytes 3145736 | tf_op jit(solution)/shard_map/ppermute | solution.py:50
  63.8 8.3 %collective-permute-start.13 = (bf16[272,512]{1,0:T(8,128)(2,1)S(1)}, bf16[272,512]{1,0:T(8,128)(2,1)S(1)}, u32[]{:S(2)}, u32[]{:S(2)}) collective-permute-start(bf16[272,512]{1,0:T(8,128)(2,1)S(1)} %get-tuple-element.72), channel_id=1, source_target_pairs={{0,7},{1,0},{2,1},{3,2},{4,3},{5,4},{6,5},{7,6},{8,9},{9,10},{10,1... | collective-permute-start | bytes 835592 | tf_op jit(solution)/shard_map/ppermute | solution.py:46
  63.9 8.1 %collective-permute-start.12 = (bf16[256,512]{1,0:T(8,128)(2,1)S(1)}, bf16[256,512]{1,0:T(8,128)(2,1)S(1)}, u32[]{:S(2)}, u32[]{:S(2)}) collective-permute-start(bf16[256,512]{1,0:T(8,128)(2,1)S(1)} %get-tuple-element.71), channel_id=1, source_target_pairs={{0,1},{1,2},{2,3},{3,4},{4,5},{5,6},{6,7},{7,0},{8,15},{9,8},{10,9... | collective-permute-start | bytes 786440 | tf_op jit(solution)/shard_map/ppermute | solution.py:46
  66.6 5.5 %copy-start.1 = (f32[4096]{0:T(1024)S(1)}, f32[4096]{0:T(1024)}, u32[]{:S(2)}) copy-start(f32[4096]{0:T(1024)} %param.8) | copy-start | bytes 49156
  72.1 4.6 %copy-start = (s32[2048]{0:T(1024)S(1)}, s32[2048]{0:T(1024)}, u32[]{:S(2)}) copy-start(s32[2048]{0:T(1024)} %param.12) | copy-start | bytes 24580
  73.8 6.6 %collective-permute-start.16 = (bf16[256,4096]{1,0:T(8,128)(2,1)S(1)}, bf16[256,4096]{1,0:T(8,128)(2,1)S(1)}, u32[]{:S(2)}, u32[]{:S(2)}) collective-permute-start(bf16[256,4096]{1,0:T(8,128)(2,1)S(1)} %shard_map.96.passages), channel_id=1, source_target_pairs={{0,8},{8,0},{16,24},{24,16},{32,40},{40,32},{48,56},{56,48},{64,72... | collective-permute-start | bytes 6291464 | tf_op jit(solution)/shard_map/ppermute | solution.py:28
  80.5 7.7 %copy-start.3 = (s32[1,256]{1,0:T(1,128)S(1)}, s32[1,256]{1,0:T(1,128)}, u32[]{:S(2)}) copy-start(s32[1,256]{1,0:T(1,128)} %owner.1) | copy-start | bytes 3076
  83.8 5.7 %collective-permute-start.17 = (f32[3,1024]{1,0:T(4,128)S(1)}, f32[3,1024]{1,0:T(4,128)S(1)}, u32[]{:S(2)}, u32[]{:S(2)}) collective-permute-start(f32[3,1024]{1,0:T(4,128)S(1)} %slice.112), channel_id=1, source_target_pairs={{0,64},{8,72},{16,80},{24,88},{32,96},{40,104},{48,112},{56,120},{... | collective-permute-start | bytes 36872 | tf_op jit(solution)/shard_map/ppermute | solution.py:28
  85.1 4.4 %collective-permute-start.18 = (f32[3,1024]{1,0:T(4,128)S(1)}, f32[3,1024]{1,0:T(4,128)S(1)}, u32[]{:S(2)}, u32[]{:S(2)}) collective-permute-start(f32[3,1024]{1,0:T(4,128)S(1)} %slice.112), channel_id=1, source_target_pairs={{0,192},{8,200},{16,208},{24,216},{32,224},{40,232},{48,240},{56,2... | collective-permute-start | bytes 36872 | tf_op jit(solution)/shard_map/ppermute | solution.py:28
  86.5 4.1 %collective-permute-start.19 = (f32[3,1024]{1,0:T(4,128)S(1)}, f32[3,1024]{1,0:T(4,128)S(1)}, u32[]{:S(2)}, u32[]{:S(2)}) collective-permute-start(f32[3,1024]{1,0:T(4,128)S(1)} %slice.112), channel_id=1, source_target_pairs={{0,128},{8,136},{16,144},{24,152},{32,160},{40,168},{48,176},{56,1... | collective-permute-start | bytes 36872 | tf_op jit(solution)/shard_map/ppermute | solution.py:28
  90.7 3.9 %collective-permute-start.20 = (f32[3,1024]{1,0:T(4,128)S(1)}, f32[3,1024]{1,0:T(4,128)S(1)}, u32[]{:S(2)}, u32[]{:S(2)}) collective-permute-start(f32[3,1024]{1,0:T(4,128)S(1)} %pad_maximum_fusion), channel_id=1, source_target_pairs={{0,16},{8,24},{16,32},{24,40},{32,48},{40,56},{48,0},{56,8},{64,80... | collective-permute-start | bytes 36872 | tf_op jit(solution)/shard_map/ppermute | solution.py:28
  92.4 2.6 %collective-permute-start.21 = (f32[3,1024]{1,0:T(4,128)S(1)}, f32[3,1024]{1,0:T(4,128)S(1)}, u32[]{:S(2)}, u32[]{:S(2)}) collective-permute-start(f32[3,1024]{1,0:T(4,128)S(1)} %pad_maximum_fusion), channel_id=1, source_target_pairs={{0,48},{8,56},{16,0},{24,8},{32,16},{40,24},{48,32},{56,40},{64,11... | collective-permute-start | bytes 36872 | tf_op jit(solution)/shard_map/ppermute | solution.py:28
  93.4 4.1 %collective-permute-start.22 = (f32[3,1024]{1,0:T(4,128)S(1)}, f32[3,1024]{1,0:T(4,128)S(1)}, u32[]{:S(2)}, u32[]{:S(2)}) collective-permute-start(f32[3,1024]{1,0:T(4,128)S(1)} %pad_maximum_fusion), channel_id=1, source_target_pairs={{0,32},{8,40},{16,48},{24,56},{32,0},{40,8},{48,16},{56,24},{64,96... | collective-permute-start | bytes 36872 | tf_op jit(solution)/shard_map/ppermute | solution.py:28
  97.6 4.4 %collective-permute-start.23 = (f32[1024]{0:T(1024)S(1)}, f32[1024]{0:T(1024)S(1)}, u32[]{:S(2)}, u32[]{:S(2)}) collective-permute-start(f32[1024]{0:T(1024)S(1)} %log_subtract_fusion), channel_id=1, source_target_pairs={{0,8},{8,0},{16,24},{24,16},{32,40},{40,32},{48,56},{56,48},{64,72... | collective-permute-start | bytes 12296 | tf_op jit(solution)/shard_map/ppermute | solution.py:28
